TPU v7x, 256 devices: a whole 4x4x8 slice. The times are simulated.
256 devices in a mesh: lon: 32 (over y_lo, z, core), lat: 8 (over y_hi, x).
Axes of the slice: x: 4, y: 4 (y_hi: 2, y_lo: 2; y = y_hi * 2 + y_lo), z: 8, core: 2. Of those that a mesh axis runs over, the one named last changes fastest.
Arguments:
- field: bfloat16 [512, 128, 512], P('lon', 'lat'), may hold values from -6 to 6
- cotangent: bfloat16 [512, 128, 512], P('lon', 'lat'), may hold values from -6 to 6
- land_sea: int32 [512, 128], P('lon', 'lat'), may hold values 0 or 1
- fold_partner: int32 [512], replicated, may hold values from 0 to 511, as said below
- depth_kernel: float32 [49, 512], replicated, may hold values from -0.875 to 0.875
- norm_gain: float32 [512], replicated, may hold values from 0.5 to 1.5
- w_up: bfloat16 [512, 2048], replicated, may hold values from -0.25 to 0.25
- b_up: float32 [2048], replicated, may hold values from -3 to 3
- w_down: bfloat16 [2048, 512], replicated, may hold values from -0.125 to 0.125
Outputs:
- grad_field: bfloat16 [512, 128, 512], P('lon', 'lat')
- grad_up: float32 [512, 2048], P(('lon', 'lat'))
- grad_down: float32 [2048, 512], P(('lon', 'lat'))
- grad_kernel: float32 [49, 512], replicated
- grad_gain: float32 [512], replicated
- grad_bias: float32 [2048], replicated
Inputs may be any that keep to these rules, and one draw needn't show every extreme that they name: fold_partner[j] = (fold_partner[0] - j) mod 512 for every column j, a mirror of the columns; 511 - fold_partner[0] is at least 16 and not a multiple of 16.
All inputs are finite; a program needn't handle non-finite values. No bound on the sum of `land_sea` on one device may be relied on, other than what follows from the above.
Results may differ from a plain program's by a relative error of at most 0.013.
Values may be sent and summed in bfloat16 or wider, within the bound.
No kernel may reach another device: no remote copies, remote signals or barrier semaphores. Data moves between devices by JAX's collectives and lax.ppermute only.
A program may use at most 128 MiB of HBM per device.

v0:
```python
import jax
import jax.numpy as jnp
from jax import lax
from jax.experimental import pallas as pl
from jax.experimental.pallas import tpu as pltpu
from jax.sharding import PartitionSpec as P


def extended_2(cells, sides, width, closed):
    for axis, dim in sides:
        count = lax.axis_size(axis)
        ends = count if closed else count - 1
        head = lax.slice_in_dim(cells, 0, width, axis=dim)
        tail = lax.slice_in_dim(cells, cells.shape[dim] - width, cells.shape[dim], axis=dim)
        cells = jnp.concatenate(
            [
                lax.ppermute(tail, axis, [(i, (i + 1) % count) for i in range(ends)]),
                cells,
                lax.ppermute(head, axis, [((i + 1) % count, i) for i in range(ends)]),
            ],
            axis=dim,
        )
    return cells


DEVICES = ("lon", "lat")


def send(value, mask):
    return lax.ppermute(value, DEVICES, [(i, i ^ mask) for i in range(256)])


def tree_sum(parts):
    while len(parts) > 1:
        parts = [parts[i] + parts[i + 1] for i in range(0, len(parts), 2)]
    return parts[0]


def whole_stage(value, masks):
    return tree_sum([value] + [send(value, mask) for mask in masks])


X_MASKS = (1, 2, 3)
Y_MASKS = (128, 4, 132)
Z_MASKS = (16, 32, 48, 64)
CORE_MASK = 8


def mirror_tiles(value, half_turn):
    def branch(k):
        pairs = [(e * 8 + 7, ((2 * k - e) % 32) * 8 + 7) for e in range(32)]
        return lambda v: lax.ppermute(v, DEVICES, pairs)

    return lax.switch(half_turn, [branch(k) for k in range(16)], value)


def to_next(value):
    return lax.ppermute(value, "lon", [(i, (i + 1) % 32) for i in range(32)])


def to_previous(value):
    return lax.ppermute(value, "lon", [((i + 1) % 32, i) for i in range(32)])


ROOT_2_PI = 0.7978845608028654
CUBIC = 0.044715
F32 = jnp.float32
BF16 = jnp.bfloat16


def spread_rows(ext_ref, wide, shifted):
    wide[...] = ext_ref[...].astype(F32)
    for b in range(7):
        shifted[b] = wide[:, b : b + 16, :]


def forward_kernel(
    at_ref, ext_ref, kern_ref, gain_ref, w_up_ref, b_up_ref, d_out_ref, d_act_ref, order_ref,
    mixed_ref, d_upper_ref, bias_ref, keep_ref, send_ref,
    wide, shifted, normed, ordered, upper, active, tile,
):
    core, x_at, y_at = at_ref[0], at_ref[1], at_ref[2]
    spread_rows(ext_ref, wide, shifted)

    def conv_step(step, carry):
        lanes = pl.ds(pl.multiple_of(step * 128, 128), 128)
        totals = [jnp.zeros((16, 128), F32)] * 16
        for b in range(7):
            weights = [kern_ref[a * 7 + b : a * 7 + b + 1, lanes] for a in range(7)]
            for r in range(22):
                cells = shifted[b, r, :, lanes]
                for a in range(max(0, r - 15), min(7, r + 1)):
                    totals[r - a] = totals[r - a] + cells * weights[a]
        for x in range(16):
            mixed_ref[x * 16 : x * 16 + 16, lanes] = totals[x]
        return carry

    lax.fori_loop(0, 4, conv_step, 0)

    def norm_step(step, carry):
        rows = pl.ds(pl.multiple_of(step * 32, 32), 32)
        cells = mixed_ref[rows, :]
        center = cells - jnp.mean(cells, axis=-1, keepdims=True)
        spread = jnp.mean(center * center, axis=-1, keepdims=True)
        normed[rows, :] = (center * lax.rsqrt(spread + 1e-6) * gain_ref[...]).astype(BF16)
        return carry

    lax.fori_loop(0, 8, norm_step, 0)
    ordered[...] = jnp.dot(normed[...], order_ref[...], preferred_element_type=F32).astype(BF16)

    for t in range(4):
        lanes = slice(t * 512, t * 512 + 512)
        upper[...] = jnp.dot(normed[...], w_up_ref[:, lanes], preferred_element_type=F32)

        def gelu_step(step, bias):
            rows = pl.ds(pl.multiple_of(step * 32, 32), 32)
            u = upper[rows, :] + b_up_ref[:, lanes]
            square = u * u
            th = jnp.tanh(ROOT_2_PI * (u + CUBIC * (square * u)))
            half = 0.5 * (1.0 + th)
            active[rows, :] = (u * half).astype(BF16)
            slope = half + (0.5 * ROOT_2_PI) * u * (1.0 - th * th) * (1.0 + (3.0 * CUBIC) * square)
            d_up = (d_act_ref[rows, lanes] * slope).astype(BF16)
            d_upper_ref[rows, lanes] = d_up
            return bias + jnp.sum(d_up.astype(F32), axis=0, keepdims=True)

        bias_ref[t : t + 1, :] = lax.fori_loop(0, 8, gelu_step, jnp.zeros((1, 512), F32))
        tile[...] = lax.dot_general(
            active[...], d_out_ref[...], (((0,), (0,)), ((), ())), preferred_element_type=F32
        )
        for y_hi in range(2):
            k_y = (y_hi * 2 + t // 2) ^ y_at
            for k_x in range(4):
                base = y_hi * 32 + (k_x ^ x_at) * 8
                for mine in range(2):
                    at = base + ((1 - core) if mine == 0 else core) * 64
                    piece = jnp.concatenate(
                        [tile[pl.ds(pl.multiple_of(at + zz * 128, 8), 8), :] for zz in range(4)],
                        axis=0,
                    )
                    rows = pl.ds(pl.multiple_of(k_y * 64 + (t % 2) * 32, 32), 32)
                    if mine == 0:
                        send_ref[k_x, rows, :] = piece.astype(BF16)
                    else:
                        keep_ref[k_x, rows, :] = piece
        tile[...] = lax.dot_general(
            ordered[...], d_upper_ref[:, lanes], (((0,), (0,)), ((), ())),
            preferred_element_type=F32,
        )
        rows = slice(256 + t * 64, 320 + t * 64)
        for k_x in range(4):
            keep_ref[k_x, rows, :] = tile[k_x * 64 : k_x * 64 + 64, :]
            send_ref[k_x, rows, :] = tile[256 + k_x * 64 : 320 + k_x * 64, :].astype(BF16)


def backward_kernel(
    ext_ref, mixed_ref, d_upper_ref, w_up_ref, gain_ref, kern_ref, bias_ref,
    small_ref, grad_ref, west_ref, east_ref, wide, shifted, d_normed, d_cells, moved,
):
    d_normed[...] = lax.dot_general(
        d_upper_ref[...], w_up_ref[...], (((1,), (1,)), ((), ())), preferred_element_type=F32
    )
    spread_rows(ext_ref, wide, shifted)

    def norm_step(step, gain_sum):
        rows = pl.ds(pl.multiple_of(step * 32, 32), 32)
        cells = mixed_ref[rows, :]
        center = cells - jnp.mean(cells, axis=-1, keepdims=True)
        spread = jnp.mean(center * center, axis=-1, keepdims=True)
        inverse = lax.rsqrt(spread + 1e-6)
        unit = center * inverse
        d = d_normed[rows, :]
        d_unit = d * gain_ref[...]
        along = jnp.mean(d_unit * unit, axis=-1, keepdims=True)
        d_center = (d_unit - unit * along) * inverse
        d_mixed = d_center - jnp.mean(d_center, axis=-1, keepdims=True)
        d_cells[pl.ds(step * 2, 2)] = d_mixed.reshape(2, 16, 512)
        return gain_sum + jnp.sum(d * unit, axis=0, keepdims=True)

    small_ref[49:50, :] = lax.fori_loop(0, 8, norm_step, jnp.zeros((1, 512), F32))
    small_ref[50:54, :] = bias_ref[0:4, :]
    small_ref[54:64, :] = jnp.zeros((10, 512), F32)
    moved[...] = jnp.zeros_like(moved)
    for b in range(7):
        moved[b, :, b : b + 16, :] = d_cells[...]

    def tap_step(step, carry):
        lanes = pl.ds(pl.multiple_of(step * 128, 128), 128)
        d = [d_cells[x, :, lanes] for x in range(16)]
        for b in range(7):
            totals = [jnp.zeros((8, 128), F32)] * 7
            for r in range(22):
                cells = shifted[b, r, :, lanes]
                for a in range(max(0, r - 15), min(7, r + 1)):
                    product = cells * d[r - a]
                    totals[a] = totals[a] + product[:8] + product[8:]
            for a in range(7):
                row = a * 7 + b
                small_ref[row : row + 1, lanes] = jnp.sum(totals[a], axis=0, keepdims=True)
        return carry

    lax.fori_loop(0, 4, tap_step, 0)

    def rim_step(step, carry):
        lanes = pl.ds(pl.multiple_of(step * 128, 128), 128)
        for q in range(3):
            rows = slice(q * 8, q * 8 + 8)
            totals = [jnp.zeros((8, 128), F32)] * 22
            for b in range(1 if q == 2 else 0, 7):
                weights = [kern_ref[a * 7 + b : a * 7 + b + 1, lanes] for a in range(7)]
                for x in range(16):
                    cells = moved[b, x, rows, lanes]
                    for a in range(7):
                        totals[x + a] = totals[x + a] + cells * weights[a]
            for i in range(22):
                grad_ref[i, rows, lanes] = totals[i]
        return carry

    lax.fori_loop(0, 4, rim_step, 0)
    filler = jnp.zeros((3, 8, 512), F32)
    west_ref[...] = jnp.concatenate([grad_ref[0:3], filler], axis=1).astype(BF16)
    east_ref[...] = jnp.concatenate([grad_ref[19:22], filler], axis=1).astype(BF16)


VMEM_BYTES = 30 * 1024 * 1024


def run_forward(at, ext, kern, gain, w_up, b_up, d_out, d_act, order):
    shapes = [
        ((256, 512), F32), ((256, 2048), BF16), ((8, 512), F32),
        ((4, 512, 512), F32), ((4, 512, 512), BF16),
    ]
    return pl.pallas_call(
        forward_kernel,
        out_shape=[jax.ShapeDtypeStruct(s, d) for s, d in shapes],
        in_specs=[pl.BlockSpec(memory_space=pltpu.SMEM)]
        + [pl.BlockSpec(memory_space=pltpu.VMEM)] * 8,
        out_specs=[pl.BlockSpec(memory_space=pltpu.VMEM)] * 5,
        scratch_shapes=[
            pltpu.VMEM((22, 32, 512), F32), pltpu.VMEM((7, 22, 16, 512), F32),
            pltpu.VMEM((256, 512), BF16), pltpu.VMEM((256, 512), BF16),
            pltpu.VMEM((256, 512), F32), pltpu.VMEM((256, 512), BF16), pltpu.VMEM((512, 512), F32),
        ],
        compiler_params=pltpu.CompilerParams(vmem_limit_bytes=VMEM_BYTES),
        cost_estimate=pl.CostEstimate(
            flops=14000000000, bytes_accessed=16000000, transcendentals=600000
        ),
        name="forward",
    )(at, ext, kern, gain, w_up, b_up, d_out, d_act, order)


def run_backward(ext, mixed, d_upper, w_up, gain, kern, bias):
    return pl.pallas_call(
        backward_kernel,
        out_shape=[
            jax.ShapeDtypeStruct((64, 512), F32), jax.ShapeDtypeStruct((22, 24, 512), F32),
            jax.ShapeDtypeStruct((3, 32, 512), BF16), jax.ShapeDtypeStruct((3, 32, 512), BF16),
        ],
        in_specs=[pl.BlockSpec(memory_space=pltpu.VMEM)] * 7,
        out_specs=[pl.BlockSpec(memory_space=pltpu.VMEM)] * 4,
        scratch_shapes=[
            pltpu.VMEM((22, 32, 512), F32), pltpu.VMEM((7, 22, 16, 512), F32),
            pltpu.VMEM((256, 512), F32), pltpu.VMEM((16, 16, 512), F32),
            pltpu.VMEM((7, 16, 24, 512), F32),
        ],
        compiler_params=pltpu.CompilerParams(vmem_limit_bytes=VMEM_BYTES),
        cost_estimate=pl.CostEstimate(flops=12000000000, bytes_accessed=8000000, transcendentals=300),
        name="backward",
    )(ext, mixed, d_upper, w_up, gain, kern, bias)


def first_sum_kernel(keep_ref, given_ref, own_ref, *give_refs):
    own_ref[...] = keep_ref[0] + given_ref[0].astype(F32)
    for k in range(3):
        give_refs[k][...] = (keep_ref[k + 1] + given_ref[k + 1].astype(F32)).astype(BF16)


def second_sum_kernel(own_ref, a_ref, b_ref, c_ref, half_ref, half_a, half_b, half_c, *outs):
    large_ref, terms_ref = outs[:2]
    half = (half_ref[...] + half_a[...]) + (half_b[...] + half_c[...])
    high = half.astype(BF16)
    low = (half - high.astype(F32)).astype(BF16)
    terms_ref[...] = high.astype(F32) + low.astype(F32)

    def total(rows):
        return (own_ref[rows, :] + a_ref[rows, :].astype(F32)) + (
            b_ref[rows, :].astype(F32) + c_ref[rows, :].astype(F32)
        )

    for k in range(4):
        pieces = [(slice(0, 64), slice(k * 64, k * 64 + 64))]
        for t in range(4):
            at = 256 + t * 64 + k * 16
            pieces.append((slice(64 + t * 16, 80 + t * 16), slice(at, at + 16)))
        for target, rows in pieces:
            if k == 0:
                large_ref[target, :] = total(rows)
            else:
                outs[1 + k][target, :] = total(rows).astype(BF16)
        if k:
            outs[1 + k][128:160, :] = high
            outs[1 + k][160:192, :] = low


def third_sum_kernel(at_ref, large_ref, terms_ref, a_ref, b_ref, c_ref, *outs):
    own_ref, half_ref, blocks = outs[0], outs[1], outs[5]
    low = at_ref[3] & 3

    def total(rows):
        return (large_ref[rows, :] + a_ref[rows, :].astype(F32)) + (
            b_ref[rows, :].astype(F32) + c_ref[rows, :].astype(F32)
        )

    def term(ref):
        return ref[128:160, :].astype(F32) + ref[160:192, :].astype(F32)

    half = (terms_ref[...] + term(a_ref)) + (term(b_ref) + term(c_ref))
    half_ref[...] = half
    down = total(slice(0, 64))
    up = total(slice(64, 128))
    for z in range(8):
        rows = [up[t * 16 + z * 2 : t * 16 + z * 2 + 2] for t in range(4)]
        blocks[z] = jnp.concatenate([down[z * 8 : z * 8 + 8]] + rows, axis=0)
    for k in range(4):
        for z_high in range(2):
            block = blocks[z_high * 4 + (low ^ k)]
            (own_ref if k == 0 else outs[1 + k])[z_high * 16 : z_high * 16 + 16, :] = block
        if k:
            outs[1 + k][32:64, :] = half


def fourth_sum_kernel(at_ref, own_ref, half_ref, a_ref, b_ref, c_ref, keep_ref, sum_ref, give_ref):
    high = at_ref[3] >> 2

    def total(rows):
        return (own_ref[rows, :] + a_ref[rows, :]) + (b_ref[rows, :] + c_ref[rows, :])

    rest = slice(32, 64)
    half = (half_ref[...] + a_ref[rest, :]) + (b_ref[rest, :] + c_ref[rest, :])
    keep_ref[...] = total(pl.ds(pl.multiple_of(high * 16, 16), 16))
    give_ref[0:16, :] = total(pl.ds(pl.multiple_of((1 - high) * 16, 16), 16))
    give_ref[16:48, :] = half
    sum_ref[...] = half


def last_sum_kernel(keep_ref, half_ref, got_ref, down_ref, up_ref, sum_ref):
    sum_ref[...] = half_ref[...] + got_ref[16:48, :]
    down_ref[...] = keep_ref[0:8, :] + got_ref[0:8, :]
    up = keep_ref[8:16, :] + got_ref[8:16, :]
    for t in range(4):
        up_ref[:, t * 512 : t * 512 + 512] = up[t * 2 : t * 2 + 2]


def local_call(kernel, shapes, operands, name, scalars=0, scratch=()):
    return pl.pallas_call(
        kernel,
        out_shape=[jax.ShapeDtypeStruct(s, d) for s, d in shapes],
        in_specs=[pl.BlockSpec(memory_space=pltpu.SMEM)] * scalars
        + [pl.BlockSpec(memory_space=pltpu.VMEM)] * (len(operands) - scalars),
        out_specs=[pl.BlockSpec(memory_space=pltpu.VMEM)] * len(shapes),
        scratch_shapes=list(scratch),
        compiler_params=pltpu.CompilerParams(vmem_limit_bytes=VMEM_BYTES),
        cost_estimate=pl.CostEstimate(flops=800000000, bytes_accessed=2000000, transcendentals=0),
        name=name,
    )(*operands)


def per_device(
    field, cotangent, land_sea, fold_partner, depth_kernel, norm_gain, w_up, b_up, w_down
):
    width_lon, width_lat, channels = field.shape
    lon_at = lax.axis_index("lon")
    lat_at = lax.axis_index("lat")
    core = lon_at % 2
    z_at = (lon_at // 2) % 8
    y_at = (lat_at // 4) * 2 + lon_at // 16
    x_at = lat_at % 4
    is_north = lat_at == lax.axis_size("lat") - 1
    from_end = 511 - fold_partner[0]
    turn = 31 - from_end // 16
    shift = 16 - from_end % 16

    lat_ext = extended_2(field, (("lat", 1),), 3, False)
    top_rows = field[:, width_lat - 3 :, :]
    mine = mirror_tiles(top_rows, turn // 2)
    from_next = to_previous(mine)
    from_previous = to_next(mine)
    even = turn % 2 == 0
    low = jnp.where(even, from_next, mine)
    high = jnp.where(even, mine, from_previous)
    facing = lax.dynamic_slice_in_dim(jnp.concatenate([low, high], axis=0), shift, 16, axis=0)
    fold_band = facing[::-1, ::-1, :]
    upper_rim = jnp.where(is_north, fold_band, lat_ext[:, width_lat + 3 :, :])
    lat_ext = jnp.concatenate([lat_ext[:, : width_lat + 3, :], upper_rim], axis=1)
    extended = extended_2(lat_ext, (("lon", 0),), 3, True)
    extended = jnp.pad(extended, ((0, 0), (0, 10), (0, 0)))
    tokens = width_lon * width_lat
    d_out = cotangent.reshape(tokens, channels) * land_sea.reshape(tokens, 1).astype(jnp.bfloat16)
    d_act = lax.dot_general(
        d_out, w_down, (((1,), (1,)), ((), ())), preferred_element_type=jnp.float32
    )
    row = jnp.arange(512, dtype=jnp.int32)
    block = row >> 1
    y_of = (((block >> 2) & 1) << 1) + (block >> 7)
    goes_to = (
        (((block >> 3) & 1) ^ core) * 256
        + ((block & 3) ^ x_at) * 64
        + (y_of ^ y_at) * 16
        + ((block >> 4) & 7) * 2
        + (row & 1)
    )
    order = (goes_to[:, None] == row[None, :]).astype(jnp.bfloat16)
    at = jnp.stack([core, x_at, y_at, z_at]).astype(jnp.int32)
    gain = norm_gain.reshape(1, channels)
    mixed, d_upper, bias, keep, give = run_forward(
        at, extended, depth_kernel, gain, w_up, b_up.reshape(1, 2048), d_out, d_act, order
    )

    given = send(give, CORE_MASK)
    own, *give = local_call(
        first_sum_kernel, [((512, 512), F32)] + [((512, 512), BF16)] * 3, [keep, given], "first_sum"
    )
    own, give, mixed = lax.optimization_barrier((own, give, mixed))
    taken = [send(piece, mask) for piece, mask in zip(give, X_MASKS)]

    small, grad_ext, west_rim, east_rim = run_backward(
        extended, mixed, d_upper, w_up, gain, depth_kernel, bias
    )

    small = small.reshape(2, 32, 512)
    half = lax.dynamic_index_in_dim(small, core, 0, False) + send(
        lax.dynamic_index_in_dim(small, 1 - core, 0, False), CORE_MASK
    )
    half, taken = lax.optimization_barrier((half, taken))
    halves = [half] + [send(half, mask) for mask in X_MASKS]

    rim = jnp.bfloat16
    from_west = to_next(east_rim)[:, :22].astype(jnp.float32)
    from_east = to_previous(west_rim)[:, :22].astype(jnp.float32)
    by_cols = (
        grad_ext[3:19, :22]
        + jnp.pad(from_west, ((0, 13), (0, 0), (0, 0)))
        + jnp.pad(from_east, ((13, 0), (0, 0), (0, 0)))
    )

    top_rim = by_cols[:, 19:22].astype(rim)
    from_south = lax.ppermute(top_rim, "lat", [(i, i + 1) for i in range(7)])
    from_north = lax.ppermute(by_cols[:, 0:3].astype(rim), "lat", [(i + 1, i) for i in range(7)])
    fold_strip = jnp.where(is_north, top_rim, jnp.zeros_like(top_rim))
    spread = lax.dynamic_update_slice_in_dim(
        jnp.zeros((32, 3, channels), rim), fold_strip[::-1, ::-1, :], shift, axis=0
    )
    none = jnp.zeros_like(spread[:16])
    mine = jnp.where(even, spread[16:], spread[:16])
    mine = mine + to_next(jnp.where(even, spread[:16], none))
    mine = mine + to_previous(jnp.where(even, none, spread[16:]))
    from_fold = mirror_tiles(mine, turn >> 1)

    large, terms, *give = local_call(
        second_sum_kernel,
        [((128, 512), F32), ((32, 512), F32)] + [((192, 512), BF16)] * 3,
        [own, *taken, *halves],
        "second_sum",
    )
    taken = [send(piece, mask) for piece, mask in zip(give, Y_MASKS)]

    own, half, *give = local_call(
        third_sum_kernel,
        [((32, 512), F32), ((32, 512), F32)] + [((64, 512), F32)] * 3,
        [at, large, terms, *taken],
        "third_sum",
        scalars=1,
        scratch=[pltpu.VMEM((8, 16, 512), F32)],
    )
    taken = [send(piece, mask) for piece, mask in zip(give, Z_MASKS[:3])]
    keep, half, give = local_call(
        fourth_sum_kernel,
        [((16, 512), F32), ((32, 512), F32), ((48, 512), F32)],
        [at, own, half, *taken],
        "fourth_sum",
        scalars=1,
    )
    grad_down, grad_up, half = local_call(
        last_sum_kernel,
        [((8, 512), F32), ((2, 2048), F32), ((32, 512), F32)],
        [keep, half, send(give, Z_MASKS[3])],
        "last_sum",
    )
    other = send(half, CORE_MASK)
    small = jnp.where(
        core == 0,
        jnp.concatenate([half, other], axis=0),
        jnp.concatenate([other, half], axis=0),
    )
    grad_kernel = small[:49]
    grad_gain = small[49]
    grad_bias = small[50:54].reshape(2048)

    from_south = jnp.pad(from_south, ((0, 0), (0, 13), (0, 0)))
    from_north = jnp.pad(from_north, ((0, 0), (13, 0), (0, 0)))
    from_fold = jnp.pad(from_fold, ((0, 0), (13, 0), (0, 0)))
    owned = by_cols[:, 3:19] + from_south.astype(jnp.float32) + from_north.astype(jnp.float32)
    owned = owned + from_fold.astype(jnp.float32)
    grad_field = (cotangent.astype(jnp.float32) + owned).astype(jnp.bfloat16)
    return (grad_field, grad_up, grad_down, grad_kernel, grad_gain, grad_bias)


def solution(mesh):
    placed = (
        P("lon", "lat", None),
        P("lon", "lat", None),
        P("lon", "lat"),
        P(),
        P(),
        P(),
        P(),
        P(),
        P(),
    )
    return jax.shard_map(
        per_device,
        mesh=mesh,
        in_specs=placed,
        out_specs=(
            P("lon", "lat", None),
            P(("lon", "lat"), None),
            P(("lon", "lat"), None),
            P(),
            P(),
            P(),
        ),
        check_vma=False,
    )
```

profile of v0, /device:TPU:7, one launch (start us, length us, event | category | flops | bytes accessed | tf_op | source)
XLA Modules:
  0.0 149.5 jit_solution(1107111282112653270)
XLA Ops:
  0.6 1.3 slice.102
  2.7 1.0 fusion.17
  3.7 1.3 conditional.2
  3.7 1.3 collective-permute-start.6
  5.0 0.7 collective-permute-start.33
  5.7 1.5 %collective-permute-start.34 = (bf16[16,3,512]{2,1,0:T(4,128)(2,1)}, bf16[16,3,512]{2,1,0:T(4,128)(2,1)S(1)}, u32[]{:S(2)}, u32[]{:S(2)}) collective-permute-start(bf16[16,3,512]{2,1,0:T(4,128)(2,1)} %get-tuple-element.161), channel_id=1, source_target_pairs={{0,8},{8,16},{16,24},{24,32},{32,40},{40,48},{48,56},{56,64},{64,7... | collective-permute-start | bytes 147464 | tf_op jit(solution)/shard_map/ppermute | solution.py:58
  7.2 4.7 %collective-permute-start.32 = (bf16[16,3,512]{2,1,0:T(4,128)(2,1)S(1)}, bf16[16,3,512]{2,1,0:T(4,128)(2,1)S(1)}, u32[]{:S(2)}, u32[]{:S(2)}) collective-permute-start(bf16[16,3,512]{2,1,0:T(4,128)(2,1)S(1)} %get-tuple-element.156), channel_id=1, source_target_pairs={{0,1},{1,2},{2,3},{3,4},{4,5},{5,6},{6,7},{8,9},{9,10},{10,11},{11... | collective-permute-start | bytes 147464 | tf_op jit(solution)/shard_map/ppermute | solution.py:17
  12.0 1.9 %collective-permute-start.35 = (bf16[16,3,512]{2,1,0:T(4,128)(2,1)S(1)}, bf16[16,3,512]{2,1,0:T(4,128)(2,1)S(1)}, u32[]{:S(2)}, u32[]{:S(2)}) collective-permute-start(bf16[16,3,512]{2,1,0:T(4,128)(2,1)S(1)} %get-tuple-element.155), channel_id=1, source_target_pairs={{1,0},{2,1},{3,2},{4,3},{5,4},{6,5},{7,6},{9,8},{10,9},{11,10},{12... | collective-permute-start | bytes 147464 | tf_op jit(solution)/shard_map/ppermute | solution.py:19
  13.9 0.7 convert_element_type.45
  14.7 1.1 bitcast_multiply_fusion.d_out_ref
  15.8 2.0 %fusion.18.d_act_ref = f32[256,2048]{1,0:T(8,128)} fusion(bf16[256,512]{1,0:T(8,128)(2,1)S(1)} %bitcast_multiply_fusion.d_out_ref, bf16[2048,512]{1,0:T(8,128)(2,1)S(1)} %copy-done), kind=kOutput, calls=%fused_computation.42 | convolution fusion | flops 536870912 | bytes 4456448 | tf_op jit(solution)/shard_map/dot_general | solution.py:399
  17.9 1.0 fusion.5.order_ref
  18.9 1.0 broadcast_select_fusion.2
  20.2 0.4 collective-permute-done.35
  20.7 2.4 %collective-permute-start.36 = (bf16[3,22,512]{2,1,0:T(8,128)(2,1)S(1)}, bf16[3,22,512]{2,1,0:T(8,128)(2,1)S(1)}, u32[]{:S(2)}, u32[]{:S(2)}) collective-permute-start(bf16[3,22,512]{2,1,0:T(8,128)(2,1)S(1)} %get-tuple-element.153), channel_id=1, source_target_pairs={{0,8},{8,16},{16,24},{24,32},{32,40},{40,48},{48,56},{56,64},{64,7... | collective-permute-start | bytes 202760 | tf_op jit(solution)/shard_map/ppermute | solution.py:17
  23.2 3.7 %collective-permute-start.37 = (bf16[3,22,512]{2,1,0:T(8,128)(2,1)S(1)}, bf16[3,22,512]{2,1,0:T(8,128)(2,1)S(1)}, u32[]{:S(2)}, u32[]{:S(2)}) collective-permute-start(bf16[3,22,512]{2,1,0:T(8,128)(2,1)S(1)} %get-tuple-element.154), channel_id=1, source_target_pairs={{8,0},{16,8},{24,16},{32,24},{40,32},{48,40},{56,48},{64,56},{72,6... | collective-permute-start | bytes 202760 | tf_op jit(solution)/shard_map/ppermute | solution.py:19
  26.9 0.6 collective-permute-done.36
  27.7 1.2 fusion.7.ext_ref
  29.0 1.6 %copy-done.3 = f32[256,2048]{1,0:T(8,128)S(1)} copy-done((f32[256,2048]{1,0:T(8,128)S(1)}, f32[256,2048]{1,0:T(8,128)}, u32[]{:S(2)}) %copy-start.3) | copy-done | bytes 2097176
  30.6 1.6 %copy-done.6 = bf16[512,2048]{1,0:T(8,128)(2,1)S(1)} copy-done((bf16[512,2048]{1,0:T(8,128)(2,1)S(1)}, bf16[512,2048]{1,0:T(8,128)(2,1)}, u32[]{:S(2)}) %copy-start.6) | copy-done | bytes 2097176
  32.2 11.6 %forward.1 = (f32[256,512]{1,0:T(8,128)S(1)}, bf16[256,2048]{1,0:T(8,128)(2,1)S(1)}, f32[8,512]{1,0:T(8,128)S(1)}, f32[4,512,512]{2,1,0:T(8,128)S(1)}, bf16[4,512,512]{2,1,0:T(8,128)(2,1)}) custom-call(s32[4]{0:T(128)S(1)} %pad_add_fusion.at_ref, bf16[22,32,512]{2,1,0:T(8,128)(2,1)S(1)} %fusion.7.ext_ref, f32[49,512]{1,0:T(8,128)S(1)} %copy-done.10, ...), custom_call_target="tpu_custom_call" | custom-call | flops 14000000000 | bytes 16000000 | tf_op jit(solution)/shard_map/forward/pallas_call | solution.py:233
  43.8 2.0 %copy-done.1 = f32[4,512,512]{2,1,0:T(8,128)} copy-done((f32[4,512,512]{2,1,0:T(8,128)}, f32[4,512,512]{2,1,0:T(8,128)S(1)}, u32[]{:S(2)}) %copy-start.1) | copy-done | bytes 4194328
  45.8 1.0 copy-done.15
  46.8 0.8 copy-done.17
  47.6 4.9 %collective-permute-start.38 = (bf16[4,512,512]{2,1,0:T(8,128)(2,1)}, bf16[4,512,512]{2,1,0:T(8,128)(2,1)}, u32[]{:S(2)}, u32[]{:S(2)}) collective-permute-start(bf16[4,512,512]{2,1,0:T(8,128)(2,1)} %get-tuple-element.111), channel_id=1, source_target_pairs={{0,8},{1,9},{2,10},{3,11},{4,12},{5,13},{6,14},{7,15},{8,0},{9,1},... | collective-permute-start | bytes 6291464 | tf_op jit(solution)/shard_map/ppermute | solution.py:30
  52.5 4.1 %collective-permute-done.38.given_ref = bf16[4,512,512]{2,1,0:T(8,128)(2,1)} collective-permute-done((bf16[4,512,512]{2,1,0:T(8,128)(2,1)}, bf16[4,512,512]{2,1,0:T(8,128)(2,1)}, u32[]{:S(2)}, u32[]{:S(2)}) %collective-permute-start.38) | collective-permute-done | bytes 2097184 | tf_op jit(solution)/shard_map/ppermute | solution.py:30
  56.6 2.2 %copy-done.2 = f32[4,512,512]{2,1,0:T(8,128)S(1)} copy-done((f32[4,512,512]{2,1,0:T(8,128)S(1)}, f32[4,512,512]{2,1,0:T(8,128)}, u32[]{:S(2)}) %copy-start.2) | copy-done | bytes 4194328
  58.8 3.1 %first_sum.1 = (f32[512,512]{1,0:T(8,128)S(1)}, bf16[512,512]{1,0:T(8,128)(2,1)}, bf16[512,512]{1,0:T(8,128)(2,1)}, bf16[512,512]{1,0:T(8,128)(2,1)}) custom-call(f32[4,512,512]{2,1,0:T(8,128)S(1)} %copy-done.2, bf16[4,512,512]{2,1,0:T(8,128)(2,1)} %collective-permute-done.38.given_ref), custom_call_target="tpu_custom_call" | custom-call | flops 800000000 | bytes 2000000 | tf_op jit(solution)/shard_map/first_sum/pallas_call | solution.py:355
  61.9 3.8 %collective-permute-start.48 = (bf16[512,512]{1,0:T(8,128)(2,1)}, bf16[512,512]{1,0:T(8,128)(2,1)}, u32[]{:S(2)}, u32[]{:S(2)}) collective-permute-start(bf16[512,512]{1,0:T(8,128)(2,1)} %get-tuple-element.127), channel_id=1, source_target_pairs={{0,3},{1,2},{2,1},{3,0},{4,7},{5,6},{6,5},{7,4},{8,11},{9,10},{10,... | collective-permute-start | bytes 1572872 | tf_op jit(solution)/shard_map/ppermute | solution.py:30
  65.8 9.9 %backward.1 = (f32[64,512]{1,0:T(8,128)S(1)}, f32[22,24,512]{2,1,0:T(8,128)S(1)}, bf16[3,32,512]{2,1,0:T(8,128)(2,1)S(1)}, bf16[3,32,512]{2,1,0:T(8,128)(2,1)S(1)}) custom-call(bf16[22,32,512]{2,1,0:T(8,128)(2,1)S(1)} %fusion.7.ext_ref, f32[256,512]{1,0:T(8,128)S(1)} %copy-done.18, bf16[256,2048]{1,0:T(8,128)(2,1)S(1)} %copy-done.16, ...), custom_call_target="tpu_custom_call" | custom-call | flops 12000000000 | bytes 8000000 | tf_op jit(solution)/shard_map/backward/pallas_call | solution.py:253
  75.8 1.0 copy-done.4
  76.7 1.2 collective-permute-start.45
  77.9 0.9 collective-permute-done.45
  79.6 3.7 %collective-permute-done.40 = bf16[3,32,512]{2,1,0:T(8,128)(2,1)S(1)} collective-permute-done((bf16[3,32,512]{2,1,0:T(8,128)(2,1)S(1)}, bf16[3,32,512]{2,1,0:T(8,128)(2,1)S(1)}, u32[]{:S(2)}, u32[]{:S(2)}) %collective-permute-start.40) | collective-permute-done | bytes 98336 | tf_op jit(solution)/shard_map/ppermute | solution.py:62
  83.3 1.5 collective-permute-done.47.b_ref
  84.8 3.9 %collective-permute-done.48.c_ref = bf16[512,512]{1,0:T(8,128)(2,1)} collective-permute-done((bf16[512,512]{1,0:T(8,128)(2,1)}, bf16[512,512]{1,0:T(8,128)(2,1)}, u32[]{:S(2)}, u32[]{:S(2)}) %collective-permute-start.48) | collective-permute-done | bytes 524320 | tf_op jit(solution)/shard_map/ppermute | solution.py:30
  88.7 3.5 %collective-permute-start.50 = (f32[32,512]{1,0:T(8,128)S(1)}, f32[32,512]{1,0:T(8,128)S(1)}, u32[]{:S(2)}, u32[]{:S(2)}) collective-permute-start(f32[32,512]{1,0:T(8,128)S(1)} %bitcast_add_fusion.half_ref), channel_id=1, source_target_pairs={{0,2},{1,3},{2,0},{3,1},{4,6},{5,7},{6,4},{7,5},{8,10},{9,11},{10,... | collective-permute-start | bytes 196616 | tf_op jit(solution)/shard_map/ppermute | solution.py:30
  92.6 2.2 %fusion.15 = (bf16[16,22,512]{2,1,0:T(8,128)(2,1)S(1)}, f32[16,22,512]{2,1,0:T(8,128)}) fusion(bf16[3,22,512]{2,1,0:T(8,128)(2,1)S(1)} %slice.118, bf16[3,22,512]{2,1,0:T(8,128)(2,1)S(1)} %slice.117, f32[22,24,512]{2,1,0:T(8,128)} %copy-done.4), kind=kLoop, calls=%fused_computation.39 | loop fusion | flops 901120 | bytes 1937408 | tf_op jit(solution)/shard_map/convert.5
  94.7 2.5 %collective-permute-done.51.half_c = f32[32,512]{1,0:T(8,128)S(1)} collective-permute-done((f32[32,512]{1,0:T(8,128)S(1)}, f32[32,512]{1,0:T(8,128)S(1)}, u32[]{:S(2)}, u32[]{:S(2)}) %collective-permute-start.51) | collective-permute-done | bytes 65568 | tf_op jit(solution)/shard_map/ppermute | solution.py:30
  97.3 1.6 %second_sum.1 = (f32[128,512]{1,0:T(8,128)S(1)}, f32[32,512]{1,0:T(8,128)S(1)}, bf16[192,512]{1,0:T(8,128)(2,1)S(1)}, bf16[192,512]{1,0:T(8,128)(2,1)S(1)}, bf16[192,512]{1,0:T(8,128)(2,1)S(1)}) custom-call(f32[512,512]{1,0:T(8,128)S(1)} %copy-done.9, bf16[512,512]{1,0:T(8,128)(2,1)} %collective-permute-done.46.a_ref, ...), custom_call_target="tpu_custom_call" | custom-call | flops 800000000 | bytes 2000000 | tf_op jit(solution)/shard_map/second_sum/pallas_call | solution.py:355
  98.9 0.6 copy-done.13
  99.5 6.4 %collective-permute-start.53 = (bf16[192,512]{1,0:T(8,128)(2,1)S(1)}, bf16[192,512]{1,0:T(8,128)(2,1)S(1)}, u32[]{:S(2)}, u32[]{:S(2)}) collective-permute-start(bf16[192,512]{1,0:T(8,128)(2,1)S(1)} %get-tuple-element.135), channel_id=1, source_target_pairs={{0,4},{1,5},{2,6},{3,7},{4,0},{5,1},{6,2},{7,3},{8,12},{9,13},{10,... | collective-permute-start | bytes 589832 | tf_op jit(solution)/shard_map/ppermute | solution.py:30
  105.9 0.7 fusion.16
  106.6 2.7 %rev.7 = bf16[16,3,512]{2,1,0:T(4,128)(2,1)} reverse(bf16[16,3,512]{2,1,0:T(4,128)(2,1)} %get-tuple-element.151), dimensions={0,1} | reverse | bytes 98304 | tf_op jit(solution)/shard_map/rev | solution.py:451
  109.4 0.9 constant_dynamic-update-slice_fusion
  110.3 1.6 %collective-permute-done.53.b_ref = bf16[192,512]{1,0:T(8,128)(2,1)S(1)} collective-permute-done((bf16[192,512]{1,0:T(8,128)(2,1)S(1)}, bf16[192,512]{1,0:T(8,128)(2,1)S(1)}, u32[]{:S(2)}, u32[]{:S(2)}) %collective-permute-start.53) | collective-permute-done | bytes 196640 | tf_op jit(solution)/shard_map/ppermute | solution.py:30
  111.9 1.4 collective-permute-done.54.c_ref
  113.3 0.8 copy-done.14
  114.2 0.7 third_sum.1
  114.9 3.8 %collective-permute-start.56 = (f32[64,512]{1,0:T(8,128)S(1)}, f32[64,512]{1,0:T(8,128)S(1)}, u32[]{:S(2)}, u32[]{:S(2)}) collective-permute-start(f32[64,512]{1,0:T(8,128)S(1)} %get-tuple-element.140), channel_id=1, source_target_pairs={{0,32},{1,33},{2,34},{3,35},{4,36},{5,37},{6,38},{7,39},{8,40},{9,... | collective-permute-start | bytes 393224 | tf_op jit(solution)/shard_map/ppermute | solution.py:30
  118.9 5.7 %collective-permute-start.43 = (bf16[16,3,512]{2,1,0:T(4,128)(2,1)S(1)}, bf16[16,3,512]{2,1,0:T(4,128)(2,1)S(1)}, u32[]{:S(2)}, u32[]{:S(2)}) collective-permute-start(bf16[16,3,512]{2,1,0:T(4,128)(2,1)S(1)} %get-tuple-element.157), channel_id=1, source_target_pairs={{0,8},{8,16},{16,24},{24,32},{32,40},{40,48},{48,56},{56,64},{64,7... | collective-permute-start | bytes 147464 | tf_op jit(solution)/shard_map/ppermute | solution.py:58
  124.7 1.9 %collective-permute-start.41 = (bf16[16,3,512]{2,1,0:T(4,128)(2,1)}, bf16[16,3,512]{2,1,0:T(4,128)(2,1)S(1)}, u32[]{:S(2)}, u32[]{:S(2)}) collective-permute-start(bf16[16,3,512]{2,1,0:T(4,128)(2,1)} %get-tuple-element.150), channel_id=1, source_target_pairs={{0,1},{1,2},{2,3},{3,4},{4,5},{5,6},{6,7},{8,9},{9,10},{10,11},{11... | collective-permute-start | bytes 147464 | tf_op jit(solution)/shard_map/ppermute | solution.py:447
  126.6 3.4 %collective-permute-start.42 = (bf16[16,3,512]{2,1,0:T(4,128)(2,1)}, bf16[16,3,512]{2,1,0:T(4,128)(2,1)S(1)}, u32[]{:S(2)}, u32[]{:S(2)}) collective-permute-start(bf16[16,3,512]{2,1,0:T(4,128)(2,1)} %get-tuple-element.152), channel_id=1, source_target_pairs={{1,0},{2,1},{3,2},{4,3},{5,4},{6,5},{7,6},{9,8},{10,9},{11,10},{12... | collective-permute-start | bytes 147464 | tf_op jit(solution)/shard_map/ppermute | solution.py:448
  130.0 0.6 fourth_sum.1
  130.6 4.2 %collective-permute-start.58 = (f32[48,512]{1,0:T(8,128)S(1)}, f32[48,512]{1,0:T(8,128)S(1)}, u32[]{:S(2)}, u32[]{:S(2)}) collective-permute-start(f32[48,512]{1,0:T(8,128)S(1)} %get-tuple-element.144), channel_id=1, source_target_pairs={{0,64},{1,65},{2,66},{3,67},{4,68},{5,69},{6,70},{7,71},{8,72},{9,... | collective-permute-start | bytes 294920 | tf_op jit(solution)/shard_map/ppermute | solution.py:30
  134.9 1.3 conditional.3
  134.9 1.3 collective-permute-start.22
  136.2 1.9 %collective-permute-done.58.got_ref = f32[48,512]{1,0:T(8,128)S(1)} collective-permute-done((f32[48,512]{1,0:T(8,128)S(1)}, f32[48,512]{1,0:T(8,128)S(1)}, u32[]{:S(2)}, u32[]{:S(2)}) %collective-permute-start.58) | collective-permute-done | bytes 98336 | tf_op jit(solution)/shard_map/ppermute | solution.py:30
  138.1 0.6 last_sum.1
  138.7 7.2 %collective-permute-start.59 = (f32[32,512]{1,0:T(8,128)S(1)}, f32[32,512]{1,0:T(8,128)S(1)}, u32[]{:S(2)}, u32[]{:S(2)}) collective-permute-start(f32[32,512]{1,0:T(8,128)S(1)} %get-tuple-element.147), channel_id=1, source_target_pairs={{0,8},{1,9},{2,10},{3,11},{4,12},{5,13},{6,14},{7,15},{8,0},{9,1},... | collective-permute-start | bytes 196616 | tf_op jit(solution)/shard_map/ppermute | solution.py:30
  145.9 1.8 %fusion.13 = bf16[16,16,512]{2,1,0:T(8,128)(2,1)} fusion(f32[16,22,512]{2,1,0:T(8,128)S(1)} %copy-done.19, bf16[16,16,512]{2,1,0:T(8,128)(2,1)S(1)} %copy-done.21, bf16[16,3,512]{2,1,0:T(4,128)(2,1)} %get-tuple-element.162, bf16[16,3,512]{2,1,0:T(4,128)(2,1)S(1)} %collective-permute-done.42, bf16[16,3,512]{2,1,0:T(4,128)(2,1)S(1)} %collective-permute-done.41), kind=kLoop, calls=%fused_computation.17 | loop fusion | flops 1179648 | bytes 1196032 | tf_op jit(solution)/shard_map/convert_element_type | solution.py:504
  147.7 0.7 slice.124
  148.3 0.6 slice.125
  148.9 0.6 copy.15
  (81 shorter events, 2.5 us)
Async XLA Ops:
  0.6 15.2 %copy-start = (bf16[2048,512]{1,0:T(8,128)(2,1)S(1)}, bf16[2048,512]{1,0:T(8,128)(2,1)}, u32[]{:S(2)}) copy-start(bf16[2048,512]{1,0:T(8,128)(2,1)} %param.49) | copy-start | bytes 6291460
  3.7 1.3 collective-permute-start.6
  5.0 13.8 %collective-permute-start.33 = (bf16[16,3,512]{2,1,0:T(4,128)(2,1)}, bf16[16,3,512]{2,1,0:T(4,128)(2,1)S(1)}, u32[]{:S(2)}, u32[]{:S(2)}) collective-permute-start(bf16[16,3,512]{2,1,0:T(4,128)(2,1)} %get-tuple-element.161), channel_id=1, source_target_pairs={{8,0},{16,8},{24,16},{32,24},{40,32},{48,40},{56,48},{64,56},{72,6... | collective-permute-start | bytes 147464 | tf_op jit(solution)/shard_map/ppermute | solution.py:62
  5.7 13.1 %collective-permute-start.34 = (bf16[16,3,512]{2,1,0:T(4,128)(2,1)}, bf16[16,3,512]{2,1,0:T(4,128)(2,1)S(1)}, u32[]{:S(2)}, u32[]{:S(2)}) collective-permute-start(bf16[16,3,512]{2,1,0:T(4,128)(2,1)} %get-tuple-element.161), channel_id=1, source_target_pairs={{0,8},{8,16},{16,24},{24,32},{32,40},{40,48},{48,56},{56,64},{64,7... | collective-permute-start | bytes 147464 | tf_op jit(solution)/shard_map/ppermute | solution.py:58
  7.2 13.4 %collective-permute-start.32 = (bf16[16,3,512]{2,1,0:T(4,128)(2,1)S(1)}, bf16[16,3,512]{2,1,0:T(4,128)(2,1)S(1)}, u32[]{:S(2)}, u32[]{:S(2)}) collective-permute-start(bf16[16,3,512]{2,1,0:T(4,128)(2,1)S(1)} %get-tuple-element.156), channel_id=1, source_target_pairs={{0,1},{1,2},{2,3},{3,4},{4,5},{5,6},{6,7},{8,9},{9,10},{10,11},{11... | collective-permute-start | bytes 147464 | tf_op jit(solution)/shard_map/ppermute | solution.py:17
  12.0 8.6 %collective-permute-start.35 = (bf16[16,3,512]{2,1,0:T(4,128)(2,1)S(1)}, bf16[16,3,512]{2,1,0:T(4,128)(2,1)S(1)}, u32[]{:S(2)}, u32[]{:S(2)}) collective-permute-start(bf16[16,3,512]{2,1,0:T(4,128)(2,1)S(1)} %get-tuple-element.155), channel_id=1, source_target_pairs={{1,0},{2,1},{3,2},{4,3},{5,4},{6,5},{7,6},{9,8},{10,9},{11,10},{12... | collective-permute-start | bytes 147464 | tf_op jit(solution)/shard_map/ppermute | solution.py:19
  17.9 2.8 %copy-start.20 = (bf16[16,16,512]{2,1,0:T(8,128)(2,1)S(1)}, bf16[16,16,512]{2,1,0:T(8,128)(2,1)}, u32[]{:S(2)}) copy-start(bf16[16,16,512]{2,1,0:T(8,128)(2,1)} %param.41) | copy-start | bytes 786436
  18.8 10.1 %copy-start.10 = (f32[49,512]{1,0:T(8,128)S(1)}, f32[49,512]{1,0:T(8,128)}, u32[]{:S(2)}) copy-start(f32[49,512]{1,0:T(8,128)} %kern_ref.3) | copy-start | bytes 301060
  18.8 10.1 %copy-start.11 = (f32[2048]{0:T(1024)S(1)}, f32[2048]{0:T(1024)}, u32[]{:S(2)}) copy-start(f32[2048]{0:T(1024)} %param.48) | copy-start | bytes 24580
  18.8 10.1 %copy-start.12 = (f32[512]{0:T(512)S(1)}, f32[512]{0:T(512)}, u32[]{:S(2)}) copy-start(f32[512]{0:T(512)} %param.46) | copy-start | bytes 6148
  20.2 8.8 %copy-start.5 = (bf16[512,512]{1,0:T(8,128)(2,1)S(1)}, bf16[512,512]{1,0:T(8,128)(2,1)}, u32[]{:S(2)}) copy-start(bf16[512,512]{1,0:T(8,128)(2,1)} %fusion.5.order_ref) | copy-start | bytes 1572868
  20.7 6.8 %collective-permute-start.36 = (bf16[3,22,512]{2,1,0:T(8,128)(2,1)S(1)}, bf16[3,22,512]{2,1,0:T(8,128)(2,1)S(1)}, u32[]{:S(2)}, u32[]{:S(2)}) collective-permute-start(bf16[3,22,512]{2,1,0:T(8,128)(2,1)S(1)} %get-tuple-element.153), channel_id=1, source_target_pairs={{0,8},{8,16},{16,24},{24,32},{32,40},{40,48},{48,56},{56,64},{64,7... | collective-permute-start | bytes 202760 | tf_op jit(solution)/shard_map/ppermute | solution.py:17
  23.2 4.6 %collective-permute-start.37 = (bf16[3,22,512]{2,1,0:T(8,128)(2,1)S(1)}, bf16[3,22,512]{2,1,0:T(8,128)(2,1)S(1)}, u32[]{:S(2)}, u32[]{:S(2)}) collective-permute-start(bf16[3,22,512]{2,1,0:T(8,128)(2,1)S(1)} %get-tuple-element.154), channel_id=1, source_target_pairs={{8,0},{16,8},{24,16},{32,24},{40,32},{48,40},{56,48},{64,56},{72,6... | collective-permute-start | bytes 202760 | tf_op jit(solution)/shard_map/ppermute | solution.py:19
  29.0 1.6 %copy-start.3 = (f32[256,2048]{1,0:T(8,128)S(1)}, f32[256,2048]{1,0:T(8,128)}, u32[]{:S(2)}) copy-start(f32[256,2048]{1,0:T(8,128)} %fusion.18.d_act_ref) | copy-start | bytes 6291460
  30.6 1.6 %copy-start.6 = (bf16[512,2048]{1,0:T(8,128)(2,1)S(1)}, bf16[512,2048]{1,0:T(8,128)(2,1)}, u32[]{:S(2)}) copy-start(bf16[512,2048]{1,0:T(8,128)(2,1)} %w_up_ref.3) | copy-start | bytes 6291460
  43.8 2.0 %copy-start.1 = (f32[4,512,512]{2,1,0:T(8,128)}, f32[4,512,512]{2,1,0:T(8,128)S(1)}, u32[]{:S(2)}) copy-start(f32[4,512,512]{2,1,0:T(8,128)S(1)} %get-tuple-element.110.keep_ref) | copy-start | bytes 12582916
  45.8 1.0 copy-start.15
  46.8 0.8 copy-start.17
  47.6 9.0 %collective-permute-start.38 = (bf16[4,512,512]{2,1,0:T(8,128)(2,1)}, bf16[4,512,512]{2,1,0:T(8,128)(2,1)}, u32[]{:S(2)}, u32[]{:S(2)}) collective-permute-start(bf16[4,512,512]{2,1,0:T(8,128)(2,1)} %get-tuple-element.111), channel_id=1, source_target_pairs={{0,8},{1,9},{2,10},{3,11},{4,12},{5,13},{6,14},{7,15},{8,0},{9,1},... | collective-permute-start | bytes 6291464 | tf_op jit(solution)/shard_map/ppermute | solution.py:30
  56.6 2.2 %copy-start.2 = (f32[4,512,512]{2,1,0:T(8,128)S(1)}, f32[4,512,512]{2,1,0:T(8,128)}, u32[]{:S(2)}) copy-start(f32[4,512,512]{2,1,0:T(8,128)} %copy-done.1) | copy-start | bytes 12582916
  58.8 7.0 %copy-start.7 = (bf16[512,2048]{1,0:T(8,128)(2,1)S(1)}, bf16[512,2048]{1,0:T(8,128)(2,1)}, u32[]{:S(2)}) copy-start(bf16[512,2048]{1,0:T(8,128)(2,1)} %w_up_ref.3) | copy-start | bytes 6291460
  58.8 7.0 %copy-start.16 = (bf16[256,2048]{1,0:T(8,128)(2,1)S(1)}, bf16[256,2048]{1,0:T(8,128)(2,1)}, u32[]{:S(2)}) copy-start(bf16[256,2048]{1,0:T(8,128)(2,1)} %copy-done.15) | copy-start | bytes 3145732
  58.8 7.0 %copy-start.18 = (f32[256,512]{1,0:T(8,128)S(1)}, f32[256,512]{1,0:T(8,128)}, u32[]{:S(2)}) copy-start(f32[256,512]{1,0:T(8,128)} %copy-done.17) | copy-start | bytes 1572868
  61.9 13.8 %copy-start.8 = (f32[512,512]{1,0:T(8,128)}, f32[512,512]{1,0:T(8,128)S(1)}, u32[]{:S(2)}) copy-start(f32[512,512]{1,0:T(8,128)S(1)} %get-tuple-element.123.own_ref) | copy-start | bytes 3145732
  61.9 21.4 %collective-permute-start.46 = (bf16[512,512]{1,0:T(8,128)(2,1)}, bf16[512,512]{1,0:T(8,128)(2,1)}, u32[]{:S(2)}, u32[]{:S(2)}) collective-permute-start(bf16[512,512]{1,0:T(8,128)(2,1)} %get-tuple-element.125), channel_id=1, source_target_pairs={{0,1},{1,0},{2,3},{3,2},{4,5},{5,4},{6,7},{7,6},{8,9},{9,8},{10,11... | collective-permute-start | bytes 1572872 | tf_op jit(solution)/shard_map/ppermute | solution.py:30
  61.9 22.9 %collective-permute-start.47 = (bf16[512,512]{1,0:T(8,128)(2,1)}, bf16[512,512]{1,0:T(8,128)(2,1)}, u32[]{:S(2)}, u32[]{:S(2)}) collective-permute-start(bf16[512,512]{1,0:T(8,128)(2,1)} %get-tuple-element.126), channel_id=1, source_target_pairs={{0,2},{1,3},{2,0},{3,1},{4,6},{5,7},{6,4},{7,5},{8,10},{9,11},{10,... | collective-permute-start | bytes 1572872 | tf_op jit(solution)/shard_map/ppermute | solution.py:30
  61.9 26.7 %collective-permute-start.48 = (bf16[512,512]{1,0:T(8,128)(2,1)}, bf16[512,512]{1,0:T(8,128)(2,1)}, u32[]{:S(2)}, u32[]{:S(2)}) collective-permute-start(bf16[512,512]{1,0:T(8,128)(2,1)} %get-tuple-element.127), channel_id=1, source_target_pairs={{0,3},{1,2},{2,1},{3,0},{4,7},{5,6},{6,5},{7,4},{8,11},{9,10},{10,... | collective-permute-start | bytes 1572872 | tf_op jit(solution)/shard_map/ppermute | solution.py:30
  75.7 1.0 copy-start.4
  76.7 2.1 %collective-permute-start.45 = (f32[32,512]{1,0:T(8,128)S(1)}, f32[32,512]{1,0:T(8,128)S(1)}, u32[]{:S(2)}, u32[]{:S(2)}) collective-permute-start(f32[32,512]{1,0:T(8,128)S(1)} %dynamic-slice_bitcast_fusion), channel_id=1, source_target_pairs={{0,8},{1,9},{2,10},{3,11},{4,12},{5,13},{6,14},{7,15},{8,0},{9,1},... | collective-permute-start | bytes 196616 | tf_op jit(solution)/shard_map/ppermute | solution.py:30
  77.9 19.3 %copy-start.9 = (f32[512,512]{1,0:T(8,128)S(1)}, f32[512,512]{1,0:T(8,128)}, u32[]{:S(2)}) copy-start(f32[512,512]{1,0:T(8,128)} %copy-done.8) | copy-start | bytes 3145732
  77.9 1.6 %collective-permute-start.39 = (bf16[3,32,512]{2,1,0:T(8,128)(2,1)S(1)}, bf16[3,32,512]{2,1,0:T(8,128)(2,1)S(1)}, u32[]{:S(2)}, u32[]{:S(2)}) collective-permute-start(bf16[3,32,512]{2,1,0:T(8,128)(2,1)S(1)} %get-tuple-element.121), channel_id=1, source_target_pairs={{0,8},{8,16},{16,24},{24,32},{32,40},{40,48},{48,56},{56,64},{64,7... | collective-permute-start | bytes 294920 | tf_op jit(solution)/shard_map/ppermute | solution.py:58
  78.8 4.4 %collective-permute-start.40 = (bf16[3,32,512]{2,1,0:T(8,128)(2,1)S(1)}, bf16[3,32,512]{2,1,0:T(8,128)(2,1)S(1)}, u32[]{:S(2)}, u32[]{:S(2)}) collective-permute-start(bf16[3,32,512]{2,1,0:T(8,128)(2,1)S(1)} %get-tuple-element.122), channel_id=1, source_target_pairs={{8,0},{16,8},{24,16},{32,24},{40,32},{48,40},{56,48},{64,56},{72,6... | collective-permute-start | bytes 294920 | tf_op jit(solution)/shard_map/ppermute | solution.py:62
  88.7 6.0 %collective-permute-start.49 = (f32[32,512]{1,0:T(8,128)S(1)}, f32[32,512]{1,0:T(8,128)S(1)}, u32[]{:S(2)}, u32[]{:S(2)}) collective-permute-start(f32[32,512]{1,0:T(8,128)S(1)} %bitcast_add_fusion.half_ref), channel_id=1, source_target_pairs={{0,1},{1,0},{2,3},{3,2},{4,5},{5,4},{6,7},{7,6},{8,9},{9,8},{10,11... | collective-permute-start | bytes 196616 | tf_op jit(solution)/shard_map/ppermute | solution.py:30
  88.7 6.0 %collective-permute-start.50 = (f32[32,512]{1,0:T(8,128)S(1)}, f32[32,512]{1,0:T(8,128)S(1)}, u32[]{:S(2)}, u32[]{:S(2)}) collective-permute-start(f32[32,512]{1,0:T(8,128)S(1)} %bitcast_add_fusion.half_ref), channel_id=1, source_target_pairs={{0,2},{1,3},{2,0},{3,1},{4,6},{5,7},{6,4},{7,5},{8,10},{9,11},{10,... | collective-permute-start | bytes 196616 | tf_op jit(solution)/shard_map/ppermute | solution.py:30
  92.2 5.0 %collective-permute-start.51 = (f32[32,512]{1,0:T(8,128)S(1)}, f32[32,512]{1,0:T(8,128)S(1)}, u32[]{:S(2)}, u32[]{:S(2)}) collective-permute-start(f32[32,512]{1,0:T(8,128)S(1)} %bitcast_add_fusion.half_ref), channel_id=1, source_target_pairs={{0,3},{1,2},{2,1},{3,0},{4,7},{5,6},{6,5},{7,4},{8,11},{9,10},{10,... | collective-permute-start | bytes 196616 | tf_op jit(solution)/shard_map/ppermute | solution.py:30
  98.9 0.6 copy-start.13
  99.5 10.8 %collective-permute-start.52 = (bf16[192,512]{1,0:T(8,128)(2,1)S(1)}, bf16[192,512]{1,0:T(8,128)(2,1)S(1)}, u32[]{:S(2)}, u32[]{:S(2)}) collective-permute-start(bf16[192,512]{1,0:T(8,128)(2,1)S(1)} %get-tuple-element.134), channel_id=1, source_target_pairs={{0,128},{1,129},{2,130},{3,131},{4,132},{5,133},{6,134},{7,135},{8... | collective-permute-start | bytes 589832 | tf_op jit(solution)/shard_map/ppermute | solution.py:30
  99.5 12.4 %collective-permute-start.53 = (bf16[192,512]{1,0:T(8,128)(2,1)S(1)}, bf16[192,512]{1,0:T(8,128)(2,1)S(1)}, u32[]{:S(2)}, u32[]{:S(2)}) collective-permute-start(bf16[192,512]{1,0:T(8,128)(2,1)S(1)} %get-tuple-element.135), channel_id=1, source_target_pairs={{0,4},{1,5},{2,6},{3,7},{4,0},{5,1},{6,2},{7,3},{8,12},{9,13},{10,... | collective-permute-start | bytes 589832 | tf_op jit(solution)/shard_map/ppermute | solution.py:30
  105.9 7.4 %collective-permute-start.54 = (bf16[192,512]{1,0:T(8,128)(2,1)S(1)}, bf16[192,512]{1,0:T(8,128)(2,1)S(1)}, u32[]{:S(2)}, u32[]{:S(2)}) collective-permute-start(bf16[192,512]{1,0:T(8,128)(2,1)S(1)} %get-tuple-element.136), channel_id=1, source_target_pairs={{0,132},{1,133},{2,134},{3,135},{4,128},{5,129},{6,130},{7,131},{8... | collective-permute-start | bytes 589832 | tf_op jit(solution)/shard_map/ppermute | solution.py:30
  113.3 0.8 copy-start.14
  114.8 9.9 %collective-permute-start.55 = (f32[64,512]{1,0:T(8,128)S(1)}, f32[64,512]{1,0:T(8,128)S(1)}, u32[]{:S(2)}, u32[]{:S(2)}) collective-permute-start(f32[64,512]{1,0:T(8,128)S(1)} %get-tuple-element.139), channel_id=1, source_target_pairs={{0,16},{1,17},{2,18},{3,19},{4,20},{5,21},{6,22},{7,23},{8,24},{9,... | collective-permute-start | bytes 393224 | tf_op jit(solution)/shard_map/ppermute | solution.py:30
  114.9 11.7 %collective-permute-start.56 = (f32[64,512]{1,0:T(8,128)S(1)}, f32[64,512]{1,0:T(8,128)S(1)}, u32[]{:S(2)}, u32[]{:S(2)}) collective-permute-start(f32[64,512]{1,0:T(8,128)S(1)} %get-tuple-element.140), channel_id=1, source_target_pairs={{0,32},{1,33},{2,34},{3,35},{4,36},{5,37},{6,38},{7,39},{8,40},{9,... | collective-permute-start | bytes 393224 | tf_op jit(solution)/shard_map/ppermute | solution.py:30
  118.8 11.2 %collective-permute-start.57 = (f32[64,512]{1,0:T(8,128)S(1)}, f32[64,512]{1,0:T(8,128)S(1)}, u32[]{:S(2)}, u32[]{:S(2)}) collective-permute-start(f32[64,512]{1,0:T(8,128)S(1)} %get-tuple-element.141), channel_id=1, source_target_pairs={{0,48},{1,49},{2,50},{3,51},{4,52},{5,53},{6,54},{7,55},{8,56},{9,... | collective-permute-start | bytes 393224 | tf_op jit(solution)/shard_map/ppermute | solution.py:30
  118.9 15.9 %collective-permute-start.43 = (bf16[16,3,512]{2,1,0:T(4,128)(2,1)S(1)}, bf16[16,3,512]{2,1,0:T(4,128)(2,1)S(1)}, u32[]{:S(2)}, u32[]{:S(2)}) collective-permute-start(bf16[16,3,512]{2,1,0:T(4,128)(2,1)S(1)} %get-tuple-element.157), channel_id=1, source_target_pairs={{0,8},{8,16},{16,24},{24,32},{32,40},{40,48},{48,56},{56,64},{64,7... | collective-permute-start | bytes 147464 | tf_op jit(solution)/shard_map/ppermute | solution.py:58
  124.6 10.2 %collective-permute-start.44 = (bf16[16,3,512]{2,1,0:T(4,128)(2,1)S(1)}, bf16[16,3,512]{2,1,0:T(4,128)(2,1)S(1)}, u32[]{:S(2)}, u32[]{:S(2)}) collective-permute-start(bf16[16,3,512]{2,1,0:T(4,128)(2,1)S(1)} %get-tuple-element.158), channel_id=1, source_target_pairs={{8,0},{16,8},{24,16},{32,24},{40,32},{48,40},{56,48},{64,56},{72,6... | collective-permute-start | bytes 147464 | tf_op jit(solution)/shard_map/ppermute | solution.py:62
  124.7 21.2 %collective-permute-start.41 = (bf16[16,3,512]{2,1,0:T(4,128)(2,1)}, bf16[16,3,512]{2,1,0:T(4,128)(2,1)S(1)}, u32[]{:S(2)}, u32[]{:S(2)}) collective-permute-start(bf16[16,3,512]{2,1,0:T(4,128)(2,1)} %get-tuple-element.150), channel_id=1, source_target_pairs={{0,1},{1,2},{2,3},{3,4},{4,5},{5,6},{6,7},{8,9},{9,10},{10,11},{11... | collective-permute-start | bytes 147464 | tf_op jit(solution)/shard_map/ppermute | solution.py:447
  126.6 19.3 %collective-permute-start.42 = (bf16[16,3,512]{2,1,0:T(4,128)(2,1)}, bf16[16,3,512]{2,1,0:T(4,128)(2,1)S(1)}, u32[]{:S(2)}, u32[]{:S(2)}) collective-permute-start(bf16[16,3,512]{2,1,0:T(4,128)(2,1)} %get-tuple-element.152), channel_id=1, source_target_pairs={{1,0},{2,1},{3,2},{4,3},{5,4},{6,5},{7,6},{9,8},{10,9},{11,10},{12... | collective-permute-start | bytes 147464 | tf_op jit(solution)/shard_map/ppermute | solution.py:448
  130.6 7.5 %collective-permute-start.58 = (f32[48,512]{1,0:T(8,128)S(1)}, f32[48,512]{1,0:T(8,128)S(1)}, u32[]{:S(2)}, u32[]{:S(2)}) collective-permute-start(f32[48,512]{1,0:T(8,128)S(1)} %get-tuple-element.144), channel_id=1, source_target_pairs={{0,64},{1,65},{2,66},{3,67},{4,68},{5,69},{6,70},{7,71},{8,72},{9,... | collective-permute-start | bytes 294920 | tf_op jit(solution)/shard_map/ppermute | solution.py:30
  134.9 1.3 collective-permute-start.22
  138.1 7.8 %copy-start.19 = (f32[16,22,512]{2,1,0:T(8,128)S(1)}, f32[16,22,512]{2,1,0:T(8,128)}, u32[]{:S(2)}) copy-start(f32[16,22,512]{2,1,0:T(8,128)} %get-tuple-element.149) | copy-start | bytes 2162692
  138.1 7.8 %copy-start.21 = (bf16[16,16,512]{2,1,0:T(8,128)(2,1)S(1)}, bf16[16,16,512]{2,1,0:T(8,128)(2,1)}, u32[]{:S(2)}) copy-start(bf16[16,16,512]{2,1,0:T(8,128)(2,1)} %param.42) | copy-start | bytes 786436
  138.7 9.0 %collective-permute-start.59 = (f32[32,512]{1,0:T(8,128)S(1)}, f32[32,512]{1,0:T(8,128)S(1)}, u32[]{:S(2)}, u32[]{:S(2)}) collective-permute-start(f32[32,512]{1,0:T(8,128)S(1)} %get-tuple-element.147), channel_id=1, source_target_pairs={{0,8},{1,9},{2,10},{3,11},{4,12},{5,13},{6,14},{7,15},{8,0},{9,1},... | collective-permute-start | bytes 196616 | tf_op jit(solution)/shard_map/ppermute | solution.py:30
where the time goes:
time: 152 us; the launch traced here: 150 us
  starting transfers between devices  64.6 us (42%)
  Pallas kernels  28.1 us (18%)
  waiting for transfers between devices  23.2 us (15%)
  local copies, waits for them, and re-layouts  19.8 us (13%)
  other arithmetic  9.99 us (7%)
  matrix products  2.04 us (1%)
  between operations  1.69 us (1%)
    ppermute x16, starting transfers between devices, send(): return lax.ppermute(value, DEVICES, [(i, i ^ mask) for i in range(256)])  35.6 us
    ppermute x16, waiting for transfers between devices, send(): return lax.ppermute(value, DEVICES, [(i, i ^ mask) for i in range(256)])  17.9 us
    unnamed x46, local copies, waits for them, and re-layouts  12.3 us
    pallas_call x1, Pallas kernels, run_forward(): pl.pallas_call(forward_kernel, out_shape=[jax.ShapeDtypeStruct(s, d) for...  11.6 us
    pallas_call x1, Pallas kernels, run_backward(): pl.pallas_call(backward_kernel, out_shape=[jax.ShapeDtypeStruct((64, 512)...  9.93 us
    ppermute x3, starting transfers between devices, to_next(): return lax.ppermute(value, 'lon', [(i, (i + 1) % 32) for i in range(32)])  7.24 us
    ppermute x2, starting transfers between devices, extended_2(): lax.ppermute(tail, axis, [(i, (i + 1) % count) for i in range(ends)])  7.16 us
    pallas_call x5, Pallas kernels, local_call(): pl.pallas_call(kernel, out_shape=[jax.ShapeDtypeStruct(s, d) for s, d in...  6.59 us
  transfers between devices with their start and end apart: 30, of which 13 were waited for; matrix products, arithmetic and copies ran while one was open for 10% of the time, Pallas kernels for 7%

commit v1 on v0

--- a/solution.py
+++ b/solution.py
@@ -75,11 +75,19 @@
 
 
 def forward_kernel(
-    at_ref, ext_ref, kern_ref, gain_ref, w_up_ref, b_up_ref, d_out_ref, d_act_ref, order_ref,
-    mixed_ref, d_upper_ref, bias_ref, keep_ref, send_ref,
-    wide, shifted, normed, ordered, upper, active, tile,
+    at_ref, ext_ref, kern_ref, gain_ref, b_up_ref, d_out_ref, order_hbm, w_up_hbm, d_act_hbm,
+    mixed_hbm, d_upper_hbm, bias_ref, own_hbm, keep_hbm, send_hbm,
+    wide, shifted, normed, ordered, upper, active, tile, mixed_ref, order_ref, w_up_ref, d_act_ref,
+    d_upper_ref, own, keep, give, sems,
 ):
     core, x_at, y_at = at_ref[0], at_ref[1], at_ref[2]
+    loads = [
+        pltpu.make_async_copy(order_hbm, order_ref, sems.at[0]),
+        pltpu.make_async_copy(w_up_hbm, w_up_ref, sems.at[1]),
+        pltpu.make_async_copy(d_act_hbm, d_act_ref, sems.at[2]),
+    ]
+    for load in loads:
+        load.start()
     spread_rows(ext_ref, wide, shifted)
 
     def conv_step(step, carry):
@@ -106,6 +114,10 @@
         return carry
 
     lax.fori_loop(0, 8, norm_step, 0)
+    stores = [pltpu.make_async_copy(mixed_ref, mixed_hbm, sems.at[3])]
+    stores[0].start()
+    for load in loads:
+        load.wait()
     ordered[...] = jnp.dot(normed[...], order_ref[...], preferred_element_type=F32).astype(BF16)
 
     for t in range(4):
@@ -125,6 +137,9 @@
             return bias + jnp.sum(d_up.astype(F32), axis=0, keepdims=True)
 
         bias_ref[t : t + 1, :] = lax.fori_loop(0, 8, gelu_step, jnp.zeros((1, 512), F32))
+        if t == 3:
+            stores.append(pltpu.make_async_copy(d_upper_ref, d_upper_hbm, sems.at[4]))
+            stores[-1].start()
         tile[...] = lax.dot_general(
             active[...], d_out_ref[...], (((0,), (0,)), ((), ())), preferred_element_type=F32
         )
@@ -140,27 +155,55 @@
                     )
                     rows = pl.ds(pl.multiple_of(k_y * 64 + (t % 2) * 32, 32), 32)
                     if mine == 0:
-                        send_ref[k_x, rows, :] = piece.astype(BF16)
+                        give[k_x, rows, :] = piece.astype(BF16)
+                    elif k_x == 0:
+                        own[rows, :] = piece
                     else:
-                        keep_ref[k_x, rows, :] = piece
+                        keep[k_x - 1, rows, :] = piece.astype(BF16)
+
+    def store(at, source, target):
+        stores.append(pltpu.make_async_copy(source, target, sems.at[at]))
+        stores[-1].start()
+
+    first, second = slice(0, 256), slice(256, 512)
+    store(5, give.at[:, first], send_hbm.at[:, first])
+    store(6, keep.at[:, first], keep_hbm.at[:, first])
+    store(7, own.at[first], own_hbm.at[first])
+    for t in range(4):
+        lanes = slice(t * 512, t * 512 + 512)
         tile[...] = lax.dot_general(
             ordered[...], d_upper_ref[:, lanes], (((0,), (0,)), ((), ())),
             preferred_element_type=F32,
         )
         rows = slice(256 + t * 64, 320 + t * 64)
-        for k_x in range(4):
-            keep_ref[k_x, rows, :] = tile[k_x * 64 : k_x * 64 + 64, :]
-            send_ref[k_x, rows, :] = tile[256 + k_x * 64 : 320 + k_x * 64, :].astype(BF16)
+        own[rows, :] = tile[0:64, :]
+        for k in range(4):
+            give[k, rows, :] = tile[256 + k * 64 : 320 + k * 64, :].astype(BF16)
+            if k:
+                keep[k - 1, rows, :] = tile[k * 64 : k * 64 + 64, :].astype(BF16)
+    store(8, give.at[:, second], send_hbm.at[:, second])
+    store(9, keep.at[:, second], keep_hbm.at[:, second])
+    store(10, own.at[second], own_hbm.at[second])
+    for copy in stores:
+        copy.wait()
 
 
 def backward_kernel(
-    ext_ref, mixed_ref, d_upper_ref, w_up_ref, gain_ref, kern_ref, bias_ref,
-    small_ref, grad_ref, west_ref, east_ref, wide, shifted, d_normed, d_cells, moved,
+    ext_ref, mixed_ref, gain_ref, bias_ref, d_upper_hbm, w_up_hbm,
+    small_ref, d_cells, wide, shifted, d_normed, d_upper_ref, w_up_ref, sems,
 ):
+    loads = [
+        pltpu.make_async_copy(d_upper_hbm, d_upper_ref, sems.at[0]),
+        pltpu.make_async_copy(w_up_hbm, w_up_ref, sems.at[1]),
+    ]
+    for load in loads:
+        load.start()
+    spread_rows(ext_ref, wide, shifted)
+    for load in loads:
+        load.wait()
     d_normed[...] = lax.dot_general(
         d_upper_ref[...], w_up_ref[...], (((1,), (1,)), ((), ())), preferred_element_type=F32
     )
-    spread_rows(ext_ref, wide, shifted)
 
     def norm_step(step, gain_sum):
         rows = pl.ds(pl.multiple_of(step * 32, 32), 32)
@@ -180,10 +223,6 @@
     small_ref[49:50, :] = lax.fori_loop(0, 8, norm_step, jnp.zeros((1, 512), F32))
     small_ref[50:54, :] = bias_ref[0:4, :]
     small_ref[54:64, :] = jnp.zeros((10, 512), F32)
-    moved[...] = jnp.zeros_like(moved)
-    for b in range(7):
-        moved[b, :, b : b + 16, :] = d_cells[...]
-
     def tap_step(step, carry):
         lanes = pl.ds(pl.multiple_of(step * 128, 128), 128)
         d = [d_cells[x, :, lanes] for x in range(16)]
@@ -201,6 +240,12 @@
 
     lax.fori_loop(0, 4, tap_step, 0)
 
+
+def rim_kernel(d_cells, kern_ref, grad_ref, west_ref, east_ref, moved):
+    moved[...] = jnp.zeros_like(moved)
+    for b in range(7):
+        moved[b, :, b : b + 16, :] = d_cells[...]
+
     def rim_step(step, carry):
         lanes = pl.ds(pl.multiple_of(step * 128, 128), 128)
         for q in range(3):
@@ -222,123 +267,165 @@
     east_ref[...] = jnp.concatenate([grad_ref[19:22], filler], axis=1).astype(BF16)
 
 
-VMEM_BYTES = 30 * 1024 * 1024
+VMEM_BYTES = 56 * 1024 * 1024
+VMEM = pl.BlockSpec(memory_space=pltpu.VMEM)
+SMEM = pl.BlockSpec(memory_space=pltpu.SMEM)
+HBM = pl.BlockSpec(memory_space=pl.ANY)
+
+
+def local_call(kernel, name, shapes, in_specs, out_specs, scratch, operands, flops):
+    return pl.pallas_call(
+        kernel,
+        out_shape=[jax.ShapeDtypeStruct(s, d) for s, d in shapes],
+        in_specs=in_specs,
+        out_specs=out_specs,
+        scratch_shapes=[pltpu.VMEM(s, d) if d else pltpu.SemaphoreType.DMA(s) for s, d in scratch],
+        compiler_params=pltpu.CompilerParams(vmem_limit_bytes=VMEM_BYTES),
+        cost_estimate=pl.CostEstimate(flops=flops, bytes_accessed=2000000, transcendentals=0),
+        name=name,
+    )(*operands)
 
 
 def run_forward(at, ext, kern, gain, w_up, b_up, d_out, d_act, order):
-    shapes = [
-        ((256, 512), F32), ((256, 2048), BF16), ((8, 512), F32),
-        ((4, 512, 512), F32), ((4, 512, 512), BF16),
+    square, long = (256, 512), (256, 2048)
+    return local_call(
+        forward_kernel,
+        "forward",
+        [
+            (square, F32), (long, BF16), ((8, 512), F32),
+            ((512, 512), F32), ((3, 512, 512), BF16), ((4, 512, 512), BF16),
+        ],
+        [SMEM] + [VMEM] * 5 + [HBM] * 3,
+        [HBM, HBM, VMEM, HBM, HBM, HBM],
+        [
+            ((22, 32, 512), F32), ((7, 22, 16, 512), F32), (square, BF16), (square, BF16),
+            (square, F32), (square, BF16), ((512, 512), F32), (square, F32), ((512, 512), BF16),
+            ((512, 2048), BF16), (long, F32), (long, BF16),
+            ((512, 512), F32), ((3, 512, 512), BF16), ((4, 512, 512), BF16), ((11,), None),
+        ],
+        [at, ext, kern, gain, b_up, d_out, order, w_up, d_act],
+        14000000000,
+    )
+
+
+def run_backward(ext, mixed, d_upper, w_up, gain, bias):
+    return local_call(
+        backward_kernel,
+        "backward",
+        [((64, 512), F32), ((16, 16, 512), F32)],
+        [VMEM] * 4 + [HBM] * 2,
+        [VMEM] * 2,
+        [
+            ((22, 32, 512), F32), ((7, 22, 16, 512), F32), ((256, 512), F32),
+            ((256, 2048), BF16), ((512, 2048), BF16), ((2,), None),
+        ],
+        [ext, mixed, gain, bias, d_upper, w_up],
+        8000000000,
+    )
+
+
+def run_rims(d_cells, kern):
+    return local_call(
+        rim_kernel,
+        "rims",
+        [((22, 24, 512), F32), ((3, 32, 512), BF16), ((3, 32, 512), BF16)],
+        [VMEM] * 2,
+        [VMEM] * 3,
+        [((7, 16, 24, 512), F32)],
+        [d_cells, kern],
+        5000000000,
+    )
+
+
+def run_sum(kernel, shapes, operands, name, scalars=0, scratch=()):
+    return local_call(
+        kernel, name, shapes, [SMEM] * scalars + [VMEM] * (len(operands) - scalars),
+        [VMEM] * len(shapes), scratch, operands, 800000000,
+    )
+
+
+def first_sum_kernel(mine_ref, keep_ref, given_ref, own_ref, *give_refs):
+    own_ref[...] = mine_ref[...] + given_ref[0].astype(F32)
+    for k in range(3):
+        for part in range(2):
+            rows = slice(part * 256, part * 256 + 256)
+            total = keep_ref[k, rows, :].astype(F32) + given_ref[k + 1, rows, :].astype(F32)
+            give_refs[part * 3 + k][...] = total.astype(BF16)
+
+
+def two_terms(value):
+    high = value.astype(BF16)
+    return high, (value - high.astype(F32)).astype(BF16)
+
+
+def whole(first, rest, rows):
+    a, b, c = [ref[rows, :].astype(F32) for ref in rest]
+    return (first + a) + (b + c)
+
+
+def second_sum_kernel(own_ref, *refs):
+    down, up, halves, outs = refs[:3], refs[3:6], refs[6:10], refs[10:]
+    large_ref, terms_ref, over_y, over_x = outs[0], outs[1], outs[2:5], outs[5:8]
+    half = (halves[0][...] + halves[1][...]) + (halves[2][...] + halves[3][...])
+    high, low = two_terms(half)
+    terms_ref[...] = high.astype(F32) + low.astype(F32)
+    for k in range(4):
+        rows = slice(k * 64, k * 64 + 64)
+        total = whole(own_ref[rows, :], down, rows)
+        if k == 0:
+            large_ref[0:64, :] = total
+        else:
+            over_y[k - 1][0:64, :] = total.astype(BF16)
+            over_y[k - 1][64:96, :] = high
+            over_y[k - 1][96:128, :] = low
+        for t in range(4):
+            at = t * 64 + k * 16
+            total = whole(own_ref[256 + at : 272 + at, :], up, slice(at, at + 16))
+            if k == 0:
+                large_ref[64 + t * 16 : 80 + t * 16, :] = total
+            else:
+                over_x[k - 1][t * 16 : t * 16 + 16, :] = total.astype(BF16)
+
+
+def whole_terms(first, refs, at):
+    a, b, c = [
+        ref[at : at + 32, :].astype(F32) + ref[at + 32 : at + 64, :].astype(F32) for ref in refs
     ]
-    return pl.pallas_call(
-        forward_kernel,
-        out_shape=[jax.ShapeDtypeStruct(s, d) for s, d in shapes],
-        in_specs=[pl.BlockSpec(memory_space=pltpu.SMEM)]
-        + [pl.BlockSpec(memory_space=pltpu.VMEM)] * 8,
-        out_specs=[pl.BlockSpec(memory_space=pltpu.VMEM)] * 5,
-        scratch_shapes=[
-            pltpu.VMEM((22, 32, 512), F32), pltpu.VMEM((7, 22, 16, 512), F32),
-            pltpu.VMEM((256, 512), BF16), pltpu.VMEM((256, 512), BF16),
-            pltpu.VMEM((256, 512), F32), pltpu.VMEM((256, 512), BF16), pltpu.VMEM((512, 512), F32),
-        ],
-        compiler_params=pltpu.CompilerParams(vmem_limit_bytes=VMEM_BYTES),
-        cost_estimate=pl.CostEstimate(
-            flops=14000000000, bytes_accessed=16000000, transcendentals=600000
-        ),
-        name="forward",
-    )(at, ext, kern, gain, w_up, b_up, d_out, d_act, order)
-
-
-def run_backward(ext, mixed, d_upper, w_up, gain, kern, bias):
-    return pl.pallas_call(
-        backward_kernel,
-        out_shape=[
-            jax.ShapeDtypeStruct((64, 512), F32), jax.ShapeDtypeStruct((22, 24, 512), F32),
-            jax.ShapeDtypeStruct((3, 32, 512), BF16), jax.ShapeDtypeStruct((3, 32, 512), BF16),
-        ],
-        in_specs=[pl.BlockSpec(memory_space=pltpu.VMEM)] * 7,
-        out_specs=[pl.BlockSpec(memory_space=pltpu.VMEM)] * 4,
-        scratch_shapes=[
-            pltpu.VMEM((22, 32, 512), F32), pltpu.VMEM((7, 22, 16, 512), F32),
-            pltpu.VMEM((256, 512), F32), pltpu.VMEM((16, 16, 512), F32),
-            pltpu.VMEM((7, 16, 24, 512), F32),
-        ],
-        compiler_params=pltpu.CompilerParams(vmem_limit_bytes=VMEM_BYTES),
-        cost_estimate=pl.CostEstimate(flops=12000000000, bytes_accessed=8000000, transcendentals=300),
-        name="backward",
-    )(ext, mixed, d_upper, w_up, gain, kern, bias)
-
-
-def first_sum_kernel(keep_ref, given_ref, own_ref, *give_refs):
-    own_ref[...] = keep_ref[0] + given_ref[0].astype(F32)
-    for k in range(3):
-        give_refs[k][...] = (keep_ref[k + 1] + given_ref[k + 1].astype(F32)).astype(BF16)
-
-
-def second_sum_kernel(own_ref, a_ref, b_ref, c_ref, half_ref, half_a, half_b, half_c, *outs):
-    large_ref, terms_ref = outs[:2]
-    half = (half_ref[...] + half_a[...]) + (half_b[...] + half_c[...])
-    high = half.astype(BF16)
-    low = (half - high.astype(F32)).astype(BF16)
-    terms_ref[...] = high.astype(F32) + low.astype(F32)
-
-    def total(rows):
-        return (own_ref[rows, :] + a_ref[rows, :].astype(F32)) + (
-            b_ref[rows, :].astype(F32) + c_ref[rows, :].astype(F32)
-        )
-
-    for k in range(4):
-        pieces = [(slice(0, 64), slice(k * 64, k * 64 + 64))]
-        for t in range(4):
-            at = 256 + t * 64 + k * 16
-            pieces.append((slice(64 + t * 16, 80 + t * 16), slice(at, at + 16)))
-        for target, rows in pieces:
-            if k == 0:
-                large_ref[target, :] = total(rows)
-            else:
-                outs[1 + k][target, :] = total(rows).astype(BF16)
-        if k:
-            outs[1 + k][128:160, :] = high
-            outs[1 + k][160:192, :] = low
-
-
-def third_sum_kernel(at_ref, large_ref, terms_ref, a_ref, b_ref, c_ref, *outs):
-    own_ref, half_ref, blocks = outs[0], outs[1], outs[5]
-    low = at_ref[3] & 3
-
-    def total(rows):
-        return (large_ref[rows, :] + a_ref[rows, :].astype(F32)) + (
-            b_ref[rows, :].astype(F32) + c_ref[rows, :].astype(F32)
-        )
-
-    def term(ref):
-        return ref[128:160, :].astype(F32) + ref[160:192, :].astype(F32)
-
-    half = (terms_ref[...] + term(a_ref)) + (term(b_ref) + term(c_ref))
-    half_ref[...] = half
-    down = total(slice(0, 64))
-    up = total(slice(64, 128))
+    return (first + a) + (b + c)
+
+
+def third_sum_kernel(at_ref, large_ref, terms_ref, *refs):
+    over_y, over_x = refs[:3], refs[3:6]
+    own_ref, half_ref, outs, blocks = refs[6], refs[7], refs[8:11], refs[11]
+    low_bits = at_ref[3] & 3
+    high, low = two_terms(whole_terms(terms_ref[...], over_y, 64))
+    half_ref[...] = high.astype(F32) + low.astype(F32)
+    down = whole(large_ref[0:64, :], over_y, slice(0, 64))
+    up = whole(large_ref[64:128, :], over_x, slice(0, 64))
     for z in range(8):
         rows = [up[t * 16 + z * 2 : t * 16 + z * 2 + 2] for t in range(4)]
         blocks[z] = jnp.concatenate([down[z * 8 : z * 8 + 8]] + rows, axis=0)
     for k in range(4):
         for z_high in range(2):
-            block = blocks[z_high * 4 + (low ^ k)]
-            (own_ref if k == 0 else outs[1 + k])[z_high * 16 : z_high * 16 + 16, :] = block
+            block = blocks[z_high * 4 + (low_bits ^ k)]
+            rows = slice(z_high * 16, z_high * 16 + 16)
+            if k == 0:
+                own_ref[rows, :] = block
+            else:
+                outs[k - 1][rows, :] = block.astype(BF16)
         if k:
-            outs[1 + k][32:64, :] = half
+            outs[k - 1][32:64, :] = high
+            outs[k - 1][64:96, :] = low
 
 
 def fourth_sum_kernel(at_ref, own_ref, half_ref, a_ref, b_ref, c_ref, keep_ref, sum_ref, give_ref):
     high = at_ref[3] >> 2
-
-    def total(rows):
-        return (own_ref[rows, :] + a_ref[rows, :]) + (b_ref[rows, :] + c_ref[rows, :])
-
-    rest = slice(32, 64)
-    half = (half_ref[...] + a_ref[rest, :]) + (b_ref[rest, :] + c_ref[rest, :])
-    keep_ref[...] = total(pl.ds(pl.multiple_of(high * 16, 16), 16))
-    give_ref[0:16, :] = total(pl.ds(pl.multiple_of((1 - high) * 16, 16), 16))
+    refs = (a_ref, b_ref, c_ref)
+    half = whole_terms(half_ref[...], refs, 32)
+    first = whole(own_ref[0:16, :], refs, slice(0, 16))
+    second = whole(own_ref[16:32, :], refs, slice(16, 32))
+    keep_ref[...] = jnp.where(high == 0, first, second)
+    give_ref[0:16, :] = jnp.where(high == 0, second, first)
     give_ref[16:48, :] = half
     sum_ref[...] = half
 
@@ -349,20 +436,6 @@
     up = keep_ref[8:16, :] + got_ref[8:16, :]
     for t in range(4):
         up_ref[:, t * 512 : t * 512 + 512] = up[t * 2 : t * 2 + 2]
-
-
-def local_call(kernel, shapes, operands, name, scalars=0, scratch=()):
-    return pl.pallas_call(
-        kernel,
-        out_shape=[jax.ShapeDtypeStruct(s, d) for s, d in shapes],
-        in_specs=[pl.BlockSpec(memory_space=pltpu.SMEM)] * scalars
-        + [pl.BlockSpec(memory_space=pltpu.VMEM)] * (len(operands) - scalars),
-        out_specs=[pl.BlockSpec(memory_space=pltpu.VMEM)] * len(shapes),
-        scratch_shapes=list(scratch),
-        compiler_params=pltpu.CompilerParams(vmem_limit_bytes=VMEM_BYTES),
-        cost_estimate=pl.CostEstimate(flops=800000000, bytes_accessed=2000000, transcendentals=0),
-        name=name,
-    )(*operands)
 
 
 def per_device(
@@ -404,35 +477,35 @@
     y_of = (((block >> 2) & 1) << 1) + (block >> 7)
     goes_to = (
         (((block >> 3) & 1) ^ core) * 256
-        + ((block & 3) ^ x_at) * 64
-        + (y_of ^ y_at) * 16
+        + (y_of ^ y_at) * 64
+        + ((block & 3) ^ x_at) * 16
         + ((block >> 4) & 7) * 2
         + (row & 1)
     )
     order = (goes_to[:, None] == row[None, :]).astype(jnp.bfloat16)
     at = jnp.stack([core, x_at, y_at, z_at]).astype(jnp.int32)
     gain = norm_gain.reshape(1, channels)
-    mixed, d_upper, bias, keep, give = run_forward(
+    mixed, d_upper, bias, mine, keep, give = run_forward(
         at, extended, depth_kernel, gain, w_up, b_up.reshape(1, 2048), d_out, d_act, order
     )
 
     given = send(give, CORE_MASK)
-    own, *give = local_call(
-        first_sum_kernel, [((512, 512), F32)] + [((512, 512), BF16)] * 3, [keep, given], "first_sum"
+    piece = ((256, 512), BF16)
+    own, *give = run_sum(
+        first_sum_kernel, [((512, 512), F32)] + [piece] * 6, [mine, keep, given], "first_sum"
     )
     own, give, mixed = lax.optimization_barrier((own, give, mixed))
-    taken = [send(piece, mask) for piece, mask in zip(give, X_MASKS)]
-
-    small, grad_ext, west_rim, east_rim = run_backward(
-        extended, mixed, d_upper, w_up, gain, depth_kernel, bias
-    )
-
+    taken = [send(piece, mask) for piece, mask in zip(give, X_MASKS + Y_MASKS)]
+
+    small, d_cells = run_backward(extended, mixed, d_upper, w_up, gain, bias)
+
+    small, taken = lax.optimization_barrier((small, taken))
     small = small.reshape(2, 32, 512)
     half = lax.dynamic_index_in_dim(small, core, 0, False) + send(
         lax.dynamic_index_in_dim(small, 1 - core, 0, False), CORE_MASK
     )
-    half, taken = lax.optimization_barrier((half, taken))
     halves = [half] + [send(half, mask) for mask in X_MASKS]
+    grad_ext, west_rim, east_rim = run_rims(d_cells, depth_kernel)
 
     rim = jnp.bfloat16
     from_west = to_next(east_rim)[:, :22].astype(jnp.float32)
@@ -456,31 +529,31 @@
     mine = mine + to_previous(jnp.where(even, none, spread[16:]))
     from_fold = mirror_tiles(mine, turn >> 1)
 
-    large, terms, *give = local_call(
+    large, terms, *give = run_sum(
         second_sum_kernel,
-        [((128, 512), F32), ((32, 512), F32)] + [((192, 512), BF16)] * 3,
+        [((128, 512), F32), ((32, 512), F32)] + [((128, 512), BF16)] * 3 + [((64, 512), BF16)] * 3,
         [own, *taken, *halves],
         "second_sum",
     )
-    taken = [send(piece, mask) for piece, mask in zip(give, Y_MASKS)]
-
-    own, half, *give = local_call(
+    taken = [send(piece, mask) for piece, mask in zip(give, Y_MASKS + X_MASKS)]
+
+    own, half, *give = run_sum(
         third_sum_kernel,
-        [((32, 512), F32), ((32, 512), F32)] + [((64, 512), F32)] * 3,
+        [((32, 512), F32), ((32, 512), F32)] + [((96, 512), BF16)] * 3,
         [at, large, terms, *taken],
         "third_sum",
         scalars=1,
-        scratch=[pltpu.VMEM((8, 16, 512), F32)],
+        scratch=[((8, 16, 512), F32)],
     )
     taken = [send(piece, mask) for piece, mask in zip(give, Z_MASKS[:3])]
-    keep, half, give = local_call(
+    keep, half, give = run_sum(
         fourth_sum_kernel,
         [((16, 512), F32), ((32, 512), F32), ((48, 512), F32)],
         [at, own, half, *taken],
         "fourth_sum",
         scalars=1,
     )
-    grad_down, grad_up, half = local_call(
+    grad_down, grad_up, half = run_sum(
         last_sum_kernel,
         [((8, 512), F32), ((2, 2048), F32), ((32, 512), F32)],
         [keep, half, send(give, Z_MASKS[3])],

time: 152 us -> 158 us (1.039)
  the two profiles are of different devices: /device:TPU:7 before, /device:TPU:25 now
where the time goes in v1:
time: 158 us; the launch traced here: 157 us
  starting transfers between devices  76.1 us (48%)
  Pallas kernels  40.8 us (26%)
  waiting for transfers between devices  16.7 us (11%)
  other arithmetic  9.8 us (6%)
  local copies, waits for them, and re-layouts  9.12 us (6%)
  matrix products  2.09 us (1%)
  between operations  1.82 us (1%)
    ppermute x22, starting transfers between devices, send(): return lax.ppermute(value, DEVICES, [(i, i ^ mask) for i in range(256)])  41.1 us
    pallas_call x8, Pallas kernels, local_call(): pl.pallas_call(kernel, out_shape=[jax.ShapeDtypeStruct(s, d) for s, d in...  40.8 us
    ppermute x22, waiting for transfers between devices, send(): return lax.ppermute(value, DEVICES, [(i, i ^ mask) for i in range(256)])  16.4 us
    ppermute x2, starting transfers between devices, extended_2(): lax.ppermute(head, axis, [((i + 1) % count, i) for i in range(ends)])  9.31 us
    ppermute x3, starting transfers between devices, to_next(): return lax.ppermute(value, 'lon', [(i, (i + 1) % 32) for i in range(32)])  7.26 us
    ppermute x1, starting transfers between devices, per_device(): lax.ppermute(by_cols[:, 0:3].astype(rim), 'lat', [(i + 1, i) for i in ran...  6.98 us
    unnamed x52, local copies, waits for them, and re-layouts  4.85 us
    ppermute x2, starting transfers between devices, extended_2(): lax.ppermute(tail, axis, [(i, (i + 1) % count) for i in range(ends)])  4.25 us
  transfers between devices with their start and end apart: 36, of which 9 were waited for; matrix products, arithmetic and copies ran while one was open for 7% of the time, Pallas kernels for 12%

profile of v1, /device:TPU:25, one launch (start us, length us, event | category | flops | bytes accessed | tf_op | source)
XLA Modules:
  0.0 156.5 jit_solution(523731412516968664)
XLA Ops:
  0.6 1.3 slice.102
  2.7 1.0 fusion.17
  3.7 1.3 conditional.2
  3.7 1.3 collective-permute-start.7
  5.0 0.7 collective-permute-start.33
  5.7 1.5 collective-permute-start.34
  7.2 3.1 %collective-permute-start.32 = (bf16[16,3,512]{2,1,0:T(4,128)(2,1)S(1)}, bf16[16,3,512]{2,1,0:T(4,128)(2,1)S(1)}, u32[]{:S(2)}, u32[]{:S(2)}) collective-permute-start(bf16[16,3,512]{2,1,0:T(4,128)(2,1)S(1)} %get-tuple-element.184), channel_id=1, source_target_pairs={{0,1},{1,2},{2,3},{3,4},{4,5},{5,6},{6,7},{8,9},{9,10},{10,11},{11... | collective-permute-start | bytes 147464 | tf_op jit(solution)/shard_map/ppermute | solution.py:17
  10.4 5.8 %collective-permute-start.35 = (bf16[16,3,512]{2,1,0:T(4,128)(2,1)S(1)}, bf16[16,3,512]{2,1,0:T(4,128)(2,1)S(1)}, u32[]{:S(2)}, u32[]{:S(2)}) collective-permute-start(bf16[16,3,512]{2,1,0:T(4,128)(2,1)S(1)} %get-tuple-element.183), channel_id=1, source_target_pairs={{1,0},{2,1},{3,2},{4,3},{5,4},{6,5},{7,6},{9,8},{10,9},{11,10},{12... | collective-permute-start | bytes 147464 | tf_op jit(solution)/shard_map/ppermute | solution.py:19
  16.2 0.7 convert_element_type.45
  17.0 1.1 bitcast_multiply_fusion.d_out_ref
  18.0 2.1 %fusion.18.d_act_hbm = f32[256,2048]{1,0:T(8,128)} fusion(bf16[256,512]{1,0:T(8,128)(2,1)S(1)} %bitcast_multiply_fusion.d_out_ref, bf16[2048,512]{1,0:T(8,128)(2,1)S(1)} %copy-done), kind=kOutput, calls=%fused_computation.42 | convolution fusion | flops 536870912 | bytes 4456448 | tf_op jit(solution)/shard_map/dot_general | solution.py:472
  20.2 1.0 fusion.5.order_hbm
  21.1 0.9 broadcast_select_fusion.2
  22.6 1.1 collective-permute-start.36
  23.7 3.5 %collective-permute-start.37 = (bf16[3,22,512]{2,1,0:T(8,128)(2,1)S(1)}, bf16[3,22,512]{2,1,0:T(8,128)(2,1)S(1)}, u32[]{:S(2)}, u32[]{:S(2)}) collective-permute-start(bf16[3,22,512]{2,1,0:T(8,128)(2,1)S(1)} %get-tuple-element.182), channel_id=1, source_target_pairs={{8,0},{16,8},{24,16},{32,24},{40,32},{48,40},{56,48},{64,56},{72,6... | collective-permute-start | bytes 202760 | tf_op jit(solution)/shard_map/ppermute | solution.py:19
  27.2 0.6 pad_add_fusion.at_ref
  28.2 1.1 fusion.7.ext_ref
  29.3 13.2 %forward.1 = (f32[256,512]{1,0:T(8,128)}, bf16[256,2048]{1,0:T(8,128)(2,1)}, f32[8,512]{1,0:T(8,128)}, f32[512,512]{1,0:T(8,128)}, bf16[3,512,512]{2,1,0:T(8,128)(2,1)}, /*index=5*/bf16[4,512,512]{2,1,0:T(8,128)(2,1)}) custom-call(s32[4]{0:T(128)} %pad_add_fusion.at_ref, bf16[22,32,512]{2,1,0:T(8,128)(2,1)} %fusion.7.ext_ref, f32[49,512]{1,0:T(8,128)} %kern_ref.3, ...), custom_call_target="tpu_custom_call" | custom-call | flops 14000000000 | bytes 2000000 | tf_op jit(solution)/shard_map/forward/pallas_call | solution.py:277
  42.5 5.0 %collective-permute-start.38 = (bf16[4,512,512]{2,1,0:T(8,128)(2,1)}, bf16[4,512,512]{2,1,0:T(8,128)(2,1)}, u32[]{:S(2)}, u32[]{:S(2)}) collective-permute-start(bf16[4,512,512]{2,1,0:T(8,128)(2,1)} %get-tuple-element.126), channel_id=1, source_target_pairs={{0,8},{1,9},{2,10},{3,11},{4,12},{5,13},{6,14},{7,15},{8,0},{9,1},... | collective-permute-start | bytes 6291464 | tf_op jit(solution)/shard_map/ppermute | solution.py:30
  47.5 4.1 %collective-permute-done.38.given_ref = bf16[4,512,512]{2,1,0:T(8,128)(2,1)} collective-permute-done((bf16[4,512,512]{2,1,0:T(8,128)(2,1)}, bf16[4,512,512]{2,1,0:T(8,128)(2,1)}, u32[]{:S(2)}, u32[]{:S(2)}) %collective-permute-start.38) | collective-permute-done | bytes 2097184 | tf_op jit(solution)/shard_map/ppermute | solution.py:30
  51.6 3.9 %first_sum.1 = (f32[512,512]{1,0:T(8,128)}, bf16[256,512]{1,0:T(8,128)(2,1)}, bf16[256,512]{1,0:T(8,128)(2,1)}, bf16[256,512]{1,0:T(8,128)(2,1)}, bf16[256,512]{...) custom-call(f32[512,512]{1,0:T(8,128)} %get-tuple-element.124.mine_ref, ...), custom_call_target="tpu_custom_call" | custom-call | flops 800000000 | bytes 2000000 | tf_op jit(solution)/shard_map/first_sum/pallas_call | solution.py:277
  55.5 4.9 %collective-permute-start.46 = (bf16[256,512]{1,0:T(8,128)(2,1)}, bf16[256,512]{1,0:T(8,128)(2,1)S(1)}, u32[]{:S(2)}, u32[]{:S(2)}) collective-permute-start(bf16[256,512]{1,0:T(8,128)(2,1)} %get-tuple-element.145), channel_id=1, source_target_pairs={{0,2},{1,3},{2,0},{3,1},{4,6},{5,7},{6,4},{7,5},{8,10},{9,11},{10,... | collective-permute-start | bytes 786440 | tf_op jit(solution)/shard_map/ppermute | solution.py:30
  60.9 9.6 %backward.1 = (f32[64,512]{1,0:T(8,128)}, f32[16,16,512]{2,1,0:T(8,128)}) custom-call(bf16[22,32,512]{2,1,0:T(8,128)(2,1)} %fusion.7.ext_ref, f32[256,512]{1,0:T(8,128)} %get-tuple-element.135.mixed_ref, f32[1,512]{1,0:T(1,128)} %bitcast.26, f32[8,512]{1,0:T(8,128)} %get-tuple-element.136.bias_ref, bf16[256,2048]{1,0:T(8,128)(2,1)} %get-tuple-element.137.d_upper_hbm, ...), custom_call_target="tpu_custom_call" | custom-call | flops 8000000000 | bytes 2000000 | tf_op jit(solution)/shard_map/backward/pallas_call | solution.py:277
  70.6 3.5 %collective-permute-start.50 = (bf16[256,512]{1,0:T(8,128)(2,1)S(1)}, bf16[256,512]{1,0:T(8,128)(2,1)S(1)}, u32[]{:S(2)}, u32[]{:S(2)}) collective-permute-start(bf16[256,512]{1,0:T(8,128)(2,1)S(1)} %copy-done.12), channel_id=1, source_target_pairs={{0,132},{1,133},{2,134},{3,135},{4,128},{5,129},{6,130},{7,131},{8... | collective-permute-start | bytes 786440 | tf_op jit(solution)/shard_map/ppermute | solution.py:30
  74.1 5.9 %rims.1 = (f32[22,24,512]{2,1,0:T(8,128)}, bf16[3,32,512]{2,1,0:T(8,128)(2,1)}, bf16[3,32,512]{2,1,0:T(8,128)(2,1)}) custom-call(f32[16,16,512]{2,1,0:T(8,128)} %get-tuple-element.138.d_cells, f32[49,512]{1,0:T(8,128)} %kern_ref.3), custom_call_target="tpu_custom_call" | custom-call | flops 5000000000 | bytes 2000000 | tf_op jit(solution)/shard_map/rims/pallas_call | solution.py:277
  80.0 1.1 collective-permute-start.39
  81.1 0.7 copy-done.8
  81.8 0.8 collective-permute-start.40
  82.6 0.7 copy-done.9
  83.5 3.8 %collective-permute-start.51 = (f32[32,512]{1,0:T(8,128)S(1)}, f32[32,512]{1,0:T(8,128)S(1)}, u32[]{:S(2)}, u32[]{:S(2)}) collective-permute-start(f32[32,512]{1,0:T(8,128)S(1)} %dynamic-slice_bitcast_fusion), channel_id=1, source_target_pairs={{0,8},{1,9},{2,10},{3,11},{4,12},{5,13},{6,14},{7,15},{8,0},{9,1},... | collective-permute-start | bytes 196616 | tf_op jit(solution)/shard_map/ppermute | solution.py:30
  87.4 0.9 collective-permute-done.51
  88.4 4.1 %collective-permute-start.53 = (f32[32,512]{1,0:T(8,128)S(1)}, f32[32,512]{1,0:T(8,128)S(1)}, u32[]{:S(2)}, u32[]{:S(2)}) collective-permute-start(f32[32,512]{1,0:T(8,128)S(1)} %bitcast_add_fusion.refs_6_), channel_id=1, source_target_pairs={{0,2},{1,3},{2,0},{3,1},{4,6},{5,7},{6,4},{7,5},{8,10},{9,11},{10,... | collective-permute-start | bytes 196616 | tf_op jit(solution)/shard_map/ppermute | solution.py:30
  92.5 1.3 fusion.15
  93.8 1.2 collective-permute-done.53.refs_8_
  95.0 1.9 %collective-permute-done.54.refs_9_ = f32[32,512]{1,0:T(8,128)S(1)} collective-permute-done((f32[32,512]{1,0:T(8,128)S(1)}, f32[32,512]{1,0:T(8,128)S(1)}, u32[]{:S(2)}, u32[]{:S(2)}) %collective-permute-start.54) | collective-permute-done | bytes 65568 | tf_op jit(solution)/shard_map/ppermute | solution.py:30
  97.0 0.6 copy-done.24
  97.6 2.7 %second_sum.1 = (f32[128,512]{1,0:T(8,128)}, f32[32,512]{1,0:T(8,128)}, bf16[128,512]{1,0:T(8,128)(2,1)}, bf16[128,512]{1,0:T(8,128)(2,1)}, bf16[128,512]{1,0:T(...) custom-call(f32[512,512]{1,0:T(8,128)} %get-tuple-element.142.own_ref, ...), custom_call_target="tpu_custom_call" | custom-call | flops 800000000 | bytes 2000000 | tf_op jit(solution)/shard_map/second_sum/pallas_call | solution.py:277
  100.3 0.9 collective-permute-start.56
  101.2 2.9 %collective-permute-start.57 = (bf16[128,512]{1,0:T(8,128)(2,1)}, bf16[128,512]{1,0:T(8,128)(2,1)S(1)}, u32[]{:S(2)}, u32[]{:S(2)}) collective-permute-start(bf16[128,512]{1,0:T(8,128)(2,1)} %get-tuple-element.161), channel_id=1, source_target_pairs={{0,132},{1,133},{2,134},{3,135},{4,128},{5,129},{6,130},{7,131},{8... | collective-permute-start | bytes 393224 | tf_op jit(solution)/shard_map/ppermute | solution.py:30
  104.5 2.1 %collective-permute-start.59 = (bf16[64,512]{1,0:T(8,128)(2,1)}, bf16[64,512]{1,0:T(8,128)(2,1)S(1)}, u32[]{:S(2)}, u32[]{:S(2)}) collective-permute-start(bf16[64,512]{1,0:T(8,128)(2,1)} %get-tuple-element.163), channel_id=1, source_target_pairs={{0,2},{1,3},{2,0},{3,1},{4,6},{5,7},{6,4},{7,5},{8,10},{9,11},{10,... | collective-permute-start | bytes 196616 | tf_op jit(solution)/shard_map/ppermute | solution.py:30
  106.6 1.2 collective-permute-done.58.refs_3_
  107.8 0.9 collective-permute-start.60
  108.8 0.9 collective-permute-done.59.refs_4_
  109.6 2.7 %collective-permute-done.60.refs_5_ = bf16[64,512]{1,0:T(8,128)(2,1)S(1)} collective-permute-done((bf16[64,512]{1,0:T(8,128)(2,1)}, bf16[64,512]{1,0:T(8,128)(2,1)S(1)}, u32[]{:S(2)}, u32[]{:S(2)}) %collective-permute-start.60) | collective-permute-done | bytes 65568 | tf_op jit(solution)/shard_map/ppermute | solution.py:30
  113.1 2.0 %third_sum.1 = (f32[32,512]{1,0:T(8,128)}, f32[32,512]{1,0:T(8,128)}, bf16[96,512]{1,0:T(8,128)(2,1)}, bf16[96,512]{1,0:T(8,128)(2,1)}, bf16[96,512]{1,0:T(8,128)(2,1)}) custom-call(s32[4]{0:T(128)} %pad_add_fusion.at_ref, f32[128,512]{1,0:T(8,128)} %get-tuple-element.157.large_ref, f32[32,512]{1,0:T(8,128)} %get-tuple-element.158.terms_ref, ...), custom_call_target="tpu_custom_call" | custom-call | flops 800000000 | bytes 2000000 | tf_op jit(solution)/shard_map/third_sum/pallas_call | solution.py:277
  115.1 3.9 %collective-permute-start.62 = (bf16[96,512]{1,0:T(8,128)(2,1)}, bf16[96,512]{1,0:T(8,128)(2,1)S(1)}, u32[]{:S(2)}, u32[]{:S(2)}) collective-permute-start(bf16[96,512]{1,0:T(8,128)(2,1)} %get-tuple-element.168), channel_id=1, source_target_pairs={{0,32},{1,33},{2,34},{3,35},{4,36},{5,37},{6,38},{7,39},{8,40},{9,... | collective-permute-start | bytes 294920 | tf_op jit(solution)/shard_map/ppermute | solution.py:30
  119.1 4.6 %collective-permute-start.43 = (bf16[16,3,512]{2,1,0:T(4,128)(2,1)S(1)}, bf16[16,3,512]{2,1,0:T(4,128)(2,1)S(1)}, u32[]{:S(2)}, u32[]{:S(2)}) collective-permute-start(bf16[16,3,512]{2,1,0:T(4,128)(2,1)S(1)} %get-tuple-element.185), channel_id=1, source_target_pairs={{0,8},{8,16},{16,24},{24,32},{32,40},{40,48},{48,56},{56,64},{64,7... | collective-permute-start | bytes 147464 | tf_op jit(solution)/shard_map/ppermute | solution.py:58
  123.7 1.3 collective-permute-start.44
  125.0 1.9 %collective-permute-start.41 = (bf16[16,3,512]{2,1,0:T(4,128)(2,1)S(1)}, bf16[16,3,512]{2,1,0:T(4,128)(2,1)S(1)}, u32[]{:S(2)}, u32[]{:S(2)}) collective-permute-start(bf16[16,3,512]{2,1,0:T(4,128)(2,1)S(1)} %get-tuple-element.178), channel_id=1, source_target_pairs={{0,1},{1,2},{2,3},{3,4},{4,5},{5,6},{6,7},{8,9},{9,10},{10,11},{11... | collective-permute-start | bytes 147464 | tf_op jit(solution)/shard_map/ppermute | solution.py:520
  127.0 7.0 %collective-permute-start.42 = (bf16[16,3,512]{2,1,0:T(4,128)(2,1)S(1)}, bf16[16,3,512]{2,1,0:T(4,128)(2,1)S(1)}, u32[]{:S(2)}, u32[]{:S(2)}) collective-permute-start(bf16[16,3,512]{2,1,0:T(4,128)(2,1)S(1)} %get-tuple-element.180), channel_id=1, source_target_pairs={{1,0},{2,1},{3,2},{4,3},{5,4},{6,5},{7,6},{9,8},{10,9},{11,10},{12... | collective-permute-start | bytes 147464 | tf_op jit(solution)/shard_map/ppermute | solution.py:521
  134.0 0.6 copy-done.19
  134.6 1.8 %fourth_sum.1 = (f32[16,512]{1,0:T(8,128)}, f32[32,512]{1,0:T(8,128)}, f32[48,512]{1,0:T(8,128)}) custom-call(s32[4]{0:T(128)} %pad_add_fusion.at_ref, f32[32,512]{1,0:T(8,128)} %get-tuple-element.165.own_ref, f32[32,512]{1,0:T(8,128)} %get-tuple-element.166.half_ref, bf16[96,512]{1,0:T(8,128)(2,1)} %copy-done.17, bf16[96,512]{1,0:T(8,128)(2,1)} %copy-done.18, ...), custom_call_target="tpu_custom_call" | custom-call | flops 800000000 | bytes 2000000 | tf_op jit(solution)/shard_map/fourth_sum/pallas_call | solution.py:277
  136.4 2.9 %collective-permute-start.64 = (f32[48,512]{1,0:T(8,128)}, f32[48,512]{1,0:T(8,128)S(1)}, u32[]{:S(2)}, u32[]{:S(2)}) collective-permute-start(f32[48,512]{1,0:T(8,128)} %get-tuple-element.172), channel_id=1, source_target_pairs={{0,64},{1,65},{2,66},{3,67},{4,68},{5,69},{6,70},{7,71},{8,72},{9,... | collective-permute-start | bytes 294920 | tf_op jit(solution)/shard_map/ppermute | solution.py:30
  139.3 1.3 conditional.3
  139.3 1.3 collective-permute-start.23
  140.6 3.4 %collective-permute-done.64.got_ref = f32[48,512]{1,0:T(8,128)S(1)} collective-permute-done((f32[48,512]{1,0:T(8,128)}, f32[48,512]{1,0:T(8,128)S(1)}, u32[]{:S(2)}, u32[]{:S(2)}) %collective-permute-start.64) | collective-permute-done | bytes 98336 | tf_op jit(solution)/shard_map/ppermute | solution.py:30
  144.1 0.6 copy-done.16
  144.7 1.6 %last_sum.1 = (f32[8,512]{1,0:T(8,128)}, f32[2,2048]{1,0:T(2,128)}, f32[32,512]{1,0:T(8,128)}) custom-call(f32[16,512]{1,0:T(8,128)} %get-tuple-element.170.keep_ref, f32[32,512]{1,0:T(8,128)} %get-tuple-element.171.half_ref, f32[48,512]{1,0:T(8,128)} %copy-done.16), custom_call_target="tpu_custom_call" | custom-call | flops 800000000 | bytes 2000000 | tf_op jit(solution)/shard_map/last_sum/pallas_call | solution.py:277
  146.3 5.6 %collective-permute-start.65 = (f32[32,512]{1,0:T(8,128)}, f32[32,512]{1,0:T(8,128)S(1)}, u32[]{:S(2)}, u32[]{:S(2)}) collective-permute-start(f32[32,512]{1,0:T(8,128)} %get-tuple-element.175), channel_id=1, source_target_pairs={{0,8},{1,9},{2,10},{3,11},{4,12},{5,13},{6,14},{7,15},{8,0},{9,1},... | collective-permute-start | bytes 196616 | tf_op jit(solution)/shard_map/ppermute | solution.py:30
  152.0 1.8 %fusion.13 = bf16[16,16,512]{2,1,0:T(8,128)(2,1)} fusion(f32[16,22,512]{2,1,0:T(8,128)S(1)} %get-tuple-element.177, bf16[16,16,512]{2,1,0:T(8,128)(2,1)S(1)} %copy-done.2, bf16[16,3,512]{2,1,0:T(4,128)(2,1)} %get-tuple-element.190, bf16[16,3,512]{2,1,0:T(4,128)(2,1)S(1)} %collective-permute-done.42, bf16[16,3,512]{2,1,0:T(4,128)(2,1)S(1)} %collective-permute-done.41), kind=kLoop, calls=%fused_computation.17 | loop fusion | flops 1179648 | bytes 1196032 | tf_op jit(solution)/shard_map/convert_element_type | solution.py:577
  153.7 0.9 maximum_select_fusion
  154.7 0.7 slice.124
  155.3 0.6 slice.125
  155.9 0.6 copy.15
  (100 shorter events, 3.1 us)
Async XLA Ops:
  0.6 17.4 %copy-start = (bf16[2048,512]{1,0:T(8,128)(2,1)S(1)}, bf16[2048,512]{1,0:T(8,128)(2,1)}, u32[]{:S(2)}) copy-start(bf16[2048,512]{1,0:T(8,128)(2,1)} %param.49) | copy-start | bytes 6291460
  3.7 1.3 collective-permute-start.7
  5.0 16.1 %collective-permute-start.33 = (bf16[16,3,512]{2,1,0:T(4,128)(2,1)}, bf16[16,3,512]{2,1,0:T(4,128)(2,1)S(1)}, u32[]{:S(2)}, u32[]{:S(2)}) collective-permute-start(bf16[16,3,512]{2,1,0:T(4,128)(2,1)} %get-tuple-element.189), channel_id=1, source_target_pairs={{8,0},{16,8},{24,16},{32,24},{40,32},{48,40},{56,48},{64,56},{72,6... | collective-permute-start | bytes 147464 | tf_op jit(solution)/shard_map/ppermute | solution.py:62
  5.7 15.4 %collective-permute-start.34 = (bf16[16,3,512]{2,1,0:T(4,128)(2,1)}, bf16[16,3,512]{2,1,0:T(4,128)(2,1)S(1)}, u32[]{:S(2)}, u32[]{:S(2)}) collective-permute-start(bf16[16,3,512]{2,1,0:T(4,128)(2,1)} %get-tuple-element.189), channel_id=1, source_target_pairs={{0,8},{8,16},{16,24},{24,32},{32,40},{40,48},{48,56},{56,64},{64,7... | collective-permute-start | bytes 147464 | tf_op jit(solution)/shard_map/ppermute | solution.py:58
  7.2 15.2 %collective-permute-start.32 = (bf16[16,3,512]{2,1,0:T(4,128)(2,1)S(1)}, bf16[16,3,512]{2,1,0:T(4,128)(2,1)S(1)}, u32[]{:S(2)}, u32[]{:S(2)}) collective-permute-start(bf16[16,3,512]{2,1,0:T(4,128)(2,1)S(1)} %get-tuple-element.184), channel_id=1, source_target_pairs={{0,1},{1,2},{2,3},{3,4},{4,5},{5,6},{6,7},{8,9},{9,10},{10,11},{11... | collective-permute-start | bytes 147464 | tf_op jit(solution)/shard_map/ppermute | solution.py:17
  10.4 12.1 %collective-permute-start.35 = (bf16[16,3,512]{2,1,0:T(4,128)(2,1)S(1)}, bf16[16,3,512]{2,1,0:T(4,128)(2,1)S(1)}, u32[]{:S(2)}, u32[]{:S(2)}) collective-permute-start(bf16[16,3,512]{2,1,0:T(4,128)(2,1)S(1)} %get-tuple-element.183), channel_id=1, source_target_pairs={{1,0},{2,1},{3,2},{4,3},{5,4},{6,5},{7,6},{9,8},{10,9},{11,10},{12... | collective-permute-start | bytes 147464 | tf_op jit(solution)/shard_map/ppermute | solution.py:19
  18.0 2.1 %copy-start.3 = (bf16[256,512]{1,0:T(8,128)(2,1)}, bf16[256,512]{1,0:T(8,128)(2,1)S(1)}, u32[]{:S(2)}) copy-start(bf16[256,512]{1,0:T(8,128)(2,1)S(1)} %bitcast_multiply_fusion.d_out_ref) | copy-start | bytes 786436
  20.1 2.3 %copy-start.1 = (bf16[16,16,512]{2,1,0:T(8,128)(2,1)S(1)}, bf16[16,16,512]{2,1,0:T(8,128)(2,1)}, u32[]{:S(2)}) copy-start(bf16[16,16,512]{2,1,0:T(8,128)(2,1)} %param.41) | copy-start | bytes 786436
  22.6 5.4 %collective-permute-start.36 = (bf16[3,22,512]{2,1,0:T(8,128)(2,1)S(1)}, bf16[3,22,512]{2,1,0:T(8,128)(2,1)S(1)}, u32[]{:S(2)}, u32[]{:S(2)}) collective-permute-start(bf16[3,22,512]{2,1,0:T(8,128)(2,1)S(1)} %get-tuple-element.181), channel_id=1, source_target_pairs={{0,8},{8,16},{16,24},{24,32},{32,40},{40,48},{48,56},{56,64},{64,7... | collective-permute-start | bytes 202760 | tf_op jit(solution)/shard_map/ppermute | solution.py:17
  23.7 4.4 %collective-permute-start.37 = (bf16[3,22,512]{2,1,0:T(8,128)(2,1)S(1)}, bf16[3,22,512]{2,1,0:T(8,128)(2,1)S(1)}, u32[]{:S(2)}, u32[]{:S(2)}) collective-permute-start(bf16[3,22,512]{2,1,0:T(8,128)(2,1)S(1)} %get-tuple-element.182), channel_id=1, source_target_pairs={{8,0},{16,8},{24,16},{32,24},{40,32},{48,40},{56,48},{64,56},{72,6... | collective-permute-start | bytes 202760 | tf_op jit(solution)/shard_map/ppermute | solution.py:19
  42.5 9.1 %collective-permute-start.38 = (bf16[4,512,512]{2,1,0:T(8,128)(2,1)}, bf16[4,512,512]{2,1,0:T(8,128)(2,1)}, u32[]{:S(2)}, u32[]{:S(2)}) collective-permute-start(bf16[4,512,512]{2,1,0:T(8,128)(2,1)} %get-tuple-element.126), channel_id=1, source_target_pairs={{0,8},{1,9},{2,10},{3,11},{4,12},{5,13},{6,14},{7,15},{8,0},{9,1},... | collective-permute-start | bytes 6291464 | tf_op jit(solution)/shard_map/ppermute | solution.py:30
  55.5 15.0 %collective-permute-start.45 = (bf16[256,512]{1,0:T(8,128)(2,1)}, bf16[256,512]{1,0:T(8,128)(2,1)S(1)}, u32[]{:S(2)}, u32[]{:S(2)}) collective-permute-start(bf16[256,512]{1,0:T(8,128)(2,1)} %get-tuple-element.144), channel_id=1, source_target_pairs={{0,1},{1,0},{2,3},{3,2},{4,5},{5,4},{6,7},{7,6},{8,9},{9,8},{10,11... | collective-permute-start | bytes 786440 | tf_op jit(solution)/shard_map/ppermute | solution.py:30
  55.5 24.4 %collective-permute-start.46 = (bf16[256,512]{1,0:T(8,128)(2,1)}, bf16[256,512]{1,0:T(8,128)(2,1)S(1)}, u32[]{:S(2)}, u32[]{:S(2)}) collective-permute-start(bf16[256,512]{1,0:T(8,128)(2,1)} %get-tuple-element.145), channel_id=1, source_target_pairs={{0,2},{1,3},{2,0},{3,1},{4,6},{5,7},{6,4},{7,5},{8,10},{9,11},{10,... | collective-permute-start | bytes 786440 | tf_op jit(solution)/shard_map/ppermute | solution.py:30
  60.4 20.7 %collective-permute-start.47 = (bf16[256,512]{1,0:T(8,128)(2,1)}, bf16[256,512]{1,0:T(8,128)(2,1)S(1)}, u32[]{:S(2)}, u32[]{:S(2)}) collective-permute-start(bf16[256,512]{1,0:T(8,128)(2,1)} %get-tuple-element.146), channel_id=1, source_target_pairs={{0,3},{1,2},{2,1},{3,0},{4,7},{5,6},{6,5},{7,4},{8,11},{9,10},{10,... | collective-permute-start | bytes 786440 | tf_op jit(solution)/shard_map/ppermute | solution.py:30
  60.4 22.2 %collective-permute-start.48 = (bf16[256,512]{1,0:T(8,128)(2,1)}, bf16[256,512]{1,0:T(8,128)(2,1)S(1)}, u32[]{:S(2)}, u32[]{:S(2)}) collective-permute-start(bf16[256,512]{1,0:T(8,128)(2,1)} %get-tuple-element.147), channel_id=1, source_target_pairs={{0,128},{1,129},{2,130},{3,131},{4,132},{5,133},{6,134},{7,135},{8... | collective-permute-start | bytes 786440 | tf_op jit(solution)/shard_map/ppermute | solution.py:30
  60.9 21.7 %collective-permute-start.49 = (bf16[256,512]{1,0:T(8,128)(2,1)}, bf16[256,512]{1,0:T(8,128)(2,1)S(1)}, u32[]{:S(2)}, u32[]{:S(2)}) collective-permute-start(bf16[256,512]{1,0:T(8,128)(2,1)} %get-tuple-element.148), channel_id=1, source_target_pairs={{0,4},{1,5},{2,6},{3,7},{4,0},{5,1},{6,2},{7,3},{8,12},{9,13},{10,... | collective-permute-start | bytes 786440 | tf_op jit(solution)/shard_map/ppermute | solution.py:30
  60.9 9.7 %copy-start.12 = (bf16[256,512]{1,0:T(8,128)(2,1)S(1)}, bf16[256,512]{1,0:T(8,128)(2,1)}, u32[]{:S(2)}) copy-start(bf16[256,512]{1,0:T(8,128)(2,1)} %get-tuple-element.149) | copy-start | bytes 786436
  70.6 9.4 %copy-start.6 = (bf16[256,512]{1,0:T(8,128)(2,1)}, bf16[256,512]{1,0:T(8,128)(2,1)S(1)}, u32[]{:S(2)}) copy-start(bf16[256,512]{1,0:T(8,128)(2,1)S(1)} %collective-permute-done.45.refs_0_) | copy-start | bytes 786436
  70.6 12.0 %collective-permute-start.50 = (bf16[256,512]{1,0:T(8,128)(2,1)S(1)}, bf16[256,512]{1,0:T(8,128)(2,1)S(1)}, u32[]{:S(2)}, u32[]{:S(2)}) collective-permute-start(bf16[256,512]{1,0:T(8,128)(2,1)S(1)} %copy-done.12), channel_id=1, source_target_pairs={{0,132},{1,133},{2,134},{3,135},{4,128},{5,129},{6,130},{7,131},{8... | collective-permute-start | bytes 786440 | tf_op jit(solution)/shard_map/ppermute | solution.py:30
  74.0 9.3 %copy-start.4 = (f32[64,512]{1,0:T(8,128)S(1)}, f32[64,512]{1,0:T(8,128)}, u32[]{:S(2)}) copy-start(f32[64,512]{1,0:T(8,128)} %get-tuple-element.156) | copy-start | bytes 393220
  80.0 17.0 %copy-start.7 = (bf16[256,512]{1,0:T(8,128)(2,1)}, bf16[256,512]{1,0:T(8,128)(2,1)S(1)}, u32[]{:S(2)}) copy-start(bf16[256,512]{1,0:T(8,128)(2,1)S(1)} %collective-permute-done.46.refs_1_) | copy-start | bytes 786436
  80.0 7.4 %collective-permute-start.39 = (bf16[3,32,512]{2,1,0:T(8,128)(2,1)}, bf16[3,32,512]{2,1,0:T(8,128)(2,1)S(1)}, u32[]{:S(2)}, u32[]{:S(2)}) collective-permute-start(bf16[3,32,512]{2,1,0:T(8,128)(2,1)} %get-tuple-element.140), channel_id=1, source_target_pairs={{0,8},{8,16},{16,24},{24,32},{32,40},{40,48},{48,56},{56,64},{64,7... | collective-permute-start | bytes 294920 | tf_op jit(solution)/shard_map/ppermute | solution.py:58
  81.1 0.7 copy-start.8
  81.8 5.5 %collective-permute-start.40 = (bf16[3,32,512]{2,1,0:T(8,128)(2,1)}, bf16[3,32,512]{2,1,0:T(8,128)(2,1)S(1)}, u32[]{:S(2)}, u32[]{:S(2)}) collective-permute-start(bf16[3,32,512]{2,1,0:T(8,128)(2,1)} %get-tuple-element.141), channel_id=1, source_target_pairs={{8,0},{16,8},{24,16},{32,24},{40,32},{48,40},{56,48},{64,56},{72,6... | collective-permute-start | bytes 294920 | tf_op jit(solution)/shard_map/ppermute | solution.py:62
  82.6 0.7 copy-start.9
  82.6 0.8 copy-start.10
  82.6 0.9 copy-start.11
  83.5 4.7 %collective-permute-start.51 = (f32[32,512]{1,0:T(8,128)S(1)}, f32[32,512]{1,0:T(8,128)S(1)}, u32[]{:S(2)}, u32[]{:S(2)}) collective-permute-start(f32[32,512]{1,0:T(8,128)S(1)} %dynamic-slice_bitcast_fusion), channel_id=1, source_target_pairs={{0,8},{1,9},{2,10},{3,11},{4,12},{5,13},{6,14},{7,15},{8,0},{9,1},... | collective-permute-start | bytes 196616 | tf_op jit(solution)/shard_map/ppermute | solution.py:30
  88.2 8.7 %copy-start.5 = (f32[32,512]{1,0:T(8,128)}, f32[32,512]{1,0:T(8,128)S(1)}, u32[]{:S(2)}) copy-start(f32[32,512]{1,0:T(8,128)S(1)} %bitcast_add_fusion.refs_6_) | copy-start | bytes 196612
  88.3 5.5 %collective-permute-start.52 = (f32[32,512]{1,0:T(8,128)S(1)}, f32[32,512]{1,0:T(8,128)S(1)}, u32[]{:S(2)}, u32[]{:S(2)}) collective-permute-start(f32[32,512]{1,0:T(8,128)S(1)} %bitcast_add_fusion.refs_6_), channel_id=1, source_target_pairs={{0,1},{1,0},{2,3},{3,2},{4,5},{5,4},{6,7},{7,6},{8,9},{9,8},{10,11... | collective-permute-start | bytes 196616 | tf_op jit(solution)/shard_map/ppermute | solution.py:30
  88.4 6.6 %collective-permute-start.53 = (f32[32,512]{1,0:T(8,128)S(1)}, f32[32,512]{1,0:T(8,128)S(1)}, u32[]{:S(2)}, u32[]{:S(2)}) collective-permute-start(f32[32,512]{1,0:T(8,128)S(1)} %bitcast_add_fusion.refs_6_), channel_id=1, source_target_pairs={{0,2},{1,3},{2,0},{3,1},{4,6},{5,7},{6,4},{7,5},{8,10},{9,11},{10,... | collective-permute-start | bytes 196616 | tf_op jit(solution)/shard_map/ppermute | solution.py:30
  92.5 4.5 %collective-permute-start.54 = (f32[32,512]{1,0:T(8,128)S(1)}, f32[32,512]{1,0:T(8,128)S(1)}, u32[]{:S(2)}, u32[]{:S(2)}) collective-permute-start(f32[32,512]{1,0:T(8,128)S(1)} %bitcast_add_fusion.refs_6_), channel_id=1, source_target_pairs={{0,3},{1,2},{2,1},{3,0},{4,7},{5,6},{6,5},{7,4},{8,11},{9,10},{10,... | collective-permute-start | bytes 196616 | tf_op jit(solution)/shard_map/ppermute | solution.py:30
  93.8 3.2 %copy-start.21 = (f32[32,512]{1,0:T(8,128)}, f32[32,512]{1,0:T(8,128)S(1)}, u32[]{:S(2)}) copy-start(f32[32,512]{1,0:T(8,128)S(1)} %collective-permute-done.52.refs_7_) | copy-start | bytes 196612
  95.0 1.9 %copy-start.23 = (f32[32,512]{1,0:T(8,128)}, f32[32,512]{1,0:T(8,128)S(1)}, u32[]{:S(2)}) copy-start(f32[32,512]{1,0:T(8,128)S(1)} %collective-permute-done.53.refs_8_) | copy-start | bytes 196612
  97.0 0.6 copy-start.24
  100.3 12.1 %collective-permute-start.55 = (bf16[128,512]{1,0:T(8,128)(2,1)}, bf16[128,512]{1,0:T(8,128)(2,1)S(1)}, u32[]{:S(2)}, u32[]{:S(2)}) collective-permute-start(bf16[128,512]{1,0:T(8,128)(2,1)} %get-tuple-element.159), channel_id=1, source_target_pairs={{0,128},{1,129},{2,130},{3,131},{4,132},{5,133},{6,134},{7,135},{8... | collective-permute-start | bytes 393224 | tf_op jit(solution)/shard_map/ppermute | solution.py:30
  100.3 12.0 %collective-permute-start.56 = (bf16[128,512]{1,0:T(8,128)(2,1)}, bf16[128,512]{1,0:T(8,128)(2,1)S(1)}, u32[]{:S(2)}, u32[]{:S(2)}) collective-permute-start(bf16[128,512]{1,0:T(8,128)(2,1)} %get-tuple-element.160), channel_id=1, source_target_pairs={{0,4},{1,5},{2,6},{3,7},{4,0},{5,1},{6,2},{7,3},{8,12},{9,13},{10,... | collective-permute-start | bytes 393224 | tf_op jit(solution)/shard_map/ppermute | solution.py:30
  101.2 11.1 %collective-permute-start.57 = (bf16[128,512]{1,0:T(8,128)(2,1)}, bf16[128,512]{1,0:T(8,128)(2,1)S(1)}, u32[]{:S(2)}, u32[]{:S(2)}) collective-permute-start(bf16[128,512]{1,0:T(8,128)(2,1)} %get-tuple-element.161), channel_id=1, source_target_pairs={{0,132},{1,133},{2,134},{3,135},{4,128},{5,129},{6,130},{7,131},{8... | collective-permute-start | bytes 393224 | tf_op jit(solution)/shard_map/ppermute | solution.py:30
  104.2 3.6 %collective-permute-start.58 = (bf16[64,512]{1,0:T(8,128)(2,1)}, bf16[64,512]{1,0:T(8,128)(2,1)}, u32[]{:S(2)}, u32[]{:S(2)}) collective-permute-start(bf16[64,512]{1,0:T(8,128)(2,1)} %get-tuple-element.162), channel_id=1, source_target_pairs={{0,1},{1,0},{2,3},{3,2},{4,5},{5,4},{6,7},{7,6},{8,9},{9,8},{10,11... | collective-permute-start | bytes 196616 | tf_op jit(solution)/shard_map/ppermute | solution.py:30
  104.5 5.1 %collective-permute-start.59 = (bf16[64,512]{1,0:T(8,128)(2,1)}, bf16[64,512]{1,0:T(8,128)(2,1)S(1)}, u32[]{:S(2)}, u32[]{:S(2)}) collective-permute-start(bf16[64,512]{1,0:T(8,128)(2,1)} %get-tuple-element.163), channel_id=1, source_target_pairs={{0,2},{1,3},{2,0},{3,1},{4,6},{5,7},{6,4},{7,5},{8,10},{9,11},{10,... | collective-permute-start | bytes 196616 | tf_op jit(solution)/shard_map/ppermute | solution.py:30
  107.8 4.5 %collective-permute-start.60 = (bf16[64,512]{1,0:T(8,128)(2,1)}, bf16[64,512]{1,0:T(8,128)(2,1)S(1)}, u32[]{:S(2)}, u32[]{:S(2)}) collective-permute-start(bf16[64,512]{1,0:T(8,128)(2,1)} %get-tuple-element.164), channel_id=1, source_target_pairs={{0,3},{1,2},{2,1},{3,0},{4,7},{5,6},{6,5},{7,4},{8,11},{9,10},{10,... | collective-permute-start | bytes 196616 | tf_op jit(solution)/shard_map/ppermute | solution.py:30
  109.6 2.7 %copy-start.20 = (bf16[64,512]{1,0:T(8,128)(2,1)}, bf16[64,512]{1,0:T(8,128)(2,1)S(1)}, u32[]{:S(2)}) copy-start(bf16[64,512]{1,0:T(8,128)(2,1)S(1)} %collective-permute-done.59.refs_4_) | copy-start | bytes 196612
  112.3 0.6 copy-start.22
  112.3 0.7 copy-start.13
  112.3 0.7 copy-start.14
  112.4 0.7 copy-start.15
  115.1 9.9 %collective-permute-start.61 = (bf16[96,512]{1,0:T(8,128)(2,1)}, bf16[96,512]{1,0:T(8,128)(2,1)S(1)}, u32[]{:S(2)}, u32[]{:S(2)}) collective-permute-start(bf16[96,512]{1,0:T(8,128)(2,1)} %get-tuple-element.167), channel_id=1, source_target_pairs={{0,16},{1,17},{2,18},{3,19},{4,20},{5,21},{6,22},{7,23},{8,24},{9,... | collective-permute-start | bytes 294920 | tf_op jit(solution)/shard_map/ppermute | solution.py:30
  115.1 11.8 %collective-permute-start.62 = (bf16[96,512]{1,0:T(8,128)(2,1)}, bf16[96,512]{1,0:T(8,128)(2,1)S(1)}, u32[]{:S(2)}, u32[]{:S(2)}) collective-permute-start(bf16[96,512]{1,0:T(8,128)(2,1)} %get-tuple-element.168), channel_id=1, source_target_pairs={{0,32},{1,33},{2,34},{3,35},{4,36},{5,37},{6,38},{7,39},{8,40},{9,... | collective-permute-start | bytes 294920 | tf_op jit(solution)/shard_map/ppermute | solution.py:30
  119.0 14.9 %collective-permute-start.63 = (bf16[96,512]{1,0:T(8,128)(2,1)}, bf16[96,512]{1,0:T(8,128)(2,1)S(1)}, u32[]{:S(2)}, u32[]{:S(2)}) collective-permute-start(bf16[96,512]{1,0:T(8,128)(2,1)} %get-tuple-element.169), channel_id=1, source_target_pairs={{0,48},{1,49},{2,50},{3,51},{4,52},{5,53},{6,54},{7,55},{8,56},{9,... | collective-permute-start | bytes 294920 | tf_op jit(solution)/shard_map/ppermute | solution.py:30
  119.1 20.1 %collective-permute-start.43 = (bf16[16,3,512]{2,1,0:T(4,128)(2,1)S(1)}, bf16[16,3,512]{2,1,0:T(4,128)(2,1)S(1)}, u32[]{:S(2)}, u32[]{:S(2)}) collective-permute-start(bf16[16,3,512]{2,1,0:T(4,128)(2,1)S(1)} %get-tuple-element.185), channel_id=1, source_target_pairs={{0,8},{8,16},{16,24},{24,32},{32,40},{40,48},{48,56},{56,64},{64,7... | collective-permute-start | bytes 147464 | tf_op jit(solution)/shard_map/ppermute | solution.py:58
  123.7 15.5 %collective-permute-start.44 = (bf16[16,3,512]{2,1,0:T(4,128)(2,1)S(1)}, bf16[16,3,512]{2,1,0:T(4,128)(2,1)S(1)}, u32[]{:S(2)}, u32[]{:S(2)}) collective-permute-start(bf16[16,3,512]{2,1,0:T(4,128)(2,1)S(1)} %get-tuple-element.186), channel_id=1, source_target_pairs={{8,0},{16,8},{24,16},{32,24},{40,32},{48,40},{56,48},{64,56},{72,6... | collective-permute-start | bytes 147464 | tf_op jit(solution)/shard_map/ppermute | solution.py:62
  125.0 8.9 %copy-start.17 = (bf16[96,512]{1,0:T(8,128)(2,1)}, bf16[96,512]{1,0:T(8,128)(2,1)S(1)}, u32[]{:S(2)}) copy-start(bf16[96,512]{1,0:T(8,128)(2,1)S(1)} %collective-permute-done.61.a_ref) | copy-start | bytes 294916
  125.0 27.0 %collective-permute-start.41 = (bf16[16,3,512]{2,1,0:T(4,128)(2,1)S(1)}, bf16[16,3,512]{2,1,0:T(4,128)(2,1)S(1)}, u32[]{:S(2)}, u32[]{:S(2)}) collective-permute-start(bf16[16,3,512]{2,1,0:T(4,128)(2,1)S(1)} %get-tuple-element.178), channel_id=1, source_target_pairs={{0,1},{1,2},{2,3},{3,4},{4,5},{5,6},{6,7},{8,9},{9,10},{10,11},{11... | collective-permute-start | bytes 147464 | tf_op jit(solution)/shard_map/ppermute | solution.py:520
  127.0 7.0 %copy-start.18 = (bf16[96,512]{1,0:T(8,128)(2,1)}, bf16[96,512]{1,0:T(8,128)(2,1)S(1)}, u32[]{:S(2)}) copy-start(bf16[96,512]{1,0:T(8,128)(2,1)S(1)} %collective-permute-done.62.b_ref) | copy-start | bytes 294916
  127.0 25.0 %collective-permute-start.42 = (bf16[16,3,512]{2,1,0:T(4,128)(2,1)S(1)}, bf16[16,3,512]{2,1,0:T(4,128)(2,1)S(1)}, u32[]{:S(2)}, u32[]{:S(2)}) collective-permute-start(bf16[16,3,512]{2,1,0:T(4,128)(2,1)S(1)} %get-tuple-element.180), channel_id=1, source_target_pairs={{1,0},{2,1},{3,2},{4,3},{5,4},{6,5},{7,6},{9,8},{10,9},{11,10},{12... | collective-permute-start | bytes 147464 | tf_op jit(solution)/shard_map/ppermute | solution.py:521
  134.0 0.6 copy-start.19
  136.4 7.7 %collective-permute-start.64 = (f32[48,512]{1,0:T(8,128)}, f32[48,512]{1,0:T(8,128)S(1)}, u32[]{:S(2)}, u32[]{:S(2)}) collective-permute-start(f32[48,512]{1,0:T(8,128)} %get-tuple-element.172), channel_id=1, source_target_pairs={{0,64},{1,65},{2,66},{3,67},{4,68},{5,69},{6,70},{7,71},{8,72},{9,... | collective-permute-start | bytes 294920 | tf_op jit(solution)/shard_map/ppermute | solution.py:30
  139.3 1.3 collective-permute-start.23
  144.1 0.6 copy-start.16
  144.7 7.3 %copy-start.2 = (bf16[16,16,512]{2,1,0:T(8,128)(2,1)S(1)}, bf16[16,16,512]{2,1,0:T(8,128)(2,1)}, u32[]{:S(2)}) copy-start(bf16[16,16,512]{2,1,0:T(8,128)(2,1)} %param.42) | copy-start | bytes 786436
  146.3 7.4 %collective-permute-start.65 = (f32[32,512]{1,0:T(8,128)}, f32[32,512]{1,0:T(8,128)S(1)}, u32[]{:S(2)}, u32[]{:S(2)}) collective-permute-start(f32[32,512]{1,0:T(8,128)} %get-tuple-element.175), channel_id=1, source_target_pairs={{0,8},{1,9},{2,10},{3,11},{4,12},{5,13},{6,14},{7,15},{8,0},{9,1},... | collective-permute-start | bytes 196616 | tf_op jit(solution)/shard_map/ppermute | solution.py:30

commit v2 on v1

v2 whole, which is shorter than its diff:
```python
import jax
import jax.numpy as jnp
from jax import lax
from jax.experimental import pallas as pl
from jax.experimental.pallas import tpu as pltpu
from jax.sharding import PartitionSpec as P

DEVICES = ("lon", "lat")
X_MASKS = (1, 2, 3)
Y_MASKS = (128, 4, 132)
Z_MASKS = (16, 32, 48, 64)
CORE_MASK = 8


def send(value, mask):
    return lax.ppermute(value, DEVICES, [(i, i ^ mask) for i in range(256)])


def to_next(value):
    return lax.ppermute(value, "lon", [(i, (i + 1) % 32) for i in range(32)])


def to_previous(value):
    return lax.ppermute(value, "lon", [((i + 1) % 32, i) for i in range(32)])


def to_north(value):
    return lax.ppermute(value, "lat", [(i, i + 1) for i in range(7)])


def to_south(value):
    return lax.ppermute(value, "lat", [(i + 1, i) for i in range(7)])


def mirror_tiles(near, far, half_turn):
    def swap(value, k):
        pairs = [(e * 8 + 7, ((2 * k - e) % 32) * 8 + 7) for e in range(32)]
        return lax.ppermute(value, DEVICES, pairs)

    def branch(k):
        return lambda a, b: (swap(a, k), swap(b, (k - 1) % 16))

    return lax.switch(half_turn, [branch(k) for k in range(16)], near, far)


ROOT_2_PI = 0.7978845608028654
CUBIC = 0.044715
F32 = jnp.float32
BF16 = jnp.bfloat16


def spread_rows(ext_ref, wide, shifted):
    wide[...] = ext_ref[...].astype(F32)
    for b in range(7):
        shifted[b] = wide[:, b : b + 16, :]


def forward_kernel(
    at_ref, ext_ref, kern_ref, gain_ref, b_up_ref, d_out_ref, order_hbm, w_up_hbm, d_act_hbm,
    d_cells, half_ref, own_hbm, keep_hbm, send_hbm,
    wide, shifted, normed, ordered, upper, active, tile, mixed_ref, order_ref, w_up_ref, d_act_ref,
    d_upper_ref, own, keep, give, small_ref, sems,
):
    core, x_at, y_at = at_ref[0], at_ref[1], at_ref[2]
    loads = [
        pltpu.make_async_copy(order_hbm, order_ref, sems.at[0]),
        pltpu.make_async_copy(w_up_hbm, w_up_ref, sems.at[1]),
        pltpu.make_async_copy(d_act_hbm, d_act_ref, sems.at[2]),
    ]
    for load in loads:
        load.start()
    spread_rows(ext_ref, wide, shifted)

    def conv_step(step, carry):
        lanes = pl.ds(pl.multiple_of(step * 128, 128), 128)
        totals = [jnp.zeros((16, 128), F32)] * 16
        for b in range(7):
            weights = [kern_ref[a * 7 + b : a * 7 + b + 1, lanes] for a in range(7)]
            for r in range(22):
                cells = shifted[b, r, :, lanes]
                for a in range(max(0, r - 15), min(7, r + 1)):
                    totals[r - a] = totals[r - a] + cells * weights[a]
        for x in range(16):
            mixed_ref[x * 16 : x * 16 + 16, lanes] = totals[x]
        return carry

    lax.fori_loop(0, 4, conv_step, 0)

    def norm_step(step, carry):
        rows = pl.ds(pl.multiple_of(step * 32, 32), 32)
        cells = mixed_ref[rows, :]
        center = cells - jnp.mean(cells, axis=-1, keepdims=True)
        spread = jnp.mean(center * center, axis=-1, keepdims=True)
        normed[rows, :] = (center * lax.rsqrt(spread + 1e-6) * gain_ref[...]).astype(BF16)
        return carry

    lax.fori_loop(0, 8, norm_step, 0)
    for load in loads:
        load.wait()
    ordered[...] = jnp.dot(normed[...], order_ref[...], preferred_element_type=F32).astype(BF16)

    for t in range(4):
        lanes = slice(t * 512, t * 512 + 512)
        upper[...] = jnp.dot(normed[...], w_up_ref[:, lanes], preferred_element_type=F32)

        def gelu_step(step, bias):
            rows = pl.ds(pl.multiple_of(step * 32, 32), 32)
            u = upper[rows, :] + b_up_ref[:, lanes]
            square = u * u
            th = jnp.tanh(ROOT_2_PI * (u + CUBIC * (square * u)))
            half = 0.5 * (1.0 + th)
            active[rows, :] = (u * half).astype(BF16)
            slope = half + (0.5 * ROOT_2_PI) * u * (1.0 - th * th) * (1.0 + (3.0 * CUBIC) * square)
            d_up = (d_act_ref[rows, lanes] * slope).astype(BF16)
            d_upper_ref[rows, lanes] = d_up
            return bias + jnp.sum(d_up.astype(F32), axis=0, keepdims=True)

        small_ref[50 + t : 51 + t, :] = lax.fori_loop(0, 8, gelu_step, jnp.zeros((1, 512), F32))
        tile[...] = lax.dot_general(
            active[...], d_out_ref[...], (((0,), (0,)), ((), ())), preferred_element_type=F32
        )
        for y_hi in range(2):
            k_y = (y_hi * 2 + t // 2) ^ y_at
            for k_x in range(4):
                base = y_hi * 32 + (k_x ^ x_at) * 8
                for mine in range(2):
                    at = base + ((1 - core) if mine == 0 else core) * 64
                    piece = jnp.concatenate(
                        [tile[pl.ds(pl.multiple_of(at + zz * 128, 8), 8), :] for zz in range(4)],
                        axis=0,
                    )
                    at = k_y * 64 + (t % 2) * 32
                    rows = pl.ds(pl.multiple_of(at, 32), 32)
                    if mine == 0:
                        give[pl.ds(pl.multiple_of(k_x * 512 + at, 32), 32), :] = piece.astype(BF16)
                    elif k_x == 0:
                        own[rows, :] = piece
                    else:
                        keep[k_x - 1, rows, :] = piece.astype(BF16)

    for t in range(4):
        lanes = slice(t * 512, t * 512 + 512)
        tile[...] = lax.dot_general(
            ordered[...], d_upper_ref[:, lanes], (((0,), (0,)), ((), ())),
            preferred_element_type=F32,
        )
        at = 256 + t * 64
        own[at : at + 64, :] = tile[0:64, :]
        for k in range(4):
            piece = tile[256 + k * 64 : 320 + k * 64, :]
            give[k * 512 + at : k * 512 + at + 64, :] = piece.astype(BF16)
            if k:
                keep[k - 1, at : at + 64, :] = tile[k * 64 : k * 64 + 64, :].astype(BF16)
    stores = [
        pltpu.make_async_copy(give.at[0:2048], send_hbm.at[0:2048], sems.at[3]),
        pltpu.make_async_copy(keep, keep_hbm, sems.at[4]),
        pltpu.make_async_copy(own, own_hbm, sems.at[5]),
    ]
    for store in stores:
        store.start()
    upper[...] = lax.dot_general(
        d_upper_ref[...], w_up_ref[...], (((1,), (1,)), ((), ())), preferred_element_type=F32
    )

    def norm_step(step, gain_sum):
        rows = pl.ds(pl.multiple_of(step * 32, 32), 32)
        cells = mixed_ref[rows, :]
        center = cells - jnp.mean(cells, axis=-1, keepdims=True)
        spread = jnp.mean(center * center, axis=-1, keepdims=True)
        inverse = lax.rsqrt(spread + 1e-6)
        unit = center * inverse
        d = upper[rows, :]
        d_unit = d * gain_ref[...]
        along = jnp.mean(d_unit * unit, axis=-1, keepdims=True)
        d_center = (d_unit - unit * along) * inverse
        d_mixed = d_center - jnp.mean(d_center, axis=-1, keepdims=True)
        d_cells[pl.ds(step * 2, 2)] = d_mixed.reshape(2, 16, 512)
        return gain_sum + jnp.sum(d * unit, axis=0, keepdims=True)

    small_ref[49:50, :] = lax.fori_loop(0, 8, norm_step, jnp.zeros((1, 512), F32))
    small_ref[54:64, :] = jnp.zeros((10, 512), F32)
    def tap_step(step, carry):
        lanes = pl.ds(pl.multiple_of(step * 128, 128), 128)
        d = [d_cells[x, :, lanes] for x in range(16)]
        for b in range(7):
            totals = [jnp.zeros((8, 128), F32)] * 7
            for r in range(22):
                cells = shifted[b, r, :, lanes]
                for a in range(max(0, r - 15), min(7, r + 1)):
                    product = cells * d[r - a]
                    totals[a] = totals[a] + product[:8] + product[8:]
            for a in range(7):
                row = a * 7 + b
                small_ref[row : row + 1, lanes] = jnp.sum(totals[a], axis=0, keepdims=True)
        return carry

    lax.fori_loop(0, 4, tap_step, 0)

    half_ref[...] = small_ref[pl.ds(pl.multiple_of(core * 32, 32), 32), :]
    high, low = two_terms(small_ref[pl.ds(pl.multiple_of((1 - core) * 32, 32), 32), :])
    give[2048:2080, :] = high
    give[2080:2112, :] = low
    stores.append(
        pltpu.make_async_copy(give.at[2048:2112], send_hbm.at[2048:2112], sems.at[6])
    )
    stores[-1].start()
    for store in stores:
        store.wait()


def rim_kernel(d_cells, kern_ref, grad_ref, moved):
    moved[...] = jnp.zeros_like(moved)
    for b in range(7):
        moved[b, :, b : b + 16, :] = d_cells[...]

    def rim_step(step, carry):
        lanes = pl.ds(pl.multiple_of(step * 128, 128), 128)
        for q in range(3):
            rows = slice(q * 8, q * 8 + 8)
            totals = [jnp.zeros((8, 128), F32)] * 22
            for b in range(1 if q == 2 else 0, 7):
                weights = [kern_ref[a * 7 + b : a * 7 + b + 1, lanes] for a in range(7)]
                for x in range(16):
                    cells = moved[b, x, rows, lanes]
                    for a in range(7):
                        totals[x + a] = totals[x + a] + cells * weights[a]
            for i in range(22):
                grad_ref[i, rows, lanes] = totals[i]
        return carry

    lax.fori_loop(0, 4, rim_step, 0)


VMEM_BYTES = 56 * 1024 * 1024
VMEM = pl.BlockSpec(memory_space=pltpu.VMEM)
SMEM = pl.BlockSpec(memory_space=pltpu.SMEM)
HBM = pl.BlockSpec(memory_space=pl.ANY)


def local_call(kernel, name, shapes, in_specs, out_specs, scratch, operands, flops):
    return pl.pallas_call(
        kernel,
        out_shape=[jax.ShapeDtypeStruct(s, d) for s, d in shapes],
        in_specs=in_specs,
        out_specs=out_specs,
        scratch_shapes=[pltpu.VMEM(s, d) if d else pltpu.SemaphoreType.DMA(s) for s, d in scratch],
        compiler_params=pltpu.CompilerParams(vmem_limit_bytes=VMEM_BYTES),
        cost_estimate=pl.CostEstimate(flops=flops, bytes_accessed=2000000, transcendentals=0),
        name=name,
    )(*operands)


def run_forward(at, ext, kern, gain, w_up, b_up, d_out, d_act, order):
    square, long = (256, 512), (256, 2048)
    return local_call(
        forward_kernel,
        "forward",
        [
            ((16, 16, 512), F32), ((32, 512), F32),
            ((512, 512), F32), ((3, 512, 512), BF16), ((2112, 512), BF16),
        ],
        [SMEM] + [VMEM] * 5 + [HBM] * 3,
        [VMEM, VMEM, HBM, HBM, HBM],
        [
            ((22, 32, 512), F32), ((7, 22, 16, 512), F32), (square, BF16), (square, BF16),
            (square, F32), (square, BF16), ((512, 512), F32), (square, F32), ((512, 512), BF16),
            ((512, 2048), BF16), (long, F32), (long, BF16),
            ((512, 512), F32), ((3, 512, 512), BF16), ((2112, 512), BF16), ((64, 512), F32),
            ((7,), None),
        ],
        [at, ext, kern, gain, b_up, d_out, order, w_up, d_act],
        20000000000,
    )


def run_rims(d_cells, kern):
    return local_call(
        rim_kernel,
        "rims",
        [((22, 24, 512), F32)],
        [VMEM] * 2,
        [VMEM],
        [((7, 16, 24, 512), F32)],
        [d_cells, kern],
        5000000000,
    )[0]


def run_sum(kernel, shapes, operands, name, scalars=0, scratch=()):
    return local_call(
        kernel, name, shapes, [SMEM] * scalars + [VMEM] * (len(operands) - scalars),
        [VMEM] * len(shapes), scratch, operands, 800000000,
    )


def two_terms(value):
    high = value.astype(BF16)
    return high, (value - high.astype(F32)).astype(BF16)


def rounded(high, low):
    return high.astype(F32) + low.astype(F32)


def whole(first, rest, rows):
    a, b, c = [ref[rows, :].astype(F32) for ref in rest]
    return (first + a) + (b + c)


def whole_terms(first, refs, at):
    a, b, c = [rounded(ref[at : at + 32, :], ref[at + 32 : at + 64, :]) for ref in refs]
    return (first + a) + (b + c)


def first_sum_kernel(mine_ref, keep_ref, given_ref, half_ref, own_ref, terms_ref, *give_refs):
    own_ref[...] = mine_ref[...] + given_ref[0:512, :].astype(F32)
    half = half_ref[...] + rounded(given_ref[2048:2080, :], given_ref[2080:2112, :])
    high, low = two_terms(half)
    terms_ref[...] = rounded(high, low)
    for k in range(3):
        rows = slice(k * 512 + 512, k * 512 + 1024)
        total = keep_ref[k].astype(F32) + given_ref[rows, :].astype(F32)
        give_refs[k][0:512, :] = total.astype(BF16)
        give_refs[k][512:544, :] = high
        give_refs[k][544:576, :] = low


def second_sum_kernel(own_ref, terms_ref, a_ref, b_ref, c_ref, large_ref, next_ref, *give_refs):
    refs = (a_ref, b_ref, c_ref)
    high, low = two_terms(whole_terms(terms_ref[...], refs, 512))
    next_ref[...] = rounded(high, low)
    for k in range(4):
        pieces = [(0, k * 64, 64)] + [(64 + t * 16, 256 + t * 64 + k * 16, 16) for t in range(4)]
        for target, at, count in pieces:
            rows = slice(at, at + count)
            total = whole(own_ref[rows, :], refs, rows)
            if k == 0:
                large_ref[target : target + count, :] = total
            else:
                give_refs[k - 1][target : target + count, :] = total.astype(BF16)
        if k:
            give_refs[k - 1][128:160, :] = high
            give_refs[k - 1][160:192, :] = low


def third_sum_kernel(at_ref, large_ref, terms_ref, a_ref, b_ref, c_ref, *outs):
    refs = (a_ref, b_ref, c_ref)
    own_ref, half_ref, give_refs, blocks = outs[0], outs[1], outs[2:5], outs[5]
    low_bits = at_ref[3] & 3
    high, low = two_terms(whole_terms(terms_ref[...], refs, 128))
    half_ref[...] = rounded(high, low)
    down = whole(large_ref[0:64, :], refs, slice(0, 64))
    up = whole(large_ref[64:128, :], refs, slice(64, 128))
    for z in range(8):
        rows = [up[t * 16 + z * 2 : t * 16 + z * 2 + 2] for t in range(4)]
        blocks[z] = jnp.concatenate([down[z * 8 : z * 8 + 8]] + rows, axis=0)
    for k in range(4):
        for z_high in range(2):
            block = blocks[z_high * 4 + (low_bits ^ k)]
            rows = slice(z_high * 16, z_high * 16 + 16)
            if k == 0:
                own_ref[rows, :] = block
            else:
                give_refs[k - 1][rows, :] = block.astype(BF16)
        if k:
            give_refs[k - 1][32:64, :] = high
            give_refs[k - 1][64:96, :] = low


def fourth_sum_kernel(at_ref, own_ref, half_ref, a_ref, b_ref, c_ref, keep_ref, sum_ref, give_ref):
    high = at_ref[3] >> 2
    refs = (a_ref, b_ref, c_ref)
    half = whole_terms(half_ref[...], refs, 32)
    first = whole(own_ref[0:16, :], refs, slice(0, 16))
    second = whole(own_ref[16:32, :], refs, slice(16, 32))
    keep_ref[...] = jnp.where(high == 0, first, second)
    give_ref[0:16, :] = jnp.where(high == 0, second, first)
    give_ref[16:48, :] = half
    sum_ref[...] = half


def last_sum_kernel(keep_ref, half_ref, got_ref, down_ref, up_ref, sum_ref):
    sum_ref[...] = half_ref[...] + got_ref[16:48, :]
    down_ref[...] = keep_ref[0:8, :] + got_ref[0:8, :]
    up = keep_ref[8:16, :] + got_ref[8:16, :]
    for t in range(4):
        up_ref[:, t * 512 : t * 512 + 512] = up[t * 2 : t * 2 + 2]


def per_device(
    field, cotangent, land_sea, fold_partner, depth_kernel, norm_gain, w_up, b_up, w_down
):
    width_lon, width_lat, channels = field.shape
    lon_at = lax.axis_index("lon")
    lat_at = lax.axis_index("lat")
    core = lon_at & 1
    z_at = (lon_at >> 1) & 7
    y_at = ((lat_at >> 2) << 1) + (lon_at >> 4)
    x_at = lat_at & 3
    is_north = lat_at == lax.axis_size("lat") - 1
    from_end = 511 - fold_partner[0]
    turn = 31 - (from_end >> 4)
    half_turn = (turn + 1) >> 1
    shift = 32 - ((turn & 1) << 4) - (from_end & 15)

    top_rows = field[:, width_lat - 3 :, :]
    south = to_north(top_rows)
    north = to_south(field[:, 0:3, :])
    near, far = mirror_tiles(top_rows, top_rows, half_turn)
    west = to_next(field[width_lon - 3 :])
    east = to_previous(field[0:3])
    from_next = to_previous(jnp.concatenate([near, far[13:], south[:3], north[:3]], axis=0))
    from_previous = to_next(jnp.concatenate([near[:3], south[13:], north[13:]], axis=0))
    fold = jnp.concatenate([from_next[16:19], far, from_next[:16], near, from_previous[:3]], axis=0)
    band = lax.dynamic_slice_in_dim(fold, shift, 22, axis=0)[::-1, ::-1, :]
    north = jnp.concatenate([from_previous[6:9], north, from_next[22:25]], axis=0)
    extended = jnp.concatenate(
        [
            jnp.concatenate([from_previous[3:6], south, from_next[19:22]], axis=0),
            jnp.concatenate([west, field, east], axis=0),
            jnp.where(is_north, band, north),
            jnp.zeros((22, 10, channels), jnp.bfloat16),
        ],
        axis=1,
    )
    tokens = width_lon * width_lat
    d_out = cotangent.reshape(tokens, channels) * land_sea.reshape(tokens, 1).astype(jnp.bfloat16)
    d_act = lax.dot_general(
        d_out, w_down, (((1,), (1,)), ((), ())), preferred_element_type=jnp.float32
    )
    row = jnp.arange(512, dtype=jnp.int32)
    block = row >> 1
    y_of = (((block >> 2) & 1) << 1) + (block >> 7)
    goes_to = (
        (((block >> 3) & 1) ^ core) * 256
        + ((block & 3) ^ x_at) * 64
        + (y_of ^ y_at) * 16
        + ((block >> 4) & 7) * 2
        + (row & 1)
    )
    order = (goes_to[:, None] == row[None, :]).astype(jnp.bfloat16)
    at = jnp.stack([core, x_at, y_at, z_at]).astype(jnp.int32)
    gain = norm_gain.reshape(1, channels)
    d_cells, half, mine, keep, give = run_forward(
        at, extended, depth_kernel, gain, w_up, b_up.reshape(1, 2048), d_out, d_act, order
    )

    given = send(give, CORE_MASK)
    own, terms, *give = run_sum(
        first_sum_kernel,
        [((512, 512), F32), ((32, 512), F32)] + [((576, 512), BF16)] * 3,
        [mine, keep, given, half],
        "first_sum",
    )
    own, give, d_cells = lax.optimization_barrier((own, give, d_cells))
    taken = [send(piece, mask) for piece, mask in zip(give, X_MASKS)]

    grad_ext = run_rims(d_cells, depth_kernel)[:, :22]
    rim = jnp.bfloat16
    window = jnp.where(is_north, grad_ext[::-1, 19:22][:, ::-1], 0.0).astype(rim)
    fold = lax.dynamic_update_slice_in_dim(
        jnp.zeros((54, 3, channels), rim), window, shift, axis=0
    )

    def flat(value):
        return value.astype(rim).reshape(-1, channels)

    west = to_next(
        jnp.concatenate([flat(grad_ext[19:22]), flat(fold[19:35]), flat(fold[0:3])], axis=0)
    ).astype(F32)
    east = to_previous(
        jnp.concatenate([flat(grad_ext[0:3]), flat(fold[51:54])], axis=0)
    ).astype(F32)
    taken, west, east = lax.optimization_barrier((taken, west, east))
    by_cols = (
        grad_ext[3:19]
        + jnp.pad(west[:66].reshape(3, 22, channels), ((0, 13), (0, 0), (0, 0)))
        + jnp.pad(east[:66].reshape(3, 22, channels), ((13, 0), (0, 0), (0, 0)))
    )
    near = fold[35:51].astype(F32) + west[66:114].reshape(16, 3, channels)
    near = near + jnp.pad(east[66:75].reshape(3, 3, channels), ((0, 13), (0, 0), (0, 0)))
    far = fold[3:19].astype(F32) + jnp.pad(
        west[114:123].reshape(3, 3, channels), ((13, 0), (0, 0), (0, 0))
    )
    from_south = to_north(by_cols[:, 19:22].astype(rim))
    from_north = to_south(by_cols[:, 0:3].astype(rim))
    near, far = mirror_tiles(near.astype(rim), far.astype(rim), half_turn)
    from_fold = near.astype(F32) + far.astype(F32)

    large, terms, *give = run_sum(
        second_sum_kernel,
        [((128, 512), F32), ((32, 512), F32)] + [((192, 512), BF16)] * 3,
        [own, terms, *taken],
        "second_sum",
    )
    taken = [send(piece, mask) for piece, mask in zip(give, Y_MASKS)]

    own, half, *give = run_sum(
        third_sum_kernel,
        [((32, 512), F32), ((32, 512), F32)] + [((96, 512), BF16)] * 3,
        [at, large, terms, *taken],
        "third_sum",
        scalars=1,
        scratch=[((8, 16, 512), F32)],
    )
    taken = [send(piece, mask) for piece, mask in zip(give, Z_MASKS[:3])]
    keep, half, give = run_sum(
        fourth_sum_kernel,
        [((16, 512), F32), ((32, 512), F32), ((48, 512), F32)],
        [at, own, half, *taken],
        "fourth_sum",
        scalars=1,
    )
    grad_down, grad_up, half = run_sum(
        last_sum_kernel,
        [((8, 512), F32), ((2, 2048), F32), ((32, 512), F32)],
        [keep, half, send(give, Z_MASKS[3])],
        "last_sum",
    )
    other = send(half, CORE_MASK)
    small = jnp.where(
        core == 0,
        jnp.concatenate([half, other], axis=0),
        jnp.concatenate([other, half], axis=0),
    )
    grad_kernel = small[:49]
    grad_gain = small[49]
    grad_bias = small[50:54].reshape(2048)
    owned = by_cols[:, 3:19] + jnp.pad(from_south.astype(F32), ((0, 0), (0, 13), (0, 0)))
    owned = owned + jnp.pad(from_north.astype(F32) + from_fold, ((0, 0), (13, 0), (0, 0)))
    grad_field = (cotangent.astype(F32) + owned).astype(jnp.bfloat16)
    return (grad_field, grad_up, grad_down, grad_kernel, grad_gain, grad_bias)


def solution(mesh):
    placed = (
        P("lon", "lat", None),
        P("lon", "lat", None),
        P("lon", "lat"),
        P(),
        P(),
        P(),
        P(),
        P(),
        P(),
    )
    return jax.shard_map(
        per_device,
        mesh=mesh,
        in_specs=placed,
        out_specs=(
            P("lon", "lat", None),
            P(("lon", "lat"), None),
            P(("lon", "lat"), None),
            P(),
            P(),
            P(),
        ),
        check_vma=False,
    )
```

time: 158 us -> 178 us (1.13)
  the two profiles are of different devices: /device:TPU:25 before, /device:TPU:93 now
where the time goes in v2:
time: 178 us; the launch traced here: 175 us
  starting transfers between devices  66.6 us (37%)
  Pallas kernels  36.3 us (20%)
  local copies, waits for them, and re-layouts  31.5 us (18%)
  waiting for transfers between devices  21.3 us (12%)
  other arithmetic  15.1 us (8%)
  matrix products  2.11 us (1%)
    pallas_call x7, Pallas kernels, local_call(): pl.pallas_call(kernel, out_shape=[jax.ShapeDtypeStruct(s, d) for s, d in...  36.3 us
    ppermute x12, starting transfers between devices, send(): return lax.ppermute(value, DEVICES, [(i, i ^ mask) for i in range(256)])  30.9 us
    ppermute x2, starting transfers between devices, to_north(): return lax.ppermute(value, 'lat', [(i, i + 1) for i in range(7)])  15.7 us
    ppermute x12, waiting for transfers between devices, send(): return lax.ppermute(value, DEVICES, [(i, i ^ mask) for i in range(256)])  14.7 us
    ppermute x3, starting transfers between devices, to_next(): return lax.ppermute(value, 'lon', [(i, (i + 1) % 32) for i in range(32)])  9.6 us
    ppermute x3, waiting for transfers between devices, to_previous(): return lax.ppermute(value, 'lon', [((i + 1) % 32, i) for i in range(32)])  6.53 us
    ppermute x2, starting transfers between devices, to_south(): return lax.ppermute(value, 'lat', [(i + 1, i) for i in range(7)])  5.65 us
    unnamed x31, local copies, waits for them, and re-layouts  5.21 us
  transfers between devices with their start and end apart: 26, of which 8 were waited for; matrix products, arithmetic and copies ran while one was open for 19% of the time, Pallas kernels for 2%

profile of v2, /device:TPU:93, one launch (start us, length us, event | category | flops | bytes accessed | tf_op | source)
XLA Modules:
  0.0 174.5 jit_solution(11880252400171827681)
XLA Ops:
  0.7 1.8 %fusion.11 = (bf16[16,3,512]{2,1,0:T(4,128)(2,1)}, bf16[16,3,512]{2,1,0:T(4,128)(2,1)S(1)}) fusion(bf16[16,16,512]{2,1,0:T(8,128)(2,1)} %param.41), kind=kLoop, calls=%fused_computation.50 | loop fusion | bytes 196608 | tf_op jit(solution)/shard_map/slice | solution.py:406
  2.5 2.8 %collective-permute-start.64 = (bf16[16,3,512]{2,1,0:T(4,128)(2,1)}, bf16[16,3,512]{2,1,0:T(4,128)(2,1)S(1)}, u32[]{:S(2)}, u32[]{:S(2)}) collective-permute-start(bf16[16,3,512]{2,1,0:T(4,128)(2,1)} %get-tuple-element.215), channel_id=1, source_target_pairs={{0,1},{1,2},{2,3},{3,4},{4,5},{5,6},{6,7},{8,9},{9,10},{10,11},{11... | collective-permute-start | bytes 147464 | tf_op jit(solution)/shard_map/ppermute | solution.py:28
  5.3 2.5 %collective-permute-start.65 = (bf16[16,3,512]{2,1,0:T(4,128)(2,1)S(1)}, bf16[16,3,512]{2,1,0:T(4,128)(2,1)S(1)}, u32[]{:S(2)}, u32[]{:S(2)}) collective-permute-start(bf16[16,3,512]{2,1,0:T(4,128)(2,1)S(1)} %get-tuple-element.216), channel_id=1, source_target_pairs={{1,0},{2,1},{3,2},{4,3},{5,4},{6,5},{7,6},{9,8},{10,9},{11,10},{12... | collective-permute-start | bytes 147464 | tf_op jit(solution)/shard_map/ppermute | solution.py:32
  7.8 0.8 fusion.10
  8.6 2.8 %collective-permute-start.68 = (bf16[3,16,512]{2,1,0:T(8,128)(2,1)S(1)}, bf16[3,16,512]{2,1,0:T(8,128)(2,1)S(1)}, u32[]{:S(2)}, u32[]{:S(2)}) collective-permute-start(bf16[3,16,512]{2,1,0:T(8,128)(2,1)S(1)} %get-tuple-element.213), channel_id=1, source_target_pairs={{0,8},{8,16},{16,24},{24,32},{32,40},{40,48},{48,56},{56,64},{64,7... | collective-permute-start | bytes 147464 | tf_op jit(solution)/shard_map/ppermute | solution.py:20
  11.4 1.2 slice.263
  13.3 4.1 %conditional.3 = (bf16[16,3,512]{2,1,0:T(4,128)(2,1)}, bf16[16,3,512]{2,1,0:T(4,128)(2,1)}, bf16[3,3,512]{2,1,0:T(4,128)(2,1)S(1)}, bf16[3,3,512]{2,1,0:T(4,128)(2,1)S(1)}) conditional(s32[]{:T(128)} %bitcast.4, bf16[16,3,512]{2,1,0:T(4,128)(2,1)} %get-tuple-element.215, ...), branch_computations={%region_0.0_spmd, %region_1.0_spmd, %region_2.0_spmd, %region_3.0_... | conditional | bytes 430192 | solution.py:43
  13.3 1.3 collective-permute-start.8
  14.6 1.3 collective-permute-start.9
  16.6 0.7 slice.308
  17.4 1.0 fusion.order_hbm
  18.6 2.1 %fusion.17.d_act_hbm = f32[256,2048]{1,0:T(8,128)} fusion(bf16[256,512]{1,0:T(8,128)(2,1)S(1)} %bitcast_multiply_fusion.d_out_ref, bf16[2048,512]{1,0:T(8,128)(2,1)S(1)} %copy-done), kind=kOutput, calls=%fused_computation.56 | convolution fusion | flops 536870912 | bytes 4456448 | tf_op jit(solution)/shard_map/dot_general | solution.py:428
  21.4 0.9 pad_maximum_fusion.1
  22.6 1.8 %collective-permute-start.66 = (bf16[9,3,512]{2,1,0:T(4,128)(2,1)S(1)}, bf16[9,3,512]{2,1,0:T(4,128)(2,1)S(1)}, u32[]{:S(2)}, u32[]{:S(2)}) collective-permute-start(bf16[9,3,512]{2,1,0:T(4,128)(2,1)S(1)} %pad_maximum_fusion.3), channel_id=1, source_target_pairs={{0,8},{8,16},{16,24},{24,32},{32,40},{40,48},{48,56},{56,64},{64,7... | collective-permute-start | bytes 82952 | tf_op jit(solution)/shard_map/ppermute | solution.py:20
  24.4 2.0 %collective-permute-done.67 = bf16[25,3,512]{2,1,0:T(4,128)(2,1)S(1)} collective-permute-done((bf16[25,3,512]{2,1,0:T(4,128)(2,1)S(1)}, bf16[25,3,512]{2,1,0:T(4,128)(2,1)S(1)}, u32[]{:S(2)}, u32[]{:S(2)}) %collective-permute-start.67) | collective-permute-done | bytes 76832 | tf_op jit(solution)/shard_map/ppermute | solution.py:24
  26.5 0.9 constant_dynamic-update-slice_fusion.1
  27.4 0.9 constant_dynamic-update-slice_fusion
  28.8 1.4 maximum_maximum_fusion.ext_ref
  30.2 17.9 %forward.1 = (f32[16,16,512]{2,1,0:T(8,128)}, f32[32,512]{1,0:T(8,128)}, f32[512,512]{1,0:T(8,128)}, bf16[3,512,512]{2,1,0:T(8,128)(2,1)}, bf16[2112,512]{1,0:T(8,128)(2,1)}) custom-call(s32[4]{0:T(128)} %pad_add_fusion.at_ref, bf16[22,32,512]{2,1,0:T(8,128)(2,1)} %maximum_maximum_fusion.ext_ref, f32[49,512]{1,0:T(8,128)} %kern_ref.3, f32[1,512]{1,0:T(1,128)} %bitcast.19, ...), custom_call_target="tpu_custom_call" | custom-call | flops 20000000000 | bytes 2000000 | tf_op jit(solution)/shard_map/forward/pallas_call | solution.py:241
  48.1 4.5 %collective-permute-done.70.given_ref = bf16[2112,512]{1,0:T(8,128)(2,1)S(1)} collective-permute-done((bf16[2112,512]{1,0:T(8,128)(2,1)}, bf16[2112,512]{1,0:T(8,128)(2,1)S(1)}, u32[]{:S(2)}, u32[]{:S(2)}) %collective-permute-start.70) | collective-permute-done | bytes 2162720 | tf_op jit(solution)/shard_map/ppermute | solution.py:16
  52.6 1.3 copy-done.3
  53.9 4.3 %first_sum.1 = (f32[512,512]{1,0:T(8,128)}, f32[32,512]{1,0:T(8,128)}, bf16[576,512]{1,0:T(8,128)(2,1)}, bf16[576,512]{1,0:T(8,128)(2,1)}, bf16[576,512]{1,0:T(8,128)(2,1)}) custom-call(f32[512,512]{1,0:T(8,128)} %get-tuple-element.170.mine_ref, bf16[3,512,512]{2,1,0:T(8,128)(2,1)} %get-tuple-element.171.keep_ref, bf16[2112,512]{1,0:T(8,128)(2,1)} %copy-done.3, ...), custom_call_target="tpu_custom_call" | custom-call | flops 800000000 | bytes 2000000 | tf_op jit(solution)/shard_map/first_sum/pallas_call | solution.py:241
  58.2 5.8 %rims.1 = f32[22,24,512]{2,1,0:T(8,128)} custom-call(f32[16,16,512]{2,1,0:T(8,128)} %get-tuple-element.179.d_cells, f32[49,512]{1,0:T(8,128)} %kern_ref.3), custom_call_target="tpu_custom_call" | custom-call | flops 5000000000 | bytes 2000000 | tf_op jit(solution)/shard_map/rims/pallas_call | solution.py:241
  64.0 1.4 convert.10
  66.9 1.6 rev.8
  68.6 9.4 %collective-permute-start.71 = (bf16[576,512]{1,0:T(8,128)(2,1)}, bf16[576,512]{1,0:T(8,128)(2,1)}, u32[]{:S(2)}, u32[]{:S(2)}) collective-permute-start(bf16[576,512]{1,0:T(8,128)(2,1)} %get-tuple-element.180), channel_id=1, source_target_pairs={{0,1},{1,0},{2,3},{3,2},{4,5},{5,4},{6,7},{7,6},{8,9},{9,8},{10,11... | collective-permute-start | bytes 1769480 | tf_op jit(solution)/shard_map/ppermute | solution.py:16
  78.0 1.3 collective-permute-start.73
  79.3 0.7 broadcast_in_dim.13
  80.7 0.9 reshape.110
  81.6 1.5 slice.345
  83.1 1.3 fusion.12
  84.5 1.5 reshape.107
  86.0 1.5 reshape.108
  87.5 0.7 reshape.109
  88.2 1.6 pad_maximum_fusion
  89.8 5.0 %collective-permute-start.74 = (bf16[123,512]{1,0:T(8,128)(2,1)}, bf16[123,512]{1,0:T(8,128)(2,1)}, u32[]{:S(2)}, u32[]{:S(2)}) collective-permute-start(bf16[123,512]{1,0:T(8,128)(2,1)} %pad_maximum_fusion), channel_id=1, source_target_pairs={{0,8},{8,16},{16,24},{24,32},{32,40},{40,48},{48,56},{56,64},{64,7... | collective-permute-start | bytes 377864 | tf_op jit(solution)/shard_map/ppermute | solution.py:20
  95.4 4.5 %collective-permute-done.75 = bf16[75,512]{1,0:T(8,128)(2,1)S(1)} collective-permute-done((bf16[75,512]{1,0:T(8,128)(2,1)}, bf16[75,512]{1,0:T(8,128)(2,1)S(1)}, u32[]{:S(2)}, u32[]{:S(2)}) %collective-permute-start.75) | collective-permute-done | bytes 76832 | tf_op jit(solution)/shard_map/ppermute | solution.py:24
  99.9 0.9 convert_element_type.165
  100.9 2.7 %collective-permute-done.72.b_ref = bf16[576,512]{1,0:T(8,128)(2,1)} collective-permute-done((bf16[576,512]{1,0:T(8,128)(2,1)}, bf16[576,512]{1,0:T(8,128)(2,1)}, u32[]{:S(2)}, u32[]{:S(2)}) %collective-permute-start.72) | collective-permute-done | bytes 589856 | tf_op jit(solution)/shard_map/ppermute | solution.py:16
  103.6 1.8 %collective-permute-done.73.c_ref = bf16[576,512]{1,0:T(8,128)(2,1)} collective-permute-done((bf16[576,512]{1,0:T(8,128)(2,1)}, bf16[576,512]{1,0:T(8,128)(2,1)}, u32[]{:S(2)}, u32[]{:S(2)}) %collective-permute-start.73) | collective-permute-done | bytes 589856 | tf_op jit(solution)/shard_map/ppermute | solution.py:16
  108.0 2.8 %second_sum.1 = (f32[128,512]{1,0:T(8,128)}, f32[32,512]{1,0:T(8,128)}, bf16[192,512]{1,0:T(8,128)(2,1)}, bf16[192,512]{1,0:T(8,128)(2,1)}, bf16[192,512]{1,0:T(8,128)(2,1)}) custom-call(f32[512,512]{1,0:T(8,128)} %get-tuple-element.186.own_ref, f32[32,512]{1,0:T(8,128)} %get-tuple-element.187.terms_ref, bf16[576,512]{1,0:T(8,128)(2,1)} %collective-permute-done.71.a_ref, ...), custom_call_target="tpu_custom_call" | custom-call | flops 800000000 | bytes 2000000 | tf_op jit(solution)/shard_map/second_sum/pallas_call | solution.py:241
  111.3 3.4 %collective-permute-start.80 = (bf16[192,512]{1,0:T(8,128)(2,1)}, bf16[192,512]{1,0:T(8,128)(2,1)}, u32[]{:S(2)}, u32[]{:S(2)}) collective-permute-start(bf16[192,512]{1,0:T(8,128)(2,1)} %get-tuple-element.195), channel_id=1, source_target_pairs={{0,132},{1,133},{2,134},{3,135},{4,128},{5,129},{6,130},{7,131},{8... | collective-permute-start | bytes 589832 | tf_op jit(solution)/shard_map/ppermute | solution.py:16
  115.3 0.8 reshape.115
  116.1 0.8 reshape.116
  116.9 1.6 reshape.112
  118.5 1.6 reshape.113
  120.0 2.0 %fusion.6 = (bf16[16,22,512]{2,1,0:T(8,128)(2,1)S(1)}, f32[16,22,512]{2,1,0:T(8,128)}) fusion(f32[3,22,512]{2,1,0:T(8,128)} %reshape.113, f32[3,22,512]{2,1,0:T(8,128)} %reshape.112, f32[22,24,512]{2,1,0:T(8,128)S(1)} %copy-done.1), kind=kLoop, calls=%fused_computation.46 | loop fusion | flops 540672 | bytes 2072576 | tf_op jit(solution)/shard_map/convert.3
  122.1 0.9 add_convert_fusion
  123.0 1.1 collective-permute-done.80.c_ref
  124.1 2.1 %third_sum.1 = (f32[32,512]{1,0:T(8,128)}, f32[32,512]{1,0:T(8,128)}, bf16[96,512]{1,0:T(8,128)(2,1)}, bf16[96,512]{1,0:T(8,128)(2,1)}, bf16[96,512]{1,0:T(8,128)(2,1)}) custom-call(s32[4]{0:T(128)} %pad_add_fusion.at_ref, f32[128,512]{1,0:T(8,128)} %get-tuple-element.191.large_ref, f32[32,512]{1,0:T(8,128)} %get-tuple-element.192.terms_ref, ...), custom_call_target="tpu_custom_call" | custom-call | flops 800000000 | bytes 2000000 | tf_op jit(solution)/shard_map/third_sum/pallas_call | solution.py:241
  126.2 4.5 %collective-permute-start.81 = (bf16[96,512]{1,0:T(8,128)(2,1)}, bf16[96,512]{1,0:T(8,128)(2,1)S(1)}, u32[]{:S(2)}, u32[]{:S(2)}) collective-permute-start(bf16[96,512]{1,0:T(8,128)(2,1)} %get-tuple-element.198), channel_id=1, source_target_pairs={{0,16},{1,17},{2,18},{3,19},{4,20},{5,21},{6,22},{7,23},{8,24},{9,... | collective-permute-start | bytes 294920 | tf_op jit(solution)/shard_map/ppermute | solution.py:16
  130.7 2.0 %collective-permute-start.82 = (bf16[96,512]{1,0:T(8,128)(2,1)}, bf16[96,512]{1,0:T(8,128)(2,1)S(1)}, u32[]{:S(2)}, u32[]{:S(2)}) collective-permute-start(bf16[96,512]{1,0:T(8,128)(2,1)} %get-tuple-element.199), channel_id=1, source_target_pairs={{0,32},{1,33},{2,34},{3,35},{4,36},{5,37},{6,38},{7,39},{8,40},{9,... | collective-permute-start | bytes 294920 | tf_op jit(solution)/shard_map/ppermute | solution.py:16
  133.0 2.9 %conditional.4 = (bf16[16,3,512]{2,1,0:T(4,128)(2,1)}, f32[16,3,512]{2,1,0:T(4,128)S(1)}) conditional(s32[]{:T(128)} %bitcast.4, (bf16[16,3,512]{2,1,0:T(4,128)(2,1)S(1)}, bf16[16,3,512]{2,1,0:T(4,128)(2,1)S(1)}) %tuple.221, (bf16[16,3,512]{2,1,0:T(4,128)(2,1)S(1)}, bf16[16,3,512]{2,1,0:T(4,128)(2,1)S(1)}) %tuple.221, ...), branch_computations={%region_16.17_spmd, %region_17.18_spmd, %region_18.19_spmd, %regio... | conditional | flops 73728 | bytes 589920
  133.0 1.3 collective-permute-start.40
  135.0 0.9 convert_add_fusion.4
  135.9 3.2 %collective-permute-start.77 = (bf16[16,3,512]{2,1,0:T(4,128)(2,1)S(1)}, bf16[16,3,512]{2,1,0:T(4,128)(2,1)S(1)}, u32[]{:S(2)}, u32[]{:S(2)}) collective-permute-start(bf16[16,3,512]{2,1,0:T(4,128)(2,1)S(1)} %get-tuple-element.212), channel_id=1, source_target_pairs={{1,0},{2,1},{3,2},{4,3},{5,4},{6,5},{7,6},{9,8},{10,9},{11,10},{12... | collective-permute-start | bytes 147464 | tf_op jit(solution)/shard_map/ppermute | solution.py:32
  139.1 12.8 %collective-permute-start.76 = (bf16[16,3,512]{2,1,0:T(4,128)(2,1)S(1)}, bf16[16,3,512]{2,1,0:T(4,128)(2,1)S(1)}, u32[]{:S(2)}, u32[]{:S(2)}) collective-permute-start(bf16[16,3,512]{2,1,0:T(4,128)(2,1)S(1)} %get-tuple-element.211), channel_id=1, source_target_pairs={{0,1},{1,2},{2,3},{3,4},{4,5},{5,6},{6,7},{8,9},{9,10},{10,11},{11... | collective-permute-start | bytes 147464 | tf_op jit(solution)/shard_map/ppermute | solution.py:28
  152.7 1.8 %fourth_sum.1 = (f32[16,512]{1,0:T(8,128)}, f32[32,512]{1,0:T(8,128)}, f32[48,512]{1,0:T(8,128)}) custom-call(s32[4]{0:T(128)} %pad_add_fusion.at_ref, f32[32,512]{1,0:T(8,128)} %get-tuple-element.196.own_ref, f32[32,512]{1,0:T(8,128)} %get-tuple-element.197.half_ref, bf16[96,512]{1,0:T(8,128)(2,1)} %copy-done.9, bf16[96,512]{1,0:T(8,128)(2,1)} %copy-done.10, ...), custom_call_target="tpu_custom_call" | custom-call | flops 800000000 | bytes 2000000 | tf_op jit(solution)/shard_map/fourth_sum/pallas_call | solution.py:241
  154.4 3.1 %collective-permute-start.84 = (f32[48,512]{1,0:T(8,128)}, f32[48,512]{1,0:T(8,128)S(1)}, u32[]{:S(2)}, u32[]{:S(2)}) collective-permute-start(f32[48,512]{1,0:T(8,128)} %get-tuple-element.203), channel_id=1, source_target_pairs={{0,64},{1,65},{2,66},{3,67},{4,68},{5,69},{6,70},{7,71},{8,72},{9,... | collective-permute-start | bytes 294920 | tf_op jit(solution)/shard_map/ppermute | solution.py:16
  157.6 4.4 %collective-permute-done.84.got_ref = f32[48,512]{1,0:T(8,128)S(1)} collective-permute-done((f32[48,512]{1,0:T(8,128)}, f32[48,512]{1,0:T(8,128)S(1)}, u32[]{:S(2)}, u32[]{:S(2)}) %collective-permute-start.84) | collective-permute-done | bytes 98336 | tf_op jit(solution)/shard_map/ppermute | solution.py:16
  162.7 1.7 last_sum.1
  164.3 6.3 %collective-permute-start.85 = (f32[32,512]{1,0:T(8,128)}, f32[32,512]{1,0:T(8,128)S(1)}, u32[]{:S(2)}, u32[]{:S(2)}) collective-permute-start(f32[32,512]{1,0:T(8,128)} %get-tuple-element.206), channel_id=1, source_target_pairs={{0,8},{1,9},{2,10},{3,11},{4,12},{5,13},{6,14},{7,15},{8,0},{9,1},... | collective-permute-start | bytes 196616 | tf_op jit(solution)/shard_map/ppermute | solution.py:16
  170.7 0.9 fusion.4
  171.8 0.9 maximum_select_fusion
  (88 shorter events, 13.6 us)
Async XLA Ops:
  0.6 17.9 %copy-start = (bf16[2048,512]{1,0:T(8,128)(2,1)S(1)}, bf16[2048,512]{1,0:T(8,128)(2,1)}, u32[]{:S(2)}) copy-start(bf16[2048,512]{1,0:T(8,128)(2,1)} %param.49) | copy-start | bytes 6291460
  0.6 17.7 %copy-start.8 = (s32[16,16]{1,0:T(8,128)S(1)}, s32[16,16]{1,0:T(8,128)}, u32[]{:S(2)}) copy-start(s32[16,16]{1,0:T(8,128)} %param.43) | copy-start | bytes 3076
  0.7 17.8 %copy-start.4 = (bf16[16,16,512]{2,1,0:T(8,128)(2,1)S(1)}, bf16[16,16,512]{2,1,0:T(8,128)(2,1)}, u32[]{:S(2)}) copy-start(bf16[16,16,512]{2,1,0:T(8,128)(2,1)} %param.42) | copy-start | bytes 786436
  2.5 18.9 %collective-permute-start.64 = (bf16[16,3,512]{2,1,0:T(4,128)(2,1)}, bf16[16,3,512]{2,1,0:T(4,128)(2,1)S(1)}, u32[]{:S(2)}, u32[]{:S(2)}) collective-permute-start(bf16[16,3,512]{2,1,0:T(4,128)(2,1)} %get-tuple-element.215), channel_id=1, source_target_pairs={{0,1},{1,2},{2,3},{3,4},{4,5},{5,6},{6,7},{8,9},{9,10},{10,11},{11... | collective-permute-start | bytes 147464 | tf_op jit(solution)/shard_map/ppermute | solution.py:28
  5.3 16.1 %collective-permute-start.65 = (bf16[16,3,512]{2,1,0:T(4,128)(2,1)S(1)}, bf16[16,3,512]{2,1,0:T(4,128)(2,1)S(1)}, u32[]{:S(2)}, u32[]{:S(2)}) collective-permute-start(bf16[16,3,512]{2,1,0:T(4,128)(2,1)S(1)} %get-tuple-element.216), channel_id=1, source_target_pairs={{1,0},{2,1},{3,2},{4,3},{5,4},{6,5},{7,6},{9,8},{10,9},{11,10},{12... | collective-permute-start | bytes 147464 | tf_op jit(solution)/shard_map/ppermute | solution.py:32
  8.6 20.2 %collective-permute-start.68 = (bf16[3,16,512]{2,1,0:T(8,128)(2,1)S(1)}, bf16[3,16,512]{2,1,0:T(8,128)(2,1)S(1)}, u32[]{:S(2)}, u32[]{:S(2)}) collective-permute-start(bf16[3,16,512]{2,1,0:T(8,128)(2,1)S(1)} %get-tuple-element.213), channel_id=1, source_target_pairs={{0,8},{8,16},{16,24},{24,32},{32,40},{40,48},{48,56},{56,64},{64,7... | collective-permute-start | bytes 147464 | tf_op jit(solution)/shard_map/ppermute | solution.py:20
  13.3 2.6 %collective-permute-start.8 = (bf16[16,3,512]{2,1,0:T(4,128)(2,1)}, bf16[16,3,512]{2,1,0:T(4,128)(2,1)}, u32[]{:S(2)}, u32[]{:S(2)}) collective-permute-start(bf16[16,3,512]{2,1,0:T(4,128)(2,1)} %param.4), channel_id=1, source_target_pairs={{7,71},{15,63},{23,55},{31,47},{39,39},{47,31},{55,23},{63,15},{71... | collective-permute-start | bytes 147464 | tf_op jit(solution)/shard_map/cond/branch_4_fun/ppermute | solution.py:38
  14.6 2.0 %collective-permute-start.9 = (bf16[16,3,512]{2,1,0:T(4,128)(2,1)}, bf16[16,3,512]{2,1,0:T(4,128)(2,1)}, u32[]{:S(2)}, u32[]{:S(2)}) collective-permute-start(bf16[16,3,512]{2,1,0:T(4,128)(2,1)} %param.4), channel_id=1, source_target_pairs={{7,55},{15,47},{23,39},{31,31},{39,23},{47,15},{55,7},{63,255},{71... | collective-permute-start | bytes 147464 | tf_op jit(solution)/shard_map/cond/branch_4_fun/ppermute | solution.py:38
  17.3 11.5 %collective-permute-start.69 = (bf16[3,16,512]{2,1,0:T(8,128)(2,1)S(1)}, bf16[3,16,512]{2,1,0:T(8,128)(2,1)S(1)}, u32[]{:S(2)}, u32[]{:S(2)}) collective-permute-start(bf16[3,16,512]{2,1,0:T(8,128)(2,1)S(1)} %get-tuple-element.214), channel_id=1, source_target_pairs={{8,0},{16,8},{24,16},{32,24},{40,32},{48,40},{56,48},{64,56},{72,6... | collective-permute-start | bytes 147464 | tf_op jit(solution)/shard_map/ppermute | solution.py:24
  18.5 2.1 %copy-start.5 = (bf16[256,512]{1,0:T(8,128)(2,1)}, bf16[256,512]{1,0:T(8,128)(2,1)S(1)}, u32[]{:S(2)}) copy-start(bf16[256,512]{1,0:T(8,128)(2,1)S(1)} %bitcast_multiply_fusion.d_out_ref) | copy-start | bytes 786436
  20.7 8.1 %copy-start.6 = (bf16[16,16,512]{2,1,0:T(8,128)(2,1)S(1)}, bf16[16,16,512]{2,1,0:T(8,128)(2,1)}, u32[]{:S(2)}) copy-start(bf16[16,16,512]{2,1,0:T(8,128)(2,1)} %param.41) | copy-start | bytes 786436
  22.3 4.2 %collective-permute-start.67 = (bf16[25,3,512]{2,1,0:T(4,128)(2,1)S(1)}, bf16[25,3,512]{2,1,0:T(4,128)(2,1)S(1)}, u32[]{:S(2)}, u32[]{:S(2)}) collective-permute-start(bf16[25,3,512]{2,1,0:T(4,128)(2,1)S(1)} %pad_maximum_fusion.1), channel_id=1, source_target_pairs={{8,0},{16,8},{24,16},{32,24},{40,32},{48,40},{56,48},{64,56},{72,6... | collective-permute-start | bytes 230408 | tf_op jit(solution)/shard_map/ppermute | solution.py:24
  22.6 5.7 %collective-permute-start.66 = (bf16[9,3,512]{2,1,0:T(4,128)(2,1)S(1)}, bf16[9,3,512]{2,1,0:T(4,128)(2,1)S(1)}, u32[]{:S(2)}, u32[]{:S(2)}) collective-permute-start(bf16[9,3,512]{2,1,0:T(4,128)(2,1)S(1)} %pad_maximum_fusion.3), channel_id=1, source_target_pairs={{0,8},{8,16},{16,24},{24,32},{32,40},{40,48},{48,56},{56,64},{64,7... | collective-permute-start | bytes 82952 | tf_op jit(solution)/shard_map/ppermute | solution.py:20
  48.0 4.6 %collective-permute-start.70 = (bf16[2112,512]{1,0:T(8,128)(2,1)}, bf16[2112,512]{1,0:T(8,128)(2,1)S(1)}, u32[]{:S(2)}, u32[]{:S(2)}) collective-permute-start(bf16[2112,512]{1,0:T(8,128)(2,1)} %get-tuple-element.172), channel_id=1, source_target_pairs={{0,8},{1,9},{2,10},{3,11},{4,12},{5,13},{6,14},{7,15},{8,0},{9,1},... | collective-permute-start | bytes 6488072 | tf_op jit(solution)/shard_map/ppermute | solution.py:16
  52.6 1.3 copy-start.3
  64.0 1.6 copy-start.1
  68.6 32.3 %collective-permute-start.71 = (bf16[576,512]{1,0:T(8,128)(2,1)}, bf16[576,512]{1,0:T(8,128)(2,1)}, u32[]{:S(2)}, u32[]{:S(2)}) collective-permute-start(bf16[576,512]{1,0:T(8,128)(2,1)} %get-tuple-element.180), channel_id=1, source_target_pairs={{0,1},{1,0},{2,3},{3,2},{4,5},{5,4},{6,7},{7,6},{8,9},{9,8},{10,11... | collective-permute-start | bytes 1769480 | tf_op jit(solution)/shard_map/ppermute | solution.py:16
  78.0 25.6 %collective-permute-start.72 = (bf16[576,512]{1,0:T(8,128)(2,1)}, bf16[576,512]{1,0:T(8,128)(2,1)}, u32[]{:S(2)}, u32[]{:S(2)}) collective-permute-start(bf16[576,512]{1,0:T(8,128)(2,1)} %get-tuple-element.181), channel_id=1, source_target_pairs={{0,2},{1,3},{2,0},{3,1},{4,6},{5,7},{6,4},{7,5},{8,10},{9,11},{10,... | collective-permute-start | bytes 1769480 | tf_op jit(solution)/shard_map/ppermute | solution.py:16
  78.0 27.4 %collective-permute-start.73 = (bf16[576,512]{1,0:T(8,128)(2,1)}, bf16[576,512]{1,0:T(8,128)(2,1)}, u32[]{:S(2)}, u32[]{:S(2)}) collective-permute-start(bf16[576,512]{1,0:T(8,128)(2,1)} %get-tuple-element.182), channel_id=1, source_target_pairs={{0,3},{1,2},{2,1},{3,0},{4,7},{5,6},{6,5},{7,4},{8,11},{9,10},{10,... | collective-permute-start | bytes 1769480 | tf_op jit(solution)/shard_map/ppermute | solution.py:16
  89.8 10.1 %collective-permute-start.74 = (bf16[123,512]{1,0:T(8,128)(2,1)}, bf16[123,512]{1,0:T(8,128)(2,1)}, u32[]{:S(2)}, u32[]{:S(2)}) collective-permute-start(bf16[123,512]{1,0:T(8,128)(2,1)} %pad_maximum_fusion), channel_id=1, source_target_pairs={{0,8},{8,16},{16,24},{24,32},{32,40},{40,48},{48,56},{56,64},{64,7... | collective-permute-start | bytes 377864 | tf_op jit(solution)/shard_map/ppermute | solution.py:20
  95.4 4.5 %collective-permute-start.75 = (bf16[75,512]{1,0:T(8,128)(2,1)}, bf16[75,512]{1,0:T(8,128)(2,1)S(1)}, u32[]{:S(2)}, u32[]{:S(2)}) collective-permute-start(bf16[75,512]{1,0:T(8,128)(2,1)} %pad_maximum_fusion.2), channel_id=1, source_target_pairs={{8,0},{16,8},{24,16},{32,24},{40,32},{48,40},{56,48},{64,56},{72,6... | collective-permute-start | bytes 230408 | tf_op jit(solution)/shard_map/ppermute | solution.py:24
  110.8 12.2 %collective-permute-start.78 = (bf16[192,512]{1,0:T(8,128)(2,1)}, bf16[192,512]{1,0:T(8,128)(2,1)}, u32[]{:S(2)}, u32[]{:S(2)}) collective-permute-start(bf16[192,512]{1,0:T(8,128)(2,1)} %get-tuple-element.193), channel_id=1, source_target_pairs={{0,128},{1,129},{2,130},{3,131},{4,132},{5,133},{6,134},{7,135},{8... | collective-permute-start | bytes 589832 | tf_op jit(solution)/shard_map/ppermute | solution.py:16
  111.3 11.8 %collective-permute-start.79 = (bf16[192,512]{1,0:T(8,128)(2,1)}, bf16[192,512]{1,0:T(8,128)(2,1)}, u32[]{:S(2)}, u32[]{:S(2)}) collective-permute-start(bf16[192,512]{1,0:T(8,128)(2,1)} %get-tuple-element.194), channel_id=1, source_target_pairs={{0,4},{1,5},{2,6},{3,7},{4,0},{5,1},{6,2},{7,3},{8,12},{9,13},{10,... | collective-permute-start | bytes 589832 | tf_op jit(solution)/shard_map/ppermute | solution.py:16
  111.3 12.9 %collective-permute-start.80 = (bf16[192,512]{1,0:T(8,128)(2,1)}, bf16[192,512]{1,0:T(8,128)(2,1)}, u32[]{:S(2)}, u32[]{:S(2)}) collective-permute-start(bf16[192,512]{1,0:T(8,128)(2,1)} %get-tuple-element.195), channel_id=1, source_target_pairs={{0,132},{1,133},{2,134},{3,135},{4,128},{5,129},{6,130},{7,131},{8... | collective-permute-start | bytes 589832 | tf_op jit(solution)/shard_map/ppermute | solution.py:16
  120.0 2.1 %copy-start.7 = (f32[16,3,512]{2,1,0:T(4,128)S(1)}, f32[16,3,512]{2,1,0:T(4,128)}, u32[]{:S(2)}) copy-start(f32[16,3,512]{2,1,0:T(4,128)} %reshape.114) | copy-start | bytes 294916
  126.2 25.8 %collective-permute-start.81 = (bf16[96,512]{1,0:T(8,128)(2,1)}, bf16[96,512]{1,0:T(8,128)(2,1)S(1)}, u32[]{:S(2)}, u32[]{:S(2)}) collective-permute-start(bf16[96,512]{1,0:T(8,128)(2,1)} %get-tuple-element.198), channel_id=1, source_target_pairs={{0,16},{1,17},{2,18},{3,19},{4,20},{5,21},{6,22},{7,23},{8,24},{9,... | collective-permute-start | bytes 294920 | tf_op jit(solution)/shard_map/ppermute | solution.py:16
  130.7 21.3 %collective-permute-start.82 = (bf16[96,512]{1,0:T(8,128)(2,1)}, bf16[96,512]{1,0:T(8,128)(2,1)S(1)}, u32[]{:S(2)}, u32[]{:S(2)}) collective-permute-start(bf16[96,512]{1,0:T(8,128)(2,1)} %get-tuple-element.199), channel_id=1, source_target_pairs={{0,32},{1,33},{2,34},{3,35},{4,36},{5,37},{6,38},{7,39},{8,40},{9,... | collective-permute-start | bytes 294920 | tf_op jit(solution)/shard_map/ppermute | solution.py:16
  132.7 19.3 %collective-permute-start.83 = (bf16[96,512]{1,0:T(8,128)(2,1)}, bf16[96,512]{1,0:T(8,128)(2,1)S(1)}, u32[]{:S(2)}, u32[]{:S(2)}) collective-permute-start(bf16[96,512]{1,0:T(8,128)(2,1)} %get-tuple-element.200), channel_id=1, source_target_pairs={{0,48},{1,49},{2,50},{3,51},{4,52},{5,53},{6,54},{7,55},{8,56},{9,... | collective-permute-start | bytes 294920 | tf_op jit(solution)/shard_map/ppermute | solution.py:16
  133.0 1.9 %collective-permute-start.40 = (bf16[16,3,512]{2,1,0:T(4,128)(2,1)S(1)}, bf16[16,3,512]{2,1,0:T(4,128)(2,1)}, u32[]{:S(2)}, u32[]{:S(2)}) collective-permute-start(bf16[16,3,512]{2,1,0:T(4,128)(2,1)S(1)} %get-tuple-element.95), channel_id=1, source_target_pairs={{7,71},{15,63},{23,55},{31,47},{39,39},{47,31},{55,23},{63,15},{71... | collective-permute-start | bytes 147464 | tf_op jit(solution)/shard_map/cond/branch_4_fun/ppermute | solution.py:38
  134.3 0.7 collective-permute-start.41
  135.9 21.7 %collective-permute-start.77 = (bf16[16,3,512]{2,1,0:T(4,128)(2,1)S(1)}, bf16[16,3,512]{2,1,0:T(4,128)(2,1)S(1)}, u32[]{:S(2)}, u32[]{:S(2)}) collective-permute-start(bf16[16,3,512]{2,1,0:T(4,128)(2,1)S(1)} %get-tuple-element.212), channel_id=1, source_target_pairs={{1,0},{2,1},{3,2},{4,3},{5,4},{6,5},{7,6},{9,8},{10,9},{11,10},{12... | collective-permute-start | bytes 147464 | tf_op jit(solution)/shard_map/ppermute | solution.py:32
  139.1 31.5 %collective-permute-start.76 = (bf16[16,3,512]{2,1,0:T(4,128)(2,1)S(1)}, bf16[16,3,512]{2,1,0:T(4,128)(2,1)S(1)}, u32[]{:S(2)}, u32[]{:S(2)}) collective-permute-start(bf16[16,3,512]{2,1,0:T(4,128)(2,1)S(1)} %get-tuple-element.211), channel_id=1, source_target_pairs={{0,1},{1,2},{2,3},{3,4},{4,5},{5,6},{6,7},{8,9},{9,10},{10,11},{11... | collective-permute-start | bytes 147464 | tf_op jit(solution)/shard_map/ppermute | solution.py:28
  152.0 0.6 copy-start.9
  152.0 0.7 copy-start.10
  152.0 0.7 copy-start.11
  154.4 7.6 %collective-permute-start.84 = (f32[48,512]{1,0:T(8,128)}, f32[48,512]{1,0:T(8,128)S(1)}, u32[]{:S(2)}, u32[]{:S(2)}) collective-permute-start(f32[48,512]{1,0:T(8,128)} %get-tuple-element.203), channel_id=1, source_target_pairs={{0,64},{1,65},{2,66},{3,67},{4,68},{5,69},{6,70},{7,71},{8,72},{9,... | collective-permute-start | bytes 294920 | tf_op jit(solution)/shard_map/ppermute | solution.py:16
  162.0 0.6 copy-start.12
  162.7 8.0 %copy-start.2 = (f32[16,22,512]{2,1,0:T(8,128)S(1)}, f32[16,22,512]{2,1,0:T(8,128)}, u32[]{:S(2)}) copy-start(f32[16,22,512]{2,1,0:T(8,128)} %get-tuple-element.208) | copy-start | bytes 2162692
  164.3 7.4 %collective-permute-start.85 = (f32[32,512]{1,0:T(8,128)}, f32[32,512]{1,0:T(8,128)S(1)}, u32[]{:S(2)}, u32[]{:S(2)}) collective-permute-start(f32[32,512]{1,0:T(8,128)} %get-tuple-element.206), channel_id=1, source_target_pairs={{0,8},{1,9},{2,10},{3,11},{4,12},{5,13},{6,14},{7,15},{8,0},{9,1},... | collective-permute-start | bytes 196616 | tf_op jit(solution)/shard_map/ppermute | solution.py:16

commit v3 on v2

--- a/solution.py
+++ b/solution.py
@@ -32,15 +32,12 @@
     return lax.ppermute(value, "lat", [(i + 1, i) for i in range(7)])
 
 
-def mirror_tiles(near, far, half_turn):
-    def swap(value, k):
+def mirror_tiles(value, half_turn):
+    def branch(k):
         pairs = [(e * 8 + 7, ((2 * k - e) % 32) * 8 + 7) for e in range(32)]
-        return lax.ppermute(value, DEVICES, pairs)
-
-    def branch(k):
-        return lambda a, b: (swap(a, k), swap(b, (k - 1) % 16))
-
-    return lax.switch(half_turn, [branch(k) for k in range(16)], near, far)
+        return lambda v: lax.ppermute(v, DEVICES, pairs)
+
+    return lax.switch(half_turn, [branch(k) for k in range(16)], value)
 
 
 ROOT_2_PI = 0.7978845608028654
@@ -208,7 +205,7 @@
         store.wait()
 
 
-def rim_kernel(d_cells, kern_ref, grad_ref, moved):
+def rim_kernel(d_cells, kern_ref, grad_ref, west_ref, east_ref, moved):
     moved[...] = jnp.zeros_like(moved)
     for b in range(7):
         moved[b, :, b : b + 16, :] = d_cells[...]
@@ -229,6 +226,9 @@
         return carry
 
     lax.fori_loop(0, 4, rim_step, 0)
+    filler = jnp.zeros((3, 8, 512), F32)
+    west_ref[...] = jnp.concatenate([grad_ref[0:3], filler], axis=1).astype(BF16)
+    east_ref[...] = jnp.concatenate([grad_ref[19:22], filler], axis=1).astype(BF16)
 
 
 VMEM_BYTES = 56 * 1024 * 1024
@@ -277,13 +277,13 @@
     return local_call(
         rim_kernel,
         "rims",
-        [((22, 24, 512), F32)],
+        [((22, 24, 512), F32), ((3, 32, 512), BF16), ((3, 32, 512), BF16)],
         [VMEM] * 2,
-        [VMEM],
+        [VMEM] * 3,
         [((7, 16, 24, 512), F32)],
         [d_cells, kern],
         5000000000,
-    )[0]
+    )
 
 
 def run_sum(kernel, shapes, operands, name, scalars=0, scratch=()):
@@ -318,39 +318,46 @@
     high, low = two_terms(half)
     terms_ref[...] = rounded(high, low)
     for k in range(3):
-        rows = slice(k * 512 + 512, k * 512 + 1024)
-        total = keep_ref[k].astype(F32) + given_ref[rows, :].astype(F32)
-        give_refs[k][0:512, :] = total.astype(BF16)
-        give_refs[k][512:544, :] = high
-        give_refs[k][544:576, :] = low
-
-
-def second_sum_kernel(own_ref, terms_ref, a_ref, b_ref, c_ref, large_ref, next_ref, *give_refs):
-    refs = (a_ref, b_ref, c_ref)
-    high, low = two_terms(whole_terms(terms_ref[...], refs, 512))
+        for part in range(2):
+            at = part * 256
+            rows = slice(k * 512 + 512 + at, k * 512 + 768 + at)
+            total = keep_ref[k, at : at + 256, :].astype(F32) + given_ref[rows, :].astype(F32)
+            give_refs[part * 3 + k][0:256, :] = total.astype(BF16)
+        give_refs[k][256:288, :] = high
+        give_refs[k][288:320, :] = low
+
+
+def second_sum_kernel(own_ref, terms_ref, *refs):
+    down, up, outs = refs[:3], refs[3:6], refs[6:]
+    large_ref, next_ref, over_y, over_x = outs[0], outs[1], outs[2:5], outs[5:8]
+    high, low = two_terms(whole_terms(terms_ref[...], down, 256))
     next_ref[...] = rounded(high, low)
     for k in range(4):
-        pieces = [(0, k * 64, 64)] + [(64 + t * 16, 256 + t * 64 + k * 16, 16) for t in range(4)]
-        for target, at, count in pieces:
-            rows = slice(at, at + count)
-            total = whole(own_ref[rows, :], refs, rows)
+        rows = slice(k * 64, k * 64 + 64)
+        total = whole(own_ref[rows, :], down, rows)
+        if k == 0:
+            large_ref[0:64, :] = total
+        else:
+            over_y[k - 1][0:64, :] = total.astype(BF16)
+            over_y[k - 1][64:96, :] = high
+            over_y[k - 1][96:128, :] = low
+        for t in range(4):
+            at = t * 64 + k * 16
+            total = whole(own_ref[256 + at : 272 + at, :], up, slice(at, at + 16))
             if k == 0:
-                large_ref[target : target + count, :] = total
+                large_ref[64 + t * 16 : 80 + t * 16, :] = total
             else:
-                give_refs[k - 1][target : target + count, :] = total.astype(BF16)
-        if k:
-            give_refs[k - 1][128:160, :] = high
-            give_refs[k - 1][160:192, :] = low
-
-
-def third_sum_kernel(at_ref, large_ref, terms_ref, a_ref, b_ref, c_ref, *outs):
-    refs = (a_ref, b_ref, c_ref)
-    own_ref, half_ref, give_refs, blocks = outs[0], outs[1], outs[2:5], outs[5]
+                over_x[k - 1][t * 16 : t * 16 + 16, :] = total.astype(BF16)
+
+
+def third_sum_kernel(at_ref, large_ref, terms_ref, *refs):
+    over_y, over_x = refs[:3], refs[3:6]
+    own_ref, half_ref, give_refs, blocks = refs[6], refs[7], refs[8:11], refs[11]
     low_bits = at_ref[3] & 3
-    high, low = two_terms(whole_terms(terms_ref[...], refs, 128))
+    high, low = two_terms(whole_terms(terms_ref[...], over_y, 64))
     half_ref[...] = rounded(high, low)
-    down = whole(large_ref[0:64, :], refs, slice(0, 64))
-    up = whole(large_ref[64:128, :], refs, slice(64, 128))
+    down = whole(large_ref[0:64, :], over_y, slice(0, 64))
+    up = whole(large_ref[64:128, :], over_x, slice(0, 64))
     for z in range(8):
         rows = [up[t * 16 + z * 2 : t * 16 + z * 2 + 2] for t in range(4)]
         blocks[z] = jnp.concatenate([down[z * 8 : z * 8 + 8]] + rows, axis=0)
@@ -400,29 +407,22 @@
     is_north = lat_at == lax.axis_size("lat") - 1
     from_end = 511 - fold_partner[0]
     turn = 31 - (from_end >> 4)
-    half_turn = (turn + 1) >> 1
-    shift = 32 - ((turn & 1) << 4) - (from_end & 15)
+    shift = 16 - (from_end & 15)
+    even = (turn & 1) == 0
 
     top_rows = field[:, width_lat - 3 :, :]
+    mine = mirror_tiles(top_rows, turn >> 1)
     south = to_north(top_rows)
     north = to_south(field[:, 0:3, :])
-    near, far = mirror_tiles(top_rows, top_rows, half_turn)
-    west = to_next(field[width_lon - 3 :])
-    east = to_previous(field[0:3])
-    from_next = to_previous(jnp.concatenate([near, far[13:], south[:3], north[:3]], axis=0))
-    from_previous = to_next(jnp.concatenate([near[:3], south[13:], north[13:]], axis=0))
-    fold = jnp.concatenate([from_next[16:19], far, from_next[:16], near, from_previous[:3]], axis=0)
-    band = lax.dynamic_slice_in_dim(fold, shift, 22, axis=0)[::-1, ::-1, :]
-    north = jnp.concatenate([from_previous[6:9], north, from_next[22:25]], axis=0)
+    low = jnp.where(even, to_previous(mine), mine)
+    high = jnp.where(even, mine, to_next(mine))
+    fold = lax.dynamic_slice_in_dim(jnp.concatenate([low, high], axis=0), shift, 16, axis=0)
+    north = jnp.where(is_north, fold[::-1, ::-1, :], north)
+    column = jnp.concatenate([south, field, north], axis=1)
     extended = jnp.concatenate(
-        [
-            jnp.concatenate([from_previous[3:6], south, from_next[19:22]], axis=0),
-            jnp.concatenate([west, field, east], axis=0),
-            jnp.where(is_north, band, north),
-            jnp.zeros((22, 10, channels), jnp.bfloat16),
-        ],
-        axis=1,
-    )
+        [to_next(column[width_lon - 3 :]), column, to_previous(column[:3])], axis=0
+    )
+    extended = jnp.pad(extended, ((0, 0), (0, 10), (0, 0)))
     tokens = width_lon * width_lat
     d_out = cotangent.reshape(tokens, channels) * land_sea.reshape(tokens, 1).astype(jnp.bfloat16)
     d_act = lax.dot_general(
@@ -433,8 +433,8 @@
     y_of = (((block >> 2) & 1) << 1) + (block >> 7)
     goes_to = (
         (((block >> 3) & 1) ^ core) * 256
-        + ((block & 3) ^ x_at) * 64
-        + (y_of ^ y_at) * 16
+        + (y_of ^ y_at) * 64
+        + ((block & 3) ^ x_at) * 16
         + ((block >> 4) & 7) * 2
         + (row & 1)
     )
@@ -448,53 +448,41 @@
     given = send(give, CORE_MASK)
     own, terms, *give = run_sum(
         first_sum_kernel,
-        [((512, 512), F32), ((32, 512), F32)] + [((576, 512), BF16)] * 3,
+        [((512, 512), F32), ((32, 512), F32)] + [((320, 512), BF16)] * 3 + [((256, 512), BF16)] * 3,
         [mine, keep, given, half],
         "first_sum",
     )
     own, give, d_cells = lax.optimization_barrier((own, give, d_cells))
-    taken = [send(piece, mask) for piece, mask in zip(give, X_MASKS)]
-
-    grad_ext = run_rims(d_cells, depth_kernel)[:, :22]
-    rim = jnp.bfloat16
-    window = jnp.where(is_north, grad_ext[::-1, 19:22][:, ::-1], 0.0).astype(rim)
-    fold = lax.dynamic_update_slice_in_dim(
-        jnp.zeros((54, 3, channels), rim), window, shift, axis=0
-    )
-
-    def flat(value):
-        return value.astype(rim).reshape(-1, channels)
-
-    west = to_next(
-        jnp.concatenate([flat(grad_ext[19:22]), flat(fold[19:35]), flat(fold[0:3])], axis=0)
-    ).astype(F32)
-    east = to_previous(
-        jnp.concatenate([flat(grad_ext[0:3]), flat(fold[51:54])], axis=0)
-    ).astype(F32)
-    taken, west, east = lax.optimization_barrier((taken, west, east))
-    by_cols = (
-        grad_ext[3:19]
-        + jnp.pad(west[:66].reshape(3, 22, channels), ((0, 13), (0, 0), (0, 0)))
-        + jnp.pad(east[:66].reshape(3, 22, channels), ((13, 0), (0, 0), (0, 0)))
-    )
-    near = fold[35:51].astype(F32) + west[66:114].reshape(16, 3, channels)
-    near = near + jnp.pad(east[66:75].reshape(3, 3, channels), ((0, 13), (0, 0), (0, 0)))
-    far = fold[3:19].astype(F32) + jnp.pad(
-        west[114:123].reshape(3, 3, channels), ((13, 0), (0, 0), (0, 0))
-    )
-    from_south = to_north(by_cols[:, 19:22].astype(rim))
-    from_north = to_south(by_cols[:, 0:3].astype(rim))
-    near, far = mirror_tiles(near.astype(rim), far.astype(rim), half_turn)
-    from_fold = near.astype(F32) + far.astype(F32)
-
+    taken = [send(piece, mask) for piece, mask in zip(give, X_MASKS + Y_MASKS)]
+    grad_ext, west_rim, east_rim = run_rims(d_cells, depth_kernel)
+    west_rim, east_rim, taken = lax.optimization_barrier((west_rim, east_rim, taken))
     large, terms, *give = run_sum(
         second_sum_kernel,
-        [((128, 512), F32), ((32, 512), F32)] + [((192, 512), BF16)] * 3,
+        [((128, 512), F32), ((32, 512), F32)] + [((128, 512), BF16)] * 3 + [((64, 512), BF16)] * 3,
         [own, terms, *taken],
         "second_sum",
     )
-    taken = [send(piece, mask) for piece, mask in zip(give, Y_MASKS)]
-
+    taken = [send(piece, mask) for piece, mask in zip(give, Y_MASKS + X_MASKS)]
+
+    rim = jnp.bfloat16
+    from_west = to_next(east_rim)[:, :22].astype(F32)
+    from_east = to_previous(west_rim)[:, :22].astype(F32)
+    by_cols = (
+        grad_ext[3:19, :22]
+        + jnp.pad(from_west, ((0, 13), (0, 0), (0, 0)))
+        + jnp.pad(from_east, ((13, 0), (0, 0), (0, 0)))
+    )
+    top_rim = by_cols[:, 19:22].astype(rim)
+    from_south = to_north(top_rim)
+    from_north = to_south(by_cols[:, 0:3].astype(rim))
+    strip = jnp.where(is_north, top_rim, jnp.zeros_like(top_rim))[::-1, ::-1, :]
+    spread = lax.dynamic_update_slice_in_dim(
+        jnp.zeros((32, 3, channels), rim), strip, shift, axis=0
+    )
+    none = jnp.zeros_like(spread[:16])
+    mine = jnp.where(even, spread[16:], spread[:16])
+    mine = mine + to_next(jnp.where(even, spread[:16], none))
+    mine = mine + to_previous(jnp.where(even, none, spread[16:]))
     own, half, *give = run_sum(
         third_sum_kernel,
         [((32, 512), F32), ((32, 512), F32)] + [((96, 512), BF16)] * 3,
@@ -511,6 +499,8 @@
         "fourth_sum",
         scalars=1,
     )
+    mine, give = lax.optimization_barrier((mine, give))
+    from_fold = mirror_tiles(mine, turn >> 1).astype(F32)
     grad_down, grad_up, half = run_sum(
         last_sum_kernel,
         [((8, 512), F32), ((2, 2048), F32), ((32, 512), F32)],

time: 178 us -> 149 us (0.84)
  the two profiles are of different devices: /device:TPU:93 before, /device:TPU:7 now
where the time goes in v3:
time: 149 us; the launch traced here: 147 us
  starting transfers between devices  74.3 us (50%)
  Pallas kernels  36.1 us (24%)
  waiting for transfers between devices  17 us (11%)
  other arithmetic  8.72 us (6%)
  local copies, waits for them, and re-layouts  7.54 us (5%)
  matrix products  2.09 us (1%)
  between operations  1.66 us (1%)
    ppermute x18, starting transfers between devices, send(): return lax.ppermute(value, DEVICES, [(i, i ^ mask) for i in range(256)])  37.7 us
    pallas_call x7, Pallas kernels, local_call(): pl.pallas_call(kernel, out_shape=[jax.ShapeDtypeStruct(s, d) for s, d in...  36.1 us
    ppermute x18, waiting for transfers between devices, send(): return lax.ppermute(value, DEVICES, [(i, i ^ mask) for i in range(256)])  16.3 us
    ppermute x2, starting transfers between devices, to_north(): return lax.ppermute(value, 'lat', [(i, i + 1) for i in range(7)])  11.7 us
    ppermute x4, starting transfers between devices, to_previous(): return lax.ppermute(value, 'lon', [((i + 1) % 32, i) for i in range(32)])  10.4 us
    ppermute x4, starting transfers between devices, to_next(): return lax.ppermute(value, 'lon', [(i, (i + 1) % 32) for i in range(32)])  8.07 us
    ppermute x2, starting transfers between devices, to_south(): return lax.ppermute(value, 'lat', [(i + 1, i) for i in range(7)])  3.83 us
    unnamed x44, local copies, waits for them, and re-layouts  3.28 us
  transfers between devices with their start and end apart: 32, of which 11 were waited for; matrix products, arithmetic and copies ran while one was open for 6% of the time, Pallas kernels for 10%

profile of v3, /device:TPU:7, one launch (start us, length us, event | category | flops | bytes accessed | tf_op | source)
XLA Modules:
  0.0 147.4 jit_solution(985530623016754830)
XLA Ops:
  0.6 1.3 slice.101
  2.0 1.0 fusion.16
  3.7 1.3 conditional.5
  3.7 1.3 collective-permute-start.8
  5.0 0.7 collective-permute-start.33
  5.6 1.5 %collective-permute-start.34 = (bf16[16,3,512]{2,1,0:T(4,128)(2,1)}, bf16[16,3,512]{2,1,0:T(4,128)(2,1)S(1)}, u32[]{:S(2)}, u32[]{:S(2)}) collective-permute-start(bf16[16,3,512]{2,1,0:T(4,128)(2,1)} %get-tuple-element.197), channel_id=1, source_target_pairs={{0,8},{8,16},{16,24},{24,32},{32,40},{40,48},{48,56},{56,64},{64,7... | collective-permute-start | bytes 147464 | tf_op jit(solution)/shard_map/ppermute | solution.py:20
  7.2 4.7 %collective-permute-start.32 = (bf16[16,3,512]{2,1,0:T(4,128)(2,1)S(1)}, bf16[16,3,512]{2,1,0:T(4,128)(2,1)S(1)}, u32[]{:S(2)}, u32[]{:S(2)}) collective-permute-start(bf16[16,3,512]{2,1,0:T(4,128)(2,1)S(1)} %get-tuple-element.192), channel_id=1, source_target_pairs={{0,1},{1,2},{2,3},{3,4},{4,5},{5,6},{6,7},{8,9},{9,10},{10,11},{11... | collective-permute-start | bytes 147464 | tf_op jit(solution)/shard_map/ppermute | solution.py:28
  11.9 1.9 %collective-permute-start.35 = (bf16[16,3,512]{2,1,0:T(4,128)(2,1)S(1)}, bf16[16,3,512]{2,1,0:T(4,128)(2,1)S(1)}, u32[]{:S(2)}, u32[]{:S(2)}) collective-permute-start(bf16[16,3,512]{2,1,0:T(4,128)(2,1)S(1)} %get-tuple-element.191), channel_id=1, source_target_pairs={{1,0},{2,1},{3,2},{4,3},{5,4},{6,5},{7,6},{9,8},{10,9},{11,10},{12... | collective-permute-start | bytes 147464 | tf_op jit(solution)/shard_map/ppermute | solution.py:32
  13.8 0.7 convert_element_type.76
  14.6 1.1 bitcast_multiply_fusion.d_out_ref
  15.7 2.1 %fusion.17.d_act_hbm = f32[256,2048]{1,0:T(8,128)} fusion(bf16[256,512]{1,0:T(8,128)(2,1)S(1)} %bitcast_multiply_fusion.d_out_ref, bf16[2048,512]{1,0:T(8,128)(2,1)S(1)} %copy-done), kind=kOutput, calls=%fused_computation.40 | convolution fusion | flops 536870912 | bytes 4456448 | tf_op jit(solution)/shard_map/dot_general | solution.py:428
  17.8 1.0 fusion.5.order_hbm
  18.8 0.9 broadcast_select_fusion.2
  19.8 0.2 rev.6
  20.1 0.4 collective-permute-done.35
  20.7 2.4 %collective-permute-start.36 = (bf16[3,22,512]{2,1,0:T(8,128)(2,1)S(1)}, bf16[3,22,512]{2,1,0:T(8,128)(2,1)S(1)}, u32[]{:S(2)}, u32[]{:S(2)}) collective-permute-start(bf16[3,22,512]{2,1,0:T(8,128)(2,1)S(1)} %get-tuple-element.189), channel_id=1, source_target_pairs={{0,8},{8,16},{16,24},{24,32},{32,40},{40,48},{48,56},{56,64},{64,7... | collective-permute-start | bytes 202760 | tf_op jit(solution)/shard_map/ppermute | solution.py:20
  23.1 3.7 %collective-permute-start.37 = (bf16[3,22,512]{2,1,0:T(8,128)(2,1)S(1)}, bf16[3,22,512]{2,1,0:T(8,128)(2,1)S(1)}, u32[]{:S(2)}, u32[]{:S(2)}) collective-permute-start(bf16[3,22,512]{2,1,0:T(8,128)(2,1)S(1)} %get-tuple-element.190), channel_id=1, source_target_pairs={{8,0},{16,8},{24,16},{32,24},{40,32},{48,40},{56,48},{64,56},{72,6... | collective-permute-start | bytes 202760 | tf_op jit(solution)/shard_map/ppermute | solution.py:24
  26.8 0.7 pad_add_fusion.at_ref
  27.4 0.2 collective-permute-done.37
  27.7 1.2 fusion.7.ext_ref
  28.8 17.9 %forward.1 = (f32[16,16,512]{2,1,0:T(8,128)}, f32[32,512]{1,0:T(8,128)}, f32[512,512]{1,0:T(8,128)}, bf16[3,512,512]{2,1,0:T(8,128)(2,1)}, bf16[2112,512]{1,0:T(8,128)(2,1)}) custom-call(s32[4]{0:T(128)} %pad_add_fusion.at_ref, bf16[22,32,512]{2,1,0:T(8,128)(2,1)} %fusion.7.ext_ref, f32[49,512]{1,0:T(8,128)} %kern_ref.3, f32[1,512]{1,0:T(1,128)} %bitcast.21, ...), custom_call_target="tpu_custom_call" | custom-call | flops 20000000000 | bytes 2000000 | tf_op jit(solution)/shard_map/forward/pallas_call | solution.py:241
  46.7 5.0 %collective-permute-start.38 = (bf16[2112,512]{1,0:T(8,128)(2,1)}, bf16[2112,512]{1,0:T(8,128)(2,1)S(1)}, u32[]{:S(2)}, u32[]{:S(2)}) collective-permute-start(bf16[2112,512]{1,0:T(8,128)(2,1)} %get-tuple-element.133), channel_id=1, source_target_pairs={{0,8},{1,9},{2,10},{3,11},{4,12},{5,13},{6,14},{7,15},{8,0},{9,1},... | collective-permute-start | bytes 6488072 | tf_op jit(solution)/shard_map/ppermute | solution.py:16
  51.7 4.1 %collective-permute-done.38.given_ref = bf16[2112,512]{1,0:T(8,128)(2,1)S(1)} collective-permute-done((bf16[2112,512]{1,0:T(8,128)(2,1)}, bf16[2112,512]{1,0:T(8,128)(2,1)S(1)}, u32[]{:S(2)}, u32[]{:S(2)}) %collective-permute-start.38) | collective-permute-done | bytes 2162720 | tf_op jit(solution)/shard_map/ppermute | solution.py:16
  55.8 1.3 copy-done.1
  57.1 4.1 %first_sum.1 = (f32[512,512]{1,0:T(8,128)}, f32[32,512]{1,0:T(8,128)}, bf16[320,512]{1,0:T(8,128)(2,1)}, bf16[320,512]{1,0:T(8,128)(2,1)}, bf16[320,512]{1,0:T(8...) custom-call(f32[512,512]{1,0:T(8,128)} %get-tuple-element.131.mine_ref, ...), custom_call_target="tpu_custom_call" | custom-call | flops 800000000 | bytes 2000000 | tf_op jit(solution)/shard_map/first_sum/pallas_call | solution.py:241
  61.4 3.7 %collective-permute-start.41 = (bf16[320,512]{1,0:T(8,128)(2,1)}, bf16[320,512]{1,0:T(8,128)(2,1)S(1)}, u32[]{:S(2)}, u32[]{:S(2)}) collective-permute-start(bf16[320,512]{1,0:T(8,128)(2,1)} %get-tuple-element.149), channel_id=1, source_target_pairs={{0,3},{1,2},{2,1},{3,0},{4,7},{5,6},{6,5},{7,4},{8,11},{9,10},{10,... | collective-permute-start | bytes 983048 | tf_op jit(solution)/shard_map/ppermute | solution.py:16
  65.1 5.7 %collective-permute-start.43 = (bf16[256,512]{1,0:T(8,128)(2,1)}, bf16[256,512]{1,0:T(8,128)(2,1)S(1)}, u32[]{:S(2)}, u32[]{:S(2)}) collective-permute-start(bf16[256,512]{1,0:T(8,128)(2,1)} %get-tuple-element.151), channel_id=1, source_target_pairs={{0,4},{1,5},{2,6},{3,7},{4,0},{5,1},{6,2},{7,3},{8,12},{9,13},{10,... | collective-permute-start | bytes 786440 | tf_op jit(solution)/shard_map/ppermute | solution.py:16
  70.8 2.7 %collective-permute-start.44 = (bf16[256,512]{1,0:T(8,128)(2,1)}, bf16[256,512]{1,0:T(8,128)(2,1)S(1)}, u32[]{:S(2)}, u32[]{:S(2)}) collective-permute-start(bf16[256,512]{1,0:T(8,128)(2,1)} %get-tuple-element.152), channel_id=1, source_target_pairs={{0,132},{1,133},{2,134},{3,135},{4,128},{5,129},{6,130},{7,131},{8... | collective-permute-start | bytes 786440 | tf_op jit(solution)/shard_map/ppermute | solution.py:16
  73.5 5.9 %rims.1 = (f32[22,24,512]{2,1,0:T(8,128)}, bf16[3,32,512]{2,1,0:T(8,128)(2,1)}, bf16[3,32,512]{2,1,0:T(8,128)(2,1)}) custom-call(f32[16,16,512]{2,1,0:T(8,128)} %get-tuple-element.143.d_cells, f32[49,512]{1,0:T(8,128)} %kern_ref.3), custom_call_target="tpu_custom_call" | custom-call | flops 5000000000 | bytes 2000000 | tf_op jit(solution)/shard_map/rims/pallas_call | solution.py:241
  79.4 5.8 %collective-permute-done.44.refs_5_ = bf16[256,512]{1,0:T(8,128)(2,1)S(1)} collective-permute-done((bf16[256,512]{1,0:T(8,128)(2,1)}, bf16[256,512]{1,0:T(8,128)(2,1)S(1)}, u32[]{:S(2)}, u32[]{:S(2)}) %collective-permute-start.44) | collective-permute-done | bytes 262176 | tf_op jit(solution)/shard_map/ppermute | solution.py:16
  85.2 0.8 collective-permute-start.45
  85.9 0.4 collective-permute-start.46
  86.4 2.9 %second_sum.1 = (f32[128,512]{1,0:T(8,128)}, f32[32,512]{1,0:T(8,128)}, bf16[128,512]{1,0:T(8,128)(2,1)}, bf16[128,512]{1,0:T(8,128)(2,1)}, bf16[128,512]{1,0:T(...) custom-call(f32[512,512]{1,0:T(8,128)} %get-tuple-element.155.own_ref, ...), custom_call_target="tpu_custom_call" | custom-call | flops 800000000 | bytes 2000000 | tf_op jit(solution)/shard_map/second_sum/pallas_call | solution.py:241
  89.2 0.4 collective-permute-start.51
  89.6 1.8 %collective-permute-start.52 = (bf16[128,512]{1,0:T(8,128)(2,1)}, bf16[128,512]{1,0:T(8,128)(2,1)S(1)}, u32[]{:S(2)}, u32[]{:S(2)}) collective-permute-start(bf16[128,512]{1,0:T(8,128)(2,1)} %get-tuple-element.166), channel_id=1, source_target_pairs={{0,4},{1,5},{2,6},{3,7},{4,0},{5,1},{6,2},{7,3},{8,12},{9,13},{10,... | collective-permute-start | bytes 393224 | tf_op jit(solution)/shard_map/ppermute | solution.py:16
  91.5 1.6 %collective-permute-start.53 = (bf16[128,512]{1,0:T(8,128)(2,1)}, bf16[128,512]{1,0:T(8,128)(2,1)}, u32[]{:S(2)}, u32[]{:S(2)}) collective-permute-start(bf16[128,512]{1,0:T(8,128)(2,1)} %get-tuple-element.167), channel_id=1, source_target_pairs={{0,132},{1,133},{2,134},{3,135},{4,128},{5,129},{6,130},{7,131},{8... | collective-permute-start | bytes 393224 | tf_op jit(solution)/shard_map/ppermute | solution.py:16
  93.1 1.5 %collective-permute-start.55 = (bf16[64,512]{1,0:T(8,128)(2,1)}, bf16[64,512]{1,0:T(8,128)(2,1)}, u32[]{:S(2)}, u32[]{:S(2)}) collective-permute-start(bf16[64,512]{1,0:T(8,128)(2,1)} %get-tuple-element.169), channel_id=1, source_target_pairs={{0,2},{1,3},{2,0},{3,1},{4,6},{5,7},{6,4},{7,5},{8,10},{9,11},{10,... | collective-permute-start | bytes 196616 | tf_op jit(solution)/shard_map/ppermute | solution.py:16
  94.9 0.2 rev.7
  95.2 1.5 %collective-permute-done.54.refs_3_ = bf16[64,512]{1,0:T(8,128)(2,1)S(1)} collective-permute-done((bf16[64,512]{1,0:T(8,128)(2,1)}, bf16[64,512]{1,0:T(8,128)(2,1)S(1)}, u32[]{:S(2)}, u32[]{:S(2)}) %collective-permute-start.54) | collective-permute-done | bytes 65568 | tf_op jit(solution)/shard_map/ppermute | solution.py:16
  96.7 1.2 collective-permute-start.56
  98.2 3.4 %collective-permute-start.49 = (bf16[16,3,512]{2,1,0:T(4,128)(2,1)S(1)}, bf16[16,3,512]{2,1,0:T(4,128)(2,1)S(1)}, u32[]{:S(2)}, u32[]{:S(2)}) collective-permute-start(bf16[16,3,512]{2,1,0:T(4,128)(2,1)S(1)} %get-tuple-element.193), channel_id=1, source_target_pairs={{0,8},{8,16},{16,24},{24,32},{32,40},{40,48},{48,56},{56,64},{64,7... | collective-permute-start | bytes 147464 | tf_op jit(solution)/shard_map/ppermute | solution.py:20
  101.5 5.7 %collective-permute-start.50 = (bf16[16,3,512]{2,1,0:T(4,128)(2,1)S(1)}, bf16[16,3,512]{2,1,0:T(4,128)(2,1)S(1)}, u32[]{:S(2)}, u32[]{:S(2)}) collective-permute-start(bf16[16,3,512]{2,1,0:T(4,128)(2,1)S(1)} %get-tuple-element.194), channel_id=1, source_target_pairs={{8,0},{16,8},{24,16},{32,24},{40,32},{48,40},{56,48},{64,56},{72,6... | collective-permute-start | bytes 147464 | tf_op jit(solution)/shard_map/ppermute | solution.py:24
  107.2 1.9 %collective-permute-start.48 = (bf16[16,3,512]{2,1,0:T(4,128)(2,1)S(1)}, bf16[16,3,512]{2,1,0:T(4,128)(2,1)S(1)}, u32[]{:S(2)}, u32[]{:S(2)}) collective-permute-start(bf16[16,3,512]{2,1,0:T(4,128)(2,1)S(1)} %get-tuple-element.188), channel_id=1, source_target_pairs={{1,0},{2,1},{3,2},{4,3},{5,4},{6,5},{7,6},{9,8},{10,9},{11,10},{12... | collective-permute-start | bytes 147464 | tf_op jit(solution)/shard_map/ppermute | solution.py:32
  109.1 7.0 %collective-permute-start.47 = (bf16[16,3,512]{2,1,0:T(4,128)(2,1)S(1)}, bf16[16,3,512]{2,1,0:T(4,128)(2,1)S(1)}, u32[]{:S(2)}, u32[]{:S(2)}) collective-permute-start(bf16[16,3,512]{2,1,0:T(4,128)(2,1)S(1)} %get-tuple-element.186), channel_id=1, source_target_pairs={{0,1},{1,2},{2,3},{3,4},{4,5},{5,6},{6,7},{8,9},{9,10},{10,11},{11... | collective-permute-start | bytes 147464 | tf_op jit(solution)/shard_map/ppermute | solution.py:28
  116.2 2.0 %third_sum.1 = (f32[32,512]{1,0:T(8,128)}, f32[32,512]{1,0:T(8,128)}, bf16[96,512]{1,0:T(8,128)(2,1)}, bf16[96,512]{1,0:T(8,128)(2,1)}, bf16[96,512]{1,0:T(8,128)(2,1)}) custom-call(s32[4]{0:T(128)} %pad_add_fusion.at_ref, f32[128,512]{1,0:T(8,128)} %get-tuple-element.163.large_ref, f32[32,512]{1,0:T(8,128)} %get-tuple-element.164.terms_ref, ...), custom_call_target="tpu_custom_call" | custom-call | flops 800000000 | bytes 2000000 | tf_op jit(solution)/shard_map/third_sum/pallas_call | solution.py:241
  118.3 3.4 %collective-permute-start.59 = (bf16[96,512]{1,0:T(8,128)(2,1)}, bf16[96,512]{1,0:T(8,128)(2,1)S(1)}, u32[]{:S(2)}, u32[]{:S(2)}) collective-permute-start(bf16[96,512]{1,0:T(8,128)(2,1)} %get-tuple-element.175), channel_id=1, source_target_pairs={{0,48},{1,49},{2,50},{3,51},{4,52},{5,53},{6,54},{7,55},{8,56},{9,... | collective-permute-start | bytes 294920 | tf_op jit(solution)/shard_map/ppermute | solution.py:16
  121.9 1.1 collective-permute-done.58.b_ref
  123.0 2.9 %collective-permute-done.59.c_ref = bf16[96,512]{1,0:T(8,128)(2,1)S(1)} collective-permute-done((bf16[96,512]{1,0:T(8,128)(2,1)}, bf16[96,512]{1,0:T(8,128)(2,1)S(1)}, u32[]{:S(2)}, u32[]{:S(2)}) %collective-permute-start.59) | collective-permute-done | bytes 98336 | tf_op jit(solution)/shard_map/ppermute | solution.py:16
  125.9 0.6 copy-done.17
  126.5 1.8 %fourth_sum.1 = (f32[16,512]{1,0:T(8,128)}, f32[32,512]{1,0:T(8,128)}, f32[48,512]{1,0:T(8,128)}) custom-call(s32[4]{0:T(128)} %pad_add_fusion.at_ref, f32[32,512]{1,0:T(8,128)} %get-tuple-element.171.own_ref, f32[32,512]{1,0:T(8,128)} %get-tuple-element.172.half_ref, bf16[96,512]{1,0:T(8,128)(2,1)} %copy-done.15, bf16[96,512]{1,0:T(8,128)(2,1)} %copy-done.16, ...), custom_call_target="tpu_custom_call" | custom-call | flops 800000000 | bytes 2000000 | tf_op jit(solution)/shard_map/fourth_sum/pallas_call | solution.py:241
  128.2 5.0 %collective-permute-start.60 = (f32[48,512]{1,0:T(8,128)}, f32[48,512]{1,0:T(8,128)S(1)}, u32[]{:S(2)}, u32[]{:S(2)}) collective-permute-start(f32[48,512]{1,0:T(8,128)} %get-tuple-element.180), channel_id=1, source_target_pairs={{0,64},{1,65},{2,66},{3,67},{4,68},{5,69},{6,70},{7,71},{8,72},{9,... | collective-permute-start | bytes 294920 | tf_op jit(solution)/shard_map/ppermute | solution.py:16
  133.2 1.3 conditional.6
  133.2 1.3 collective-permute-start.24
  134.5 0.9 convert_add_fusion.1
  135.4 0.5 collective-permute-done.60.got_ref
  135.8 0.6 copy-done.14
  136.5 1.6 %last_sum.1 = (f32[8,512]{1,0:T(8,128)}, f32[2,2048]{1,0:T(2,128)}, f32[32,512]{1,0:T(8,128)}) custom-call(f32[16,512]{1,0:T(8,128)} %get-tuple-element.178.keep_ref, f32[32,512]{1,0:T(8,128)} %get-tuple-element.179.half_ref, f32[48,512]{1,0:T(8,128)} %copy-done.14), custom_call_target="tpu_custom_call" | custom-call | flops 800000000 | bytes 2000000 | tf_op jit(solution)/shard_map/last_sum/pallas_call | solution.py:241
  138.1 5.4 %collective-permute-start.61 = (f32[32,512]{1,0:T(8,128)}, f32[32,512]{1,0:T(8,128)S(1)}, u32[]{:S(2)}, u32[]{:S(2)}) collective-permute-start(f32[32,512]{1,0:T(8,128)} %get-tuple-element.183), channel_id=1, source_target_pairs={{0,8},{1,9},{2,10},{3,11},{4,12},{5,13},{6,14},{7,15},{8,0},{9,1},... | collective-permute-start | bytes 196616 | tf_op jit(solution)/shard_map/ppermute | solution.py:16
  143.5 0.9 fusion.12
  144.4 0.2 collective-permute-done.61
  144.6 0.9 maximum_select_fusion
  145.6 0.7 slice.123
  146.2 0.6 slice.124
  146.8 0.6 copy.15
  (82 shorter events, 1.4 us)
Async XLA Ops:
  0.6 15.1 %copy-start = (bf16[2048,512]{1,0:T(8,128)(2,1)S(1)}, bf16[2048,512]{1,0:T(8,128)(2,1)}, u32[]{:S(2)}) copy-start(bf16[2048,512]{1,0:T(8,128)(2,1)} %param.49) | copy-start | bytes 6291460
  3.7 1.3 collective-permute-start.8
  5.0 13.8 %collective-permute-start.33 = (bf16[16,3,512]{2,1,0:T(4,128)(2,1)}, bf16[16,3,512]{2,1,0:T(4,128)(2,1)S(1)}, u32[]{:S(2)}, u32[]{:S(2)}) collective-permute-start(bf16[16,3,512]{2,1,0:T(4,128)(2,1)} %get-tuple-element.197), channel_id=1, source_target_pairs={{8,0},{16,8},{24,16},{32,24},{40,32},{48,40},{56,48},{64,56},{72,6... | collective-permute-start | bytes 147464 | tf_op jit(solution)/shard_map/ppermute | solution.py:24
  5.6 13.2 %collective-permute-start.34 = (bf16[16,3,512]{2,1,0:T(4,128)(2,1)}, bf16[16,3,512]{2,1,0:T(4,128)(2,1)S(1)}, u32[]{:S(2)}, u32[]{:S(2)}) collective-permute-start(bf16[16,3,512]{2,1,0:T(4,128)(2,1)} %get-tuple-element.197), channel_id=1, source_target_pairs={{0,8},{8,16},{16,24},{24,32},{32,40},{40,48},{48,56},{56,64},{64,7... | collective-permute-start | bytes 147464 | tf_op jit(solution)/shard_map/ppermute | solution.py:20
  7.2 13.4 %collective-permute-start.32 = (bf16[16,3,512]{2,1,0:T(4,128)(2,1)S(1)}, bf16[16,3,512]{2,1,0:T(4,128)(2,1)S(1)}, u32[]{:S(2)}, u32[]{:S(2)}) collective-permute-start(bf16[16,3,512]{2,1,0:T(4,128)(2,1)S(1)} %get-tuple-element.192), channel_id=1, source_target_pairs={{0,1},{1,2},{2,3},{3,4},{4,5},{5,6},{6,7},{8,9},{9,10},{10,11},{11... | collective-permute-start | bytes 147464 | tf_op jit(solution)/shard_map/ppermute | solution.py:28
  11.9 8.6 %collective-permute-start.35 = (bf16[16,3,512]{2,1,0:T(4,128)(2,1)S(1)}, bf16[16,3,512]{2,1,0:T(4,128)(2,1)S(1)}, u32[]{:S(2)}, u32[]{:S(2)}) collective-permute-start(bf16[16,3,512]{2,1,0:T(4,128)(2,1)S(1)} %get-tuple-element.191), channel_id=1, source_target_pairs={{1,0},{2,1},{3,2},{4,3},{5,4},{6,5},{7,6},{9,8},{10,9},{11,10},{12... | collective-permute-start | bytes 147464 | tf_op jit(solution)/shard_map/ppermute | solution.py:32
  15.7 2.1 %copy-start.4 = (bf16[256,512]{1,0:T(8,128)(2,1)}, bf16[256,512]{1,0:T(8,128)(2,1)S(1)}, u32[]{:S(2)}) copy-start(bf16[256,512]{1,0:T(8,128)(2,1)S(1)} %bitcast_multiply_fusion.d_out_ref) | copy-start | bytes 786436
  17.8 2.8 %copy-start.2 = (bf16[16,16,512]{2,1,0:T(8,128)(2,1)S(1)}, bf16[16,16,512]{2,1,0:T(8,128)(2,1)}, u32[]{:S(2)}) copy-start(bf16[16,16,512]{2,1,0:T(8,128)(2,1)} %param.41) | copy-start | bytes 786436
  20.7 6.8 %collective-permute-start.36 = (bf16[3,22,512]{2,1,0:T(8,128)(2,1)S(1)}, bf16[3,22,512]{2,1,0:T(8,128)(2,1)S(1)}, u32[]{:S(2)}, u32[]{:S(2)}) collective-permute-start(bf16[3,22,512]{2,1,0:T(8,128)(2,1)S(1)} %get-tuple-element.189), channel_id=1, source_target_pairs={{0,8},{8,16},{16,24},{24,32},{32,40},{40,48},{48,56},{56,64},{64,7... | collective-permute-start | bytes 202760 | tf_op jit(solution)/shard_map/ppermute | solution.py:20
  23.1 4.6 %collective-permute-start.37 = (bf16[3,22,512]{2,1,0:T(8,128)(2,1)S(1)}, bf16[3,22,512]{2,1,0:T(8,128)(2,1)S(1)}, u32[]{:S(2)}, u32[]{:S(2)}) collective-permute-start(bf16[3,22,512]{2,1,0:T(8,128)(2,1)S(1)} %get-tuple-element.190), channel_id=1, source_target_pairs={{8,0},{16,8},{24,16},{32,24},{40,32},{48,40},{56,48},{64,56},{72,6... | collective-permute-start | bytes 202760 | tf_op jit(solution)/shard_map/ppermute | solution.py:24
  46.7 9.1 %collective-permute-start.38 = (bf16[2112,512]{1,0:T(8,128)(2,1)}, bf16[2112,512]{1,0:T(8,128)(2,1)S(1)}, u32[]{:S(2)}, u32[]{:S(2)}) collective-permute-start(bf16[2112,512]{1,0:T(8,128)(2,1)} %get-tuple-element.133), channel_id=1, source_target_pairs={{0,8},{1,9},{2,10},{3,11},{4,12},{5,13},{6,14},{7,15},{8,0},{9,1},... | collective-permute-start | bytes 6488072 | tf_op jit(solution)/shard_map/ppermute | solution.py:16
  55.8 1.3 copy-start.1
  61.2 9.6 %collective-permute-start.42 = (bf16[256,512]{1,0:T(8,128)(2,1)}, bf16[256,512]{1,0:T(8,128)(2,1)S(1)}, u32[]{:S(2)}, u32[]{:S(2)}) collective-permute-start(bf16[256,512]{1,0:T(8,128)(2,1)} %get-tuple-element.150), channel_id=1, source_target_pairs={{0,128},{1,129},{2,130},{3,131},{4,132},{5,133},{6,134},{7,135},{8... | collective-permute-start | bytes 786440 | tf_op jit(solution)/shard_map/ppermute | solution.py:16
  61.2 24.0 %collective-permute-start.39 = (bf16[320,512]{1,0:T(8,128)(2,1)}, bf16[320,512]{1,0:T(8,128)(2,1)S(1)}, u32[]{:S(2)}, u32[]{:S(2)}) collective-permute-start(bf16[320,512]{1,0:T(8,128)(2,1)} %get-tuple-element.147), channel_id=1, source_target_pairs={{0,1},{1,0},{2,3},{3,2},{4,5},{5,4},{6,7},{7,6},{8,9},{9,8},{10,11... | collective-permute-start | bytes 983048 | tf_op jit(solution)/shard_map/ppermute | solution.py:16
  61.3 23.9 %collective-permute-start.40 = (bf16[320,512]{1,0:T(8,128)(2,1)}, bf16[320,512]{1,0:T(8,128)(2,1)S(1)}, u32[]{:S(2)}, u32[]{:S(2)}) collective-permute-start(bf16[320,512]{1,0:T(8,128)(2,1)} %get-tuple-element.148), channel_id=1, source_target_pairs={{0,2},{1,3},{2,0},{3,1},{4,6},{5,7},{6,4},{7,5},{8,10},{9,11},{10,... | collective-permute-start | bytes 983048 | tf_op jit(solution)/shard_map/ppermute | solution.py:16
  61.4 23.8 %collective-permute-start.41 = (bf16[320,512]{1,0:T(8,128)(2,1)}, bf16[320,512]{1,0:T(8,128)(2,1)S(1)}, u32[]{:S(2)}, u32[]{:S(2)}) collective-permute-start(bf16[320,512]{1,0:T(8,128)(2,1)} %get-tuple-element.149), channel_id=1, source_target_pairs={{0,3},{1,2},{2,1},{3,0},{4,7},{5,6},{6,5},{7,4},{8,11},{9,10},{10,... | collective-permute-start | bytes 983048 | tf_op jit(solution)/shard_map/ppermute | solution.py:16
  65.1 14.2 %collective-permute-start.43 = (bf16[256,512]{1,0:T(8,128)(2,1)}, bf16[256,512]{1,0:T(8,128)(2,1)S(1)}, u32[]{:S(2)}, u32[]{:S(2)}) collective-permute-start(bf16[256,512]{1,0:T(8,128)(2,1)} %get-tuple-element.151), channel_id=1, source_target_pairs={{0,4},{1,5},{2,6},{3,7},{4,0},{5,1},{6,2},{7,3},{8,12},{9,13},{10,... | collective-permute-start | bytes 786440 | tf_op jit(solution)/shard_map/ppermute | solution.py:16
  70.8 8.6 %copy-start.9 = (bf16[256,512]{1,0:T(8,128)(2,1)}, bf16[256,512]{1,0:T(8,128)(2,1)S(1)}, u32[]{:S(2)}) copy-start(bf16[256,512]{1,0:T(8,128)(2,1)S(1)} %collective-permute-done.42.refs_3_) | copy-start | bytes 786436
  70.8 14.3 %collective-permute-start.44 = (bf16[256,512]{1,0:T(8,128)(2,1)}, bf16[256,512]{1,0:T(8,128)(2,1)S(1)}, u32[]{:S(2)}, u32[]{:S(2)}) collective-permute-start(bf16[256,512]{1,0:T(8,128)(2,1)} %get-tuple-element.152), channel_id=1, source_target_pairs={{0,132},{1,133},{2,134},{3,135},{4,128},{5,129},{6,130},{7,131},{8... | collective-permute-start | bytes 786440 | tf_op jit(solution)/shard_map/ppermute | solution.py:16
  79.3 5.8 %copy-start.10 = (bf16[256,512]{1,0:T(8,128)(2,1)}, bf16[256,512]{1,0:T(8,128)(2,1)S(1)}, u32[]{:S(2)}) copy-start(bf16[256,512]{1,0:T(8,128)(2,1)S(1)} %collective-permute-done.43.refs_4_) | copy-start | bytes 786436
  85.1 0.8 copy-start.11
  85.1 1.2 copy-start.6
  85.1 1.2 copy-start.7
  85.2 1.2 copy-start.8
  85.2 7.9 %collective-permute-start.45 = (bf16[3,32,512]{2,1,0:T(8,128)(2,1)}, bf16[3,32,512]{2,1,0:T(8,128)(2,1)S(1)}, u32[]{:S(2)}, u32[]{:S(2)}) collective-permute-start(bf16[3,32,512]{2,1,0:T(8,128)(2,1)} %get-tuple-element.153), channel_id=1, source_target_pairs={{0,8},{8,16},{16,24},{24,32},{32,40},{40,48},{48,56},{56,64},{64,7... | collective-permute-start | bytes 294920 | tf_op jit(solution)/shard_map/ppermute | solution.py:20
  85.9 7.2 %collective-permute-start.46 = (bf16[3,32,512]{2,1,0:T(8,128)(2,1)}, bf16[3,32,512]{2,1,0:T(8,128)(2,1)S(1)}, u32[]{:S(2)}, u32[]{:S(2)}) collective-permute-start(bf16[3,32,512]{2,1,0:T(8,128)(2,1)} %get-tuple-element.154), channel_id=1, source_target_pairs={{8,0},{16,8},{24,16},{32,24},{40,32},{48,40},{56,48},{64,56},{72,6... | collective-permute-start | bytes 294920 | tf_op jit(solution)/shard_map/ppermute | solution.py:24
  86.4 8.3 %copy-start.5 = (f32[22,24,512]{2,1,0:T(8,128)S(1)}, f32[22,24,512]{2,1,0:T(8,128)}, u32[]{:S(2)}) copy-start(f32[22,24,512]{2,1,0:T(8,128)} %get-tuple-element.144) | copy-start | bytes 3244036
  89.2 18.0 %collective-permute-start.51 = (bf16[128,512]{1,0:T(8,128)(2,1)}, bf16[128,512]{1,0:T(8,128)(2,1)S(1)}, u32[]{:S(2)}, u32[]{:S(2)}) collective-permute-start(bf16[128,512]{1,0:T(8,128)(2,1)} %get-tuple-element.165), channel_id=1, source_target_pairs={{0,128},{1,129},{2,130},{3,131},{4,132},{5,133},{6,134},{7,135},{8... | collective-permute-start | bytes 393224 | tf_op jit(solution)/shard_map/ppermute | solution.py:16
  89.6 19.5 %collective-permute-start.52 = (bf16[128,512]{1,0:T(8,128)(2,1)}, bf16[128,512]{1,0:T(8,128)(2,1)S(1)}, u32[]{:S(2)}, u32[]{:S(2)}) collective-permute-start(bf16[128,512]{1,0:T(8,128)(2,1)} %get-tuple-element.166), channel_id=1, source_target_pairs={{0,4},{1,5},{2,6},{3,7},{4,0},{5,1},{6,2},{7,3},{8,12},{9,13},{10,... | collective-permute-start | bytes 393224 | tf_op jit(solution)/shard_map/ppermute | solution.py:16
  91.5 24.7 %collective-permute-start.53 = (bf16[128,512]{1,0:T(8,128)(2,1)}, bf16[128,512]{1,0:T(8,128)(2,1)}, u32[]{:S(2)}, u32[]{:S(2)}) collective-permute-start(bf16[128,512]{1,0:T(8,128)(2,1)} %get-tuple-element.167), channel_id=1, source_target_pairs={{0,132},{1,133},{2,134},{3,135},{4,128},{5,129},{6,130},{7,131},{8... | collective-permute-start | bytes 393224 | tf_op jit(solution)/shard_map/ppermute | solution.py:16
  93.1 3.6 %collective-permute-start.54 = (bf16[64,512]{1,0:T(8,128)(2,1)}, bf16[64,512]{1,0:T(8,128)(2,1)S(1)}, u32[]{:S(2)}, u32[]{:S(2)}) collective-permute-start(bf16[64,512]{1,0:T(8,128)(2,1)} %get-tuple-element.168), channel_id=1, source_target_pairs={{0,1},{1,0},{2,3},{3,2},{4,5},{5,4},{6,7},{7,6},{8,9},{9,8},{10,11... | collective-permute-start | bytes 196616 | tf_op jit(solution)/shard_map/ppermute | solution.py:16
  93.1 5.0 %collective-permute-start.55 = (bf16[64,512]{1,0:T(8,128)(2,1)}, bf16[64,512]{1,0:T(8,128)(2,1)}, u32[]{:S(2)}, u32[]{:S(2)}) collective-permute-start(bf16[64,512]{1,0:T(8,128)(2,1)} %get-tuple-element.169), channel_id=1, source_target_pairs={{0,2},{1,3},{2,0},{3,1},{4,6},{5,7},{6,4},{7,5},{8,10},{9,11},{10,... | collective-permute-start | bytes 196616 | tf_op jit(solution)/shard_map/ppermute | solution.py:16
  94.6 2.1 %copy-start.19 = (bf16[64,512]{1,0:T(8,128)(2,1)S(1)}, bf16[64,512]{1,0:T(8,128)(2,1)}, u32[]{:S(2)}) copy-start(bf16[64,512]{1,0:T(8,128)(2,1)} %get-tuple-element.170) | copy-start | bytes 196612
  96.7 19.4 %copy-start.18 = (bf16[64,512]{1,0:T(8,128)(2,1)}, bf16[64,512]{1,0:T(8,128)(2,1)S(1)}, u32[]{:S(2)}) copy-start(bf16[64,512]{1,0:T(8,128)(2,1)S(1)} %collective-permute-done.54.refs_3_) | copy-start | bytes 196612
  96.7 4.8 %collective-permute-start.56 = (bf16[64,512]{1,0:T(8,128)(2,1)S(1)}, bf16[64,512]{1,0:T(8,128)(2,1)S(1)}, u32[]{:S(2)}, u32[]{:S(2)}) collective-permute-start(bf16[64,512]{1,0:T(8,128)(2,1)S(1)} %copy-done.19), channel_id=1, source_target_pairs={{0,3},{1,2},{2,1},{3,0},{4,7},{5,6},{6,5},{7,4},{8,11},{9,10},{10,... | collective-permute-start | bytes 196616 | tf_op jit(solution)/shard_map/ppermute | solution.py:16
  98.2 20.1 %collective-permute-start.49 = (bf16[16,3,512]{2,1,0:T(4,128)(2,1)S(1)}, bf16[16,3,512]{2,1,0:T(4,128)(2,1)S(1)}, u32[]{:S(2)}, u32[]{:S(2)}) collective-permute-start(bf16[16,3,512]{2,1,0:T(4,128)(2,1)S(1)} %get-tuple-element.193), channel_id=1, source_target_pairs={{0,8},{8,16},{16,24},{24,32},{32,40},{40,48},{48,56},{56,64},{64,7... | collective-permute-start | bytes 147464 | tf_op jit(solution)/shard_map/ppermute | solution.py:20
  101.5 14.6 %copy-start.20 = (bf16[64,512]{1,0:T(8,128)(2,1)}, bf16[64,512]{1,0:T(8,128)(2,1)S(1)}, u32[]{:S(2)}) copy-start(bf16[64,512]{1,0:T(8,128)(2,1)S(1)} %collective-permute-done.56.refs_5_) | copy-start | bytes 196612
  101.5 16.8 %collective-permute-start.50 = (bf16[16,3,512]{2,1,0:T(4,128)(2,1)S(1)}, bf16[16,3,512]{2,1,0:T(4,128)(2,1)S(1)}, u32[]{:S(2)}, u32[]{:S(2)}) collective-permute-start(bf16[16,3,512]{2,1,0:T(4,128)(2,1)S(1)} %get-tuple-element.194), channel_id=1, source_target_pairs={{8,0},{16,8},{24,16},{32,24},{40,32},{48,40},{56,48},{64,56},{72,6... | collective-permute-start | bytes 147464 | tf_op jit(solution)/shard_map/ppermute | solution.py:24
  107.2 9.0 %copy-start.12 = (bf16[128,512]{1,0:T(8,128)(2,1)}, bf16[128,512]{1,0:T(8,128)(2,1)S(1)}, u32[]{:S(2)}) copy-start(bf16[128,512]{1,0:T(8,128)(2,1)S(1)} %collective-permute-done.51.refs_0_) | copy-start | bytes 393220
  107.2 27.3 %collective-permute-start.48 = (bf16[16,3,512]{2,1,0:T(4,128)(2,1)S(1)}, bf16[16,3,512]{2,1,0:T(4,128)(2,1)S(1)}, u32[]{:S(2)}, u32[]{:S(2)}) collective-permute-start(bf16[16,3,512]{2,1,0:T(4,128)(2,1)S(1)} %get-tuple-element.188), channel_id=1, source_target_pairs={{1,0},{2,1},{3,2},{4,3},{5,4},{6,5},{7,6},{9,8},{10,9},{11,10},{12... | collective-permute-start | bytes 147464 | tf_op jit(solution)/shard_map/ppermute | solution.py:32
  109.1 7.1 %copy-start.13 = (bf16[128,512]{1,0:T(8,128)(2,1)}, bf16[128,512]{1,0:T(8,128)(2,1)S(1)}, u32[]{:S(2)}) copy-start(bf16[128,512]{1,0:T(8,128)(2,1)S(1)} %collective-permute-done.52.refs_1_) | copy-start | bytes 393220
  109.1 34.4 %collective-permute-start.47 = (bf16[16,3,512]{2,1,0:T(4,128)(2,1)S(1)}, bf16[16,3,512]{2,1,0:T(4,128)(2,1)S(1)}, u32[]{:S(2)}, u32[]{:S(2)}) collective-permute-start(bf16[16,3,512]{2,1,0:T(4,128)(2,1)S(1)} %get-tuple-element.186), channel_id=1, source_target_pairs={{0,1},{1,2},{2,3},{3,4},{4,5},{5,6},{6,7},{8,9},{9,10},{10,11},{11... | collective-permute-start | bytes 147464 | tf_op jit(solution)/shard_map/ppermute | solution.py:28
  118.2 3.7 %collective-permute-start.57 = (bf16[96,512]{1,0:T(8,128)(2,1)}, bf16[96,512]{1,0:T(8,128)(2,1)S(1)}, u32[]{:S(2)}, u32[]{:S(2)}) collective-permute-start(bf16[96,512]{1,0:T(8,128)(2,1)} %get-tuple-element.173), channel_id=1, source_target_pairs={{0,16},{1,17},{2,18},{3,19},{4,20},{5,21},{6,22},{7,23},{8,24},{9,... | collective-permute-start | bytes 294920 | tf_op jit(solution)/shard_map/ppermute | solution.py:16
  118.2 4.8 %collective-permute-start.58 = (bf16[96,512]{1,0:T(8,128)(2,1)}, bf16[96,512]{1,0:T(8,128)(2,1)S(1)}, u32[]{:S(2)}, u32[]{:S(2)}) collective-permute-start(bf16[96,512]{1,0:T(8,128)(2,1)} %get-tuple-element.174), channel_id=1, source_target_pairs={{0,32},{1,33},{2,34},{3,35},{4,36},{5,37},{6,38},{7,39},{8,40},{9,... | collective-permute-start | bytes 294920 | tf_op jit(solution)/shard_map/ppermute | solution.py:16
  118.3 7.5 %collective-permute-start.59 = (bf16[96,512]{1,0:T(8,128)(2,1)}, bf16[96,512]{1,0:T(8,128)(2,1)S(1)}, u32[]{:S(2)}, u32[]{:S(2)}) collective-permute-start(bf16[96,512]{1,0:T(8,128)(2,1)} %get-tuple-element.175), channel_id=1, source_target_pairs={{0,48},{1,49},{2,50},{3,51},{4,52},{5,53},{6,54},{7,55},{8,56},{9,... | collective-permute-start | bytes 294920 | tf_op jit(solution)/shard_map/ppermute | solution.py:16
  121.9 4.0 %copy-start.15 = (bf16[96,512]{1,0:T(8,128)(2,1)}, bf16[96,512]{1,0:T(8,128)(2,1)S(1)}, u32[]{:S(2)}) copy-start(bf16[96,512]{1,0:T(8,128)(2,1)S(1)} %collective-permute-done.57.a_ref) | copy-start | bytes 294916
  123.0 2.9 %copy-start.16 = (bf16[96,512]{1,0:T(8,128)(2,1)}, bf16[96,512]{1,0:T(8,128)(2,1)S(1)}, u32[]{:S(2)}) copy-start(bf16[96,512]{1,0:T(8,128)(2,1)S(1)} %collective-permute-done.58.b_ref) | copy-start | bytes 294916
  125.8 0.6 copy-start.17
  128.2 7.6 %collective-permute-start.60 = (f32[48,512]{1,0:T(8,128)}, f32[48,512]{1,0:T(8,128)S(1)}, u32[]{:S(2)}, u32[]{:S(2)}) collective-permute-start(f32[48,512]{1,0:T(8,128)} %get-tuple-element.180), channel_id=1, source_target_pairs={{0,64},{1,65},{2,66},{3,67},{4,68},{5,69},{6,70},{7,71},{8,72},{9,... | collective-permute-start | bytes 294920 | tf_op jit(solution)/shard_map/ppermute | solution.py:16
  133.2 1.3 collective-permute-start.24
  135.8 0.6 copy-start.14
  136.5 7.0 %copy-start.3 = (bf16[16,16,512]{2,1,0:T(8,128)(2,1)S(1)}, bf16[16,16,512]{2,1,0:T(8,128)(2,1)}, u32[]{:S(2)}) copy-start(bf16[16,16,512]{2,1,0:T(8,128)(2,1)} %param.42) | copy-start | bytes 786436
  138.1 6.5 %collective-permute-start.61 = (f32[32,512]{1,0:T(8,128)}, f32[32,512]{1,0:T(8,128)S(1)}, u32[]{:S(2)}, u32[]{:S(2)}) collective-permute-start(f32[32,512]{1,0:T(8,128)} %get-tuple-element.183), channel_id=1, source_target_pairs={{0,8},{1,9},{2,10},{3,11},{4,12},{5,13},{6,14},{7,15},{8,0},{9,1},... | collective-permute-start | bytes 196616 | tf_op jit(solution)/shard_map/ppermute | solution.py:16
